TPU v7x, 512 devices: a whole 4x4x16 slice. The times are simulated.
512 devices in a mesh: dp: 64 (over z, x_hi, core), head: 8 (over x_lo, y).
Axes of the slice: x: 4 (x_hi: 2, x_lo: 2; x = x_hi * 2 + x_lo), y: 4, z: 16, core: 2. Of those that a mesh axis runs over, the one named last changes fastest.
Arguments:
- queries: bfloat16 [16384, 8192], P('dp', 'head'), may hold values from -8 to 8
- resp_keys: bfloat16 [16384, 1024], P('dp', 'head'), may hold values from -6 to 6
- resp_values: bfloat16 [16384, 1024], P('dp', 'head'), may hold values from -6 to 6
- out_grad: bfloat16 [16384, 8192], P('dp', 'head'), may hold values from -72 to 72
- prefix_keys: bfloat16 [65536, 1024], P(('dp', 'head')), may hold values from -8 to 8, as said below
- prefix_values: bfloat16 [65536, 1024], P(('dp', 'head')), may hold values from -6 to 6
- resp_slot: int32 [16384], P('dp'), may hold values from 0 to 4, as said below
- prefix_len: int32 [16], replicated, may hold values from 512 to 1024, as said below
- prefix_owner: int32 [16], replicated, may hold values from 0 to 3
Outputs:
- query_grad: bfloat16 [16384, 8192], P('dp', 'head')
- resp_key_grad: bfloat16 [16384, 1024], P('dp', 'head')
- resp_value_grad: bfloat16 [16384, 1024], P('dp', 'head')
- prefix_key_grad: bfloat16 [65536, 1024], P(('dp', 'head'))
- prefix_value_grad: bfloat16 [65536, 1024], P(('dp', 'head'))
Inputs may be any that keep to these rules, and one draw needn't show every extreme that they name: `resp_slot`: in each block of 4 devices, responses 0 to 3 of the block's prompt lie in this order, each a run of 96 to 256 rows on one device, starting where the previous ended or at the first row of the next device; 4 marks empty rows. In every draw some device is filled by one response and some rows are empty. `prefix_len`: some prompt's prefix has exactly 1024 positions. `prefix_keys`: only the slots of the devices named by prefix_owner are read.
All inputs are finite; a program needn't handle non-finite values.
Results may differ from a plain program's by a relative error of at most 0.035.
Values may be sent and summed in bfloat16 or wider, within the bound.
No kernel may reach another device: no remote copies, remote signals or barrier semaphores. Data moves between devices by JAX's collectives and lax.ppermute only.
A program may use at most 64 MiB of HBM per device.

v0:
```python
import math

import jax
import jax.numpy as jnp
from jax import lax
from jax.sharding import PartitionSpec as P

HD = 128
QH = 64
KVH = 8
BLOCK = 4


masked_score = -1e30


def partner(block, axis, bit):
    count = lax.axis_size(axis)
    route = []
    for low in range(count):
        high = low | 1 << bit
        if high != low and high < count:
            route += [(low, high), (high, low)]
    return lax.ppermute(block, axis, route)


def head_pass(query_group, grad_group, key_rows, value_rows, visible, live_weight, pair_count):
    row_count = query_group.shape[0]
    group_size = query_group.shape[1]
    head_width = query_group.shape[2]
    score_scale = 1.0 / math.sqrt(head_width)
    query_items = jnp.moveaxis(
        query_group.reshape(row_count, group_size // pair_count, pair_count, head_width), 1, 0
    )
    grad_items = jnp.moveaxis(
        grad_group.reshape(row_count, group_size // pair_count, pair_count, head_width), 1, 0
    )

    def one_item(operands):
        query_item, grad_item = operands
        scores = (
            jnp.einsum("rhd,kd->hrk", query_item, key_rows, preferred_element_type=jnp.float32)
            * score_scale
        )
        scores = jnp.where(visible[None], scores, masked_score)
        exp_terms = jnp.exp(scores - jnp.max(scores, axis=-1, keepdims=True))
        weights = (
            exp_terms / jnp.sum(exp_terms, axis=-1, keepdims=True) * live_weight[None, :, None]
        )
        weights_low = weights.astype(jnp.bfloat16)
        attended = jnp.einsum(
            "hrk,kd->rhd", weights_low, value_rows, preferred_element_type=jnp.float32
        ).astype(jnp.bfloat16)
        out_dot = jnp.sum(grad_item.astype(jnp.float32) * attended.astype(jnp.float32), axis=-1)
        grad_weights = jnp.einsum(
            "rhd,kd->hrk", grad_item, value_rows, preferred_element_type=jnp.float32
        )
        score_grad = (weights * (grad_weights - out_dot.T[:, :, None]) * score_scale).astype(
            jnp.bfloat16
        )
        query_grad = jnp.einsum(
            "hrk,kd->rhd", score_grad, key_rows, preferred_element_type=jnp.float32
        ).astype(jnp.bfloat16)
        key_grad = jnp.einsum(
            "hrk,rhd->kd", score_grad, query_item, preferred_element_type=jnp.float32
        )
        value_grad = jnp.einsum(
            "hrk,rhd->kd", weights_low, grad_item, preferred_element_type=jnp.float32
        )
        return (query_grad, key_grad, value_grad)

    query_grads, key_grads, value_grads = lax.map(one_item, (query_items, grad_items))
    query_grad = jnp.moveaxis(query_grads, 0, 1).reshape(row_count, group_size, head_width)
    return (query_grad, jnp.sum(key_grads, axis=0), jnp.sum(value_grads, axis=0))


def on_device(
    queries,
    resp_keys,
    resp_values,
    out_grad,
    prefix_keys,
    prefix_values,
    resp_slot,
    prefix_len,
    prefix_owner,
):
    row_count = queries.shape[0]
    kv_local = KVH // lax.axis_size("head")
    group_size = QH // KVH
    device_index = lax.axis_index("dp")
    prompt_index = device_index // BLOCK
    block_place = device_index % BLOCK
    owner_place = prefix_owner[prompt_index]
    prefix_count = prefix_len[prompt_index]
    bit_count = BLOCK.bit_length() - 1
    near_keys, near_values = (
        lax.all_to_all(prefix_keys, "head", split_axis=1, concat_axis=0, tiled=True),
        lax.all_to_all(prefix_values, "head", split_axis=1, concat_axis=0, tiled=True),
    )
    pre_rows = near_keys.shape[0]
    stacked = jnp.stack([near_keys, near_values])
    for bit_index in range(bit_count):
        arrived = partner(stacked, "dp", bit_index)
        holds_now = (block_place ^ owner_place) >> bit_index == 0
        partner_holds = (block_place ^ 1 << bit_index ^ owner_place) >> bit_index == 0
        taking = jnp.logical_and(jnp.logical_not(holds_now), partner_holds)
        stacked = jnp.where(taking, arrived, stacked)
    live_rows = resp_slot < BLOCK
    live_weight = live_rows.astype(jnp.float32)
    row_index = jnp.arange(row_count, dtype=jnp.int32)
    prefix_seen = jnp.logical_and(
        (jnp.arange(pre_rows, dtype=jnp.int32) < prefix_count)[None, :], live_rows[:, None]
    )
    same_resp = jnp.logical_and(
        resp_slot[:, None] == resp_slot[None, :], row_index[None, :] <= row_index[:, None]
    )
    resp_seen = jnp.logical_and(same_resp, live_rows[:, None])
    visible = jnp.concatenate([prefix_seen, resp_seen], axis=1)
    pair_count = 1
    while pair_count * 2 * row_count <= 512 and group_size % (pair_count * 2) == 0:
        pair_count = pair_count * 2
    query_heads = queries.reshape(row_count, kv_local, group_size, HD)
    grad_heads = out_grad.reshape(row_count, kv_local, group_size, HD)
    resp_key_heads = resp_keys.reshape(row_count, kv_local, HD)
    resp_value_heads = resp_values.reshape(row_count, kv_local, HD)
    pre_key_heads = stacked[0].reshape(pre_rows, kv_local, HD)
    pre_value_heads = stacked[1].reshape(pre_rows, kv_local, HD)
    query_parts, key_parts, value_parts = ([], [], [])
    key_rows = jnp.concatenate([pre_key_heads[:, 0], resp_key_heads[:, 0]], 0)
    value_rows = jnp.concatenate([pre_value_heads[:, 0], resp_value_heads[:, 0]], 0)
    query_grad, key_grad, value_grad = head_pass(
        query_heads[:, 0], grad_heads[:, 0], key_rows, value_rows, visible, live_weight, pair_count
    )
    query_parts.append(query_grad)
    key_parts.append(key_grad)
    value_parts.append(value_grad)
    query_grad = jnp.stack(query_parts, 1).reshape(row_count, kv_local * group_size * HD)
    key_grads = jnp.stack(key_parts, 1)
    value_grads = jnp.stack(value_parts, 1)
    resp_key_grad = key_grads[pre_rows:].reshape(row_count, kv_local * HD).astype(jnp.bfloat16)
    resp_value_grad = value_grads[pre_rows:].reshape(row_count, kv_local * HD).astype(jnp.bfloat16)
    partial_sum = jnp.stack(
        [
            key_grads[:pre_rows].reshape(pre_rows, kv_local * HD),
            value_grads[:pre_rows].reshape(pre_rows, kv_local * HD),
        ]
    )
    total = partial_sum
    for bit_index in range(bit_count):
        total = total + partner(total, "dp", bit_index)
    summed = total.astype(jnp.bfloat16)
    summed = jnp.where(block_place == owner_place, summed, jnp.zeros_like(summed))
    prefix_key_grad, prefix_value_grad = (
        lax.all_to_all(summed[0], "head", split_axis=0, concat_axis=1, tiled=True),
        lax.all_to_all(summed[1], "head", split_axis=0, concat_axis=1, tiled=True),
    )
    return (query_grad, resp_key_grad, resp_value_grad, prefix_key_grad, prefix_value_grad)


def solution(mesh):
    placed = (
        P("dp", "head"),
        P("dp", "head"),
        P("dp", "head"),
        P("dp", "head"),
        P(("dp", "head"), None),
        P(("dp", "head"), None),
        P("dp"),
        P(),
        P(),
    )
    return jax.shard_map(
        on_device,
        mesh=mesh,
        in_specs=placed,
        out_specs=(
            P("dp", "head"),
            P("dp", "head"),
            P("dp", "head"),
            P(("dp", "head"), None),
            P(("dp", "head"), None),
        ),
        check_vma=False,
    )
```

profile of v0, /device:TPU:1, one launch (start us, length us, event | category | flops | bytes accessed | tf_op | source)
XLA Modules:
  0.0 162.3 jit_solution(65857725925679189)
XLA Ops:
  2.6 5.9 %all-to-all-start = ((bf16[128,8,128]{0,2,1:T(8,128)(2,1)}), bf16[128,8,128]{0,2,1:T(8,128)(2,1)S(1)}, u32[]{:S(2)}, u32[]{:S(2)}) async-start(bf16[128,8,128]{0,2,1:T(8,128)(2,1)} %bitcast.19), calls=%async_computation | async-start | bytes 524288 | tf_op jit(solution)/shard_map/all_to_all | solution.py:98
  10.3 4.3 %all-to-all-done = bf16[128,8,128]{0,2,1:T(8,128)(2,1)S(1)} async-done(((bf16[128,8,128]{0,2,1:T(8,128)(2,1)}), bf16[128,8,128]{0,2,1:T(8,128)(2,1)S(1)}, u32[]{:S(2)}, u32[]{:S(2)}) %all-to-all-start) | async-done | bytes 262176 | tf_op jit(solution)/shard_map/all_to_all | solution.py:98
  14.6 3.4 %all-to-all-start.1 = ((bf16[128,8,128]{0,2,1:T(8,128)(2,1)}), bf16[128,8,128]{0,2,1:T(8,128)(2,1)S(1)}, u32[]{:S(2)}, u32[]{:S(2)}) async-start(bf16[128,8,128]{0,2,1:T(8,128)(2,1)} %bitcast.22), calls=%async_computation.1 | async-start | bytes 524288 | tf_op jit(solution)/shard_map/all_to_all | solution.py:99
  18.2 5.8 %all-to-all-done.1 = bf16[128,8,128]{0,2,1:T(8,128)(2,1)S(1)} async-done(((bf16[128,8,128]{0,2,1:T(8,128)(2,1)}), bf16[128,8,128]{0,2,1:T(8,128)(2,1)S(1)}, u32[]{:S(2)}, u32[]{:S(2)}) %all-to-all-start.1) | async-done | bytes 262176 | tf_op jit(solution)/shard_map/all_to_all | solution.py:99
  24.3 8.5 %collective-permute-start = (bf16[2,1024,128]{2,1,0:T(8,128)(2,1)S(1)}, bf16[2,1024,128]{2,1,0:T(8,128)(2,1)S(1)}, u32[]{:S(2)}, u32[]{:S(2)}) collective-permute-start(bf16[2,1024,128]{2,1,0:T(8,128)(2,1)S(1)} %pad_maximum_fusion.1), channel_id=1, source_target_pairs={{0,8},{8,0},{16,24},{24,16},{32,40},{40,32},{48,56},{56,48},{64,72... | collective-permute-start | bytes 1572872 | tf_op jit(solution)/shard_map/ppermute | solution.py:24
  36.7 1.9 %collective-permute-start.1 = (bf16[2,1024,128]{2,1,0:T(8,128)(2,1)S(1)}, bf16[2,1024,128]{2,1,0:T(8,128)(2,1)S(1)}, u32[]{:S(2)}, u32[]{:S(2)}) collective-permute-start(bf16[2,1024,128]{2,1,0:T(8,128)(2,1)S(1)} %broadcast_select_fusion), channel_id=1, source_target_pairs={{0,16},{16,0},{8,24},{24,8},{32,48},{48,32},{40,56},{56,40},{64,80... | collective-permute-start | bytes 1572872 | tf_op jit(solution)/shard_map/ppermute | solution.py:24
  39.5 14.1 %collective-permute-done.1 = bf16[2,1024,128]{2,1,0:T(8,128)(2,1)S(1)} collective-permute-done((bf16[2,1024,128]{2,1,0:T(8,128)(2,1)S(1)}, bf16[2,1024,128]{2,1,0:T(8,128)(2,1)S(1)}, u32[]{:S(2)}, u32[]{:S(2)}) %collective-permute-start.1) | collective-permute-done | bytes 524320 | tf_op jit(solution)/shard_map/ppermute | solution.py:24
  54.0 48.1 %while.14 = (s32[]{:T(128)}, bf16[4,256,2,128]{3,1,2,0:T(8,128)(2,1)S(1)}, f32[4,1280,128]{2,1,0:T(8,128)}, f32[4,1280,128]{2,1,0:T(8,128)}, pred[256,1280]{1,0:...) while((s32[]{:T(128)}, ...), condition=%wide.region_4.5_spmd, body=%wide.region_0.4_spmd.sunk | while | flops 1356992768 | bytes 15025285 | solution.py:72
  54.2 2.6 %fusion.113 = (f32[2,256]{1,0:T(2,128)S(1)}, f32[2,256,1280]{2,1,0:T(8,128)}) fusion(pred[256,1280]{1,0:T(8,128)(4,1)S(1)} %get-tuple-element.228, bf16[1280,128]{1,0:T(8,128)(2,1)S(1)} %get-tuple-element.230, bf16[4,256,2,128]{1,3,2,0:T(8,128)(2,1)S(1)} %get-tuple-element.229, s32[]{:T(128)S(6)} %copy.90), kind=kOutput, calls=%fused_computation.68.clone.1 | convolution fusion | flops 170394880 | bytes 3409924 | tf_op jit(solution)/shard_map/while/body/eval_jaxpr/sub | solution.py:46
  56.8 2.1 %fusion.114 = f32[256,2]{0,1:T(2,128)S(1)} fusion(bf16[1280,128]{0,1:T(8,128)(2,1)S(1)} %get-tuple-element.233, bf16[1,256,2,128]{3,1,2,0:T(8,128)(2,1)S(1)} %copy.82, f32[256]{0:T(256)S(1)} %get-tuple-element.231, f32[2,256]{1,0:T(2,128)S(1)} %get-tuple-element.200, pred[256,1280]{1,0:T(8,128)(4,1)S(1)} %get-tuple-element.228, ...), kind=kOutput, calls=%fused_computation.21.clone.1 | convolution fusion | flops 339805440 | bytes 1250308 | tf_op jit(solution)/shard_map/while/body/eval_jaxpr/hrk,kd->rhd/dot_general | solution.py:51
  58.9 2.4 %fusion.115 = bf16[2,256,1280]{2,1,0:T(8,128)(2,1)S(1)} fusion(f32[2,256]{1,0:T(2,128)S(1)} %bitcast.199, bf16[1280,128]{0,1:T(8,128)(2,1)S(1)} %get-tuple-element.233, bf16[1,256,2,128]{1,3,2,0:T(8,128)(2,1)S(1)} %constant_dynamic-slice_fusion.2, f32[256]{0:T(256)S(1)} %get-tuple-element.231, f32[2,256,1280]{2,1,0:T(8,128)} %get-tuple-element.201, ...), kind=kOutput, calls=%fused_computation.10.clone.1 | convolution fusion | flops 171704320 | bytes 4396032 | tf_op jit(solution)/shard_map/while/body/eval_jaxpr/rhd,kd->hrk/dot_general | solution.py:55
  63.3 2.8 %fusion.118 = f32[4,1280,128]{2,1,0:T(8,128)} fusion(f32[4,1280,128]{2,1,0:T(8,128)} %get-tuple-element.216, s32[]{:T(128)S(6)} %copy.90, bf16[1,256,2,128]{1,3,2,0:T(8,128)(2,1)S(1)} %constant_dynamic-slice_fusion.2, f32[256]{0:T(256)S(1)} %get-tuple-element.231, f32[2,256]{1,0:T(2,128)S(1)} %get-tuple-element.200, ...), kind=kOutput, calls=%fused_computation.13.clone.1 | convolution fusion | flops 339478272 | bytes 1576960 | tf_op jit(solution)/shard_map/while/body/eval_jaxpr/hrk,rhd->kd/dot_general | solution.py:67
  66.2 2.6 %fusion.113 = (f32[2,256]{1,0:T(2,128)S(1)}, f32[2,256,1280]{2,1,0:T(8,128)}) fusion(pred[256,1280]{1,0:T(8,128)(4,1)S(1)} %get-tuple-element.228, bf16[1280,128]{1,0:T(8,128)(2,1)S(1)} %get-tuple-element.230, bf16[4,256,2,128]{1,3,2,0:T(8,128)(2,1)S(1)} %get-tuple-element.229, s32[]{:T(128)S(6)} %copy.90), kind=kOutput, calls=%fused_computation.68.clone.1 | convolution fusion | flops 170394880 | bytes 3409924 | tf_op jit(solution)/shard_map/while/body/eval_jaxpr/sub | solution.py:46
  68.8 2.1 %fusion.114 = f32[256,2]{0,1:T(2,128)S(1)} fusion(bf16[1280,128]{0,1:T(8,128)(2,1)S(1)} %get-tuple-element.233, bf16[1,256,2,128]{3,1,2,0:T(8,128)(2,1)S(1)} %copy.82, f32[256]{0:T(256)S(1)} %get-tuple-element.231, f32[2,256]{1,0:T(2,128)S(1)} %get-tuple-element.200, pred[256,1280]{1,0:T(8,128)(4,1)S(1)} %get-tuple-element.228, ...), kind=kOutput, calls=%fused_computation.21.clone.1 | convolution fusion | flops 339805440 | bytes 1250308 | tf_op jit(solution)/shard_map/while/body/eval_jaxpr/hrk,kd->rhd/dot_general | solution.py:51
  70.9 2.4 %fusion.115 = bf16[2,256,1280]{2,1,0:T(8,128)(2,1)S(1)} fusion(f32[2,256]{1,0:T(2,128)S(1)} %bitcast.199, bf16[1280,128]{0,1:T(8,128)(2,1)S(1)} %get-tuple-element.233, bf16[1,256,2,128]{1,3,2,0:T(8,128)(2,1)S(1)} %constant_dynamic-slice_fusion.2, f32[256]{0:T(256)S(1)} %get-tuple-element.231, f32[2,256,1280]{2,1,0:T(8,128)} %get-tuple-element.201, ...), kind=kOutput, calls=%fused_computation.10.clone.1 | convolution fusion | flops 171704320 | bytes 4396032 | tf_op jit(solution)/shard_map/while/body/eval_jaxpr/rhd,kd->hrk/dot_general | solution.py:55
  75.3 2.8 %fusion.118 = f32[4,1280,128]{2,1,0:T(8,128)} fusion(f32[4,1280,128]{2,1,0:T(8,128)} %get-tuple-element.216, s32[]{:T(128)S(6)} %copy.90, bf16[1,256,2,128]{1,3,2,0:T(8,128)(2,1)S(1)} %constant_dynamic-slice_fusion.2, f32[256]{0:T(256)S(1)} %get-tuple-element.231, f32[2,256]{1,0:T(2,128)S(1)} %get-tuple-element.200, ...), kind=kOutput, calls=%fused_computation.13.clone.1 | convolution fusion | flops 339478272 | bytes 1576960 | tf_op jit(solution)/shard_map/while/body/eval_jaxpr/hrk,rhd->kd/dot_general | solution.py:67
  78.2 2.6 %fusion.113 = (f32[2,256]{1,0:T(2,128)S(1)}, f32[2,256,1280]{2,1,0:T(8,128)}) fusion(pred[256,1280]{1,0:T(8,128)(4,1)S(1)} %get-tuple-element.228, bf16[1280,128]{1,0:T(8,128)(2,1)S(1)} %get-tuple-element.230, bf16[4,256,2,128]{1,3,2,0:T(8,128)(2,1)S(1)} %get-tuple-element.229, s32[]{:T(128)S(6)} %copy.90), kind=kOutput, calls=%fused_computation.68.clone.1 | convolution fusion | flops 170394880 | bytes 3409924 | tf_op jit(solution)/shard_map/while/body/eval_jaxpr/sub | solution.py:46
  80.8 2.1 %fusion.114 = f32[256,2]{0,1:T(2,128)S(1)} fusion(bf16[1280,128]{0,1:T(8,128)(2,1)S(1)} %get-tuple-element.233, bf16[1,256,2,128]{3,1,2,0:T(8,128)(2,1)S(1)} %copy.82, f32[256]{0:T(256)S(1)} %get-tuple-element.231, f32[2,256]{1,0:T(2,128)S(1)} %get-tuple-element.200, pred[256,1280]{1,0:T(8,128)(4,1)S(1)} %get-tuple-element.228, ...), kind=kOutput, calls=%fused_computation.21.clone.1 | convolution fusion | flops 339805440 | bytes 1250308 | tf_op jit(solution)/shard_map/while/body/eval_jaxpr/hrk,kd->rhd/dot_general | solution.py:51
  82.9 2.4 %fusion.115 = bf16[2,256,1280]{2,1,0:T(8,128)(2,1)S(1)} fusion(f32[2,256]{1,0:T(2,128)S(1)} %bitcast.199, bf16[1280,128]{0,1:T(8,128)(2,1)S(1)} %get-tuple-element.233, bf16[1,256,2,128]{1,3,2,0:T(8,128)(2,1)S(1)} %constant_dynamic-slice_fusion.2, f32[256]{0:T(256)S(1)} %get-tuple-element.231, f32[2,256,1280]{2,1,0:T(8,128)} %get-tuple-element.201, ...), kind=kOutput, calls=%fused_computation.10.clone.1 | convolution fusion | flops 171704320 | bytes 4396032 | tf_op jit(solution)/shard_map/while/body/eval_jaxpr/rhd,kd->hrk/dot_general | solution.py:55
  87.4 2.8 %fusion.118 = f32[4,1280,128]{2,1,0:T(8,128)} fusion(f32[4,1280,128]{2,1,0:T(8,128)} %get-tuple-element.216, s32[]{:T(128)S(6)} %copy.90, bf16[1,256,2,128]{1,3,2,0:T(8,128)(2,1)S(1)} %constant_dynamic-slice_fusion.2, f32[256]{0:T(256)S(1)} %get-tuple-element.231, f32[2,256]{1,0:T(2,128)S(1)} %get-tuple-element.200, ...), kind=kOutput, calls=%fused_computation.13.clone.1 | convolution fusion | flops 339478272 | bytes 1576960 | tf_op jit(solution)/shard_map/while/body/eval_jaxpr/hrk,rhd->kd/dot_general | solution.py:67
  90.3 2.6 %fusion.113 = (f32[2,256]{1,0:T(2,128)S(1)}, f32[2,256,1280]{2,1,0:T(8,128)}) fusion(pred[256,1280]{1,0:T(8,128)(4,1)S(1)} %get-tuple-element.228, bf16[1280,128]{1,0:T(8,128)(2,1)S(1)} %get-tuple-element.230, bf16[4,256,2,128]{1,3,2,0:T(8,128)(2,1)S(1)} %get-tuple-element.229, s32[]{:T(128)S(6)} %copy.90), kind=kOutput, calls=%fused_computation.68.clone.1 | convolution fusion | flops 170394880 | bytes 3409924 | tf_op jit(solution)/shard_map/while/body/eval_jaxpr/sub | solution.py:46
  92.9 2.1 %fusion.114 = f32[256,2]{0,1:T(2,128)S(1)} fusion(bf16[1280,128]{0,1:T(8,128)(2,1)S(1)} %get-tuple-element.233, bf16[1,256,2,128]{3,1,2,0:T(8,128)(2,1)S(1)} %copy.82, f32[256]{0:T(256)S(1)} %get-tuple-element.231, f32[2,256]{1,0:T(2,128)S(1)} %get-tuple-element.200, pred[256,1280]{1,0:T(8,128)(4,1)S(1)} %get-tuple-element.228, ...), kind=kOutput, calls=%fused_computation.21.clone.1 | convolution fusion | flops 339805440 | bytes 1250308 | tf_op jit(solution)/shard_map/while/body/eval_jaxpr/hrk,kd->rhd/dot_general | solution.py:51
  95.0 2.4 %fusion.115 = bf16[2,256,1280]{2,1,0:T(8,128)(2,1)S(1)} fusion(f32[2,256]{1,0:T(2,128)S(1)} %bitcast.199, bf16[1280,128]{0,1:T(8,128)(2,1)S(1)} %get-tuple-element.233, bf16[1,256,2,128]{1,3,2,0:T(8,128)(2,1)S(1)} %constant_dynamic-slice_fusion.2, f32[256]{0:T(256)S(1)} %get-tuple-element.231, f32[2,256,1280]{2,1,0:T(8,128)} %get-tuple-element.201, ...), kind=kOutput, calls=%fused_computation.10.clone.1 | convolution fusion | flops 171704320 | bytes 4396032 | tf_op jit(solution)/shard_map/while/body/eval_jaxpr/rhd,kd->hrk/dot_general | solution.py:55
  99.4 2.8 %fusion.118 = f32[4,1280,128]{2,1,0:T(8,128)} fusion(f32[4,1280,128]{2,1,0:T(8,128)} %get-tuple-element.216, s32[]{:T(128)S(6)} %copy.90, bf16[1,256,2,128]{1,3,2,0:T(8,128)(2,1)S(1)} %constant_dynamic-slice_fusion.2, f32[256]{0:T(256)S(1)} %get-tuple-element.231, f32[2,256]{1,0:T(2,128)S(1)} %get-tuple-element.200, ...), kind=kOutput, calls=%fused_computation.13.clone.1 | convolution fusion | flops 339478272 | bytes 1576960 | tf_op jit(solution)/shard_map/while/body/eval_jaxpr/hrk,rhd->kd/dot_general | solution.py:67
  103.0 1.9 %reduce_sum.37 = f32[1280,128]{1,0:T(8,128)S(1)} reduce(f32[4,1280,128]{2,1,0:T(8,128)} %get-tuple-element.61, f32[]{:T(128)} %constant.56.clone.1), dimensions={0}, to_apply=%region_6.7 | reduce | flops 491520 | bytes 3276804 | tf_op jit(solution)/shard_map/reduce_sum | solution.py:74
  104.9 2.0 %reduce_sum.36 = f32[1280,128]{1,0:T(8,128)S(1)} reduce(f32[4,1280,128]{2,1,0:T(8,128)} %get-tuple-element.60, f32[]{:T(128)} %constant.56.clone.1), dimensions={0}, to_apply=%region_5.6 | reduce | flops 491520 | bytes 3276804 | tf_op jit(solution)/shard_map/reduce_sum | solution.py:74
  107.0 2.7 %collective-permute-start.2 = (f32[2,1024,128]{2,1,0:T(8,128)S(1)}, f32[2,1024,128]{2,1,0:T(8,128)S(1)}, u32[]{:S(2)}, u32[]{:S(2)}) collective-permute-start(f32[2,1024,128]{2,1,0:T(8,128)S(1)} %pad_maximum_fusion), channel_id=1, source_target_pairs={{0,8},{8,0},{16,24},{24,16},{32,40},{40,32},{48,56},{56,48},{64,72... | collective-permute-start | bytes 3145736 | tf_op jit(solution)/shard_map/ppermute | solution.py:24
  109.7 2.3 %collective-permute-done.2 = f32[2,1024,128]{2,1,0:T(8,128)S(1)} collective-permute-done((f32[2,1024,128]{2,1,0:T(8,128)S(1)}, f32[2,1024,128]{2,1,0:T(8,128)S(1)}, u32[]{:S(2)}, u32[]{:S(2)}) %collective-permute-start.2) | collective-permute-done | bytes 1048608 | tf_op jit(solution)/shard_map/ppermute | solution.py:24
  115.6 25.5 %collective-permute-done.3 = f32[2,1024,128]{2,1,0:T(8,128)} collective-permute-done((f32[2,1024,128]{2,1,0:T(8,128)}, f32[2,1024,128]{2,1,0:T(8,128)}, u32[]{:S(2)}, u32[]{:S(2)}) %collective-permute-start.3) | collective-permute-done | bytes 1048608 | tf_op jit(solution)/shard_map/ppermute | solution.py:24
  143.3 8.5 %all_to_all.70 = bf16[8,128,128]{2,1,0:T(8,128)(2,1)S(1)} all-to-all(bf16[8,128,128]{2,1,0:T(8,128)(2,1)S(1)} %bitcast.197), channel_id=1, replica_groups=mesh['dp'=64,'head'=8] {'head'}, dimensions={0} | all-to-all | bytes 524288 | tf_op jit(solution)/shard_map/all_to_all | solution.py:155
  151.8 3.4 %all-to-all-start.3 = ((bf16[8,128,128]{2,1,0:T(8,128)(2,1)}), bf16[8,128,128]{2,1,0:T(8,128)(2,1)S(1)}, u32[]{:S(2)}, u32[]{:S(2)}) async-start(bf16[8,128,128]{2,1,0:T(8,128)(2,1)} %bitcast.35), calls=%async_computation.3 | async-start | bytes 524288 | tf_op jit(solution)/shard_map/all_to_all | solution.py:156
  159.2 2.0 %all-to-all-done.3 = bf16[8,128,128]{2,1,0:T(8,128)(2,1)S(1)} async-done(((bf16[8,128,128]{2,1,0:T(8,128)(2,1)}), bf16[8,128,128]{2,1,0:T(8,128)(2,1)S(1)}, u32[]{:S(2)}, u32[]{:S(2)}) %all-to-all-start.3) | async-done | bytes 262176 | tf_op jit(solution)/shard_map/all_to_all | solution.py:156
  (74 shorter events, 26.6 us)
Async XLA Ops:
  0.6 32.1 %copy-start.8 = (s32[16]{0:T(128)S(1)}, s32[16]{0:T(128)}, u32[]{:S(2)}) copy-start(s32[16]{0:T(128)} %param.19) | copy-start | bytes 196
  0.6 34.7 %copy-start.9 = (s32[16]{0:T(128)S(1)}, s32[16]{0:T(128)}, u32[]{:S(2)}) copy-start(s32[16]{0:T(128)} %param.18) | copy-start | bytes 196
  0.7 35.3 %copy-start = (bf16[256,1024]{1,0:T(8,128)(2,1)S(1)}, bf16[256,1024]{1,0:T(8,128)(2,1)}, u32[]{:S(2)}) copy-start(bf16[256,1024]{1,0:T(8,128)(2,1)} %param.11) | copy-start | bytes 1572868
  0.7 35.5 %copy-start.1 = (bf16[256,1024]{1,0:T(8,128)(2,1)S(1)}, bf16[256,1024]{1,0:T(8,128)(2,1)}, u32[]{:S(2)}) copy-start(bf16[256,1024]{1,0:T(8,128)(2,1)} %param.14) | copy-start | bytes 1572868
  2.6 12.0 %all-to-all-start = ((bf16[128,8,128]{0,2,1:T(8,128)(2,1)}), bf16[128,8,128]{0,2,1:T(8,128)(2,1)S(1)}, u32[]{:S(2)}, u32[]{:S(2)}) async-start(bf16[128,8,128]{0,2,1:T(8,128)(2,1)} %bitcast.19), calls=%async_computation | async-start | bytes 524288 | tf_op jit(solution)/shard_map/all_to_all | solution.py:98
  8.5 27.9 %copy-start.7 = (s32[256]{0:T(256)S(1)}, s32[256]{0:T(256)}, u32[]{:S(2)}) copy-start(s32[256]{0:T(256)} %param.17) | copy-start | bytes 3076
  14.6 9.4 %all-to-all-start.1 = ((bf16[128,8,128]{0,2,1:T(8,128)(2,1)}), bf16[128,8,128]{0,2,1:T(8,128)(2,1)S(1)}, u32[]{:S(2)}, u32[]{:S(2)}) async-start(bf16[128,8,128]{0,2,1:T(8,128)(2,1)} %bitcast.22), calls=%async_computation.1 | async-start | bytes 524288 | tf_op jit(solution)/shard_map/all_to_all | solution.py:99
  24.3 12.3 %collective-permute-start = (bf16[2,1024,128]{2,1,0:T(8,128)(2,1)S(1)}, bf16[2,1024,128]{2,1,0:T(8,128)(2,1)S(1)}, u32[]{:S(2)}, u32[]{:S(2)}) collective-permute-start(bf16[2,1024,128]{2,1,0:T(8,128)(2,1)S(1)} %pad_maximum_fusion.1), channel_id=1, source_target_pairs={{0,8},{8,0},{16,24},{24,16},{32,40},{40,32},{48,56},{56,48},{64,72... | collective-permute-start | bytes 1572872 | tf_op jit(solution)/shard_map/ppermute | solution.py:24
  36.6 17.2 %copy-start.5 = (bf16[256,128]{1,0:T(8,128)(2,1)S(1)}, bf16[256,128]{1,0:T(8,128)(2,1)}, u32[]{:S(2)}) copy-start(bf16[256,128]{1,0:T(8,128)(2,1)} %param.12) | copy-start | bytes 196612
  36.6 17.2 %copy-start.6 = (bf16[256,128]{1,0:T(8,128)(2,1)S(1)}, bf16[256,128]{1,0:T(8,128)(2,1)}, u32[]{:S(2)}) copy-start(bf16[256,128]{1,0:T(8,128)(2,1)} %param.13) | copy-start | bytes 196612
  36.7 16.9 %collective-permute-start.1 = (bf16[2,1024,128]{2,1,0:T(8,128)(2,1)S(1)}, bf16[2,1024,128]{2,1,0:T(8,128)(2,1)S(1)}, u32[]{:S(2)}, u32[]{:S(2)}) collective-permute-start(bf16[2,1024,128]{2,1,0:T(8,128)(2,1)S(1)} %broadcast_select_fusion), channel_id=1, source_target_pairs={{0,16},{16,0},{8,24},{24,8},{32,48},{48,32},{40,56},{56,40},{64,80... | collective-permute-start | bytes 1572872 | tf_op jit(solution)/shard_map/ppermute | solution.py:24
  39.5 14.5 %copy-start.2 = (bf16[4,256,2,128]{3,1,2,0:T(8,128)(2,1)S(1)}, bf16[4,256,2,128]{3,1,2,0:T(8,128)(2,1)}, u32[]{:S(2)}) copy-start(bf16[4,256,2,128]{3,1,2,0:T(8,128)(2,1)} %custom-call) | copy-start | bytes 1572868
  102.2 0.8 copy-start.3
  107.0 5.0 %collective-permute-start.2 = (f32[2,1024,128]{2,1,0:T(8,128)S(1)}, f32[2,1024,128]{2,1,0:T(8,128)S(1)}, u32[]{:S(2)}, u32[]{:S(2)}) collective-permute-start(f32[2,1024,128]{2,1,0:T(8,128)S(1)} %pad_maximum_fusion), channel_id=1, source_target_pairs={{0,8},{8,0},{16,24},{24,16},{32,40},{40,32},{48,56},{56,48},{64,72... | collective-permute-start | bytes 3145736 | tf_op jit(solution)/shard_map/ppermute | solution.py:24
  113.1 28.1 %collective-permute-start.3 = (f32[2,1024,128]{2,1,0:T(8,128)}, f32[2,1024,128]{2,1,0:T(8,128)}, u32[]{:S(2)}, u32[]{:S(2)}) collective-permute-start(f32[2,1024,128]{2,1,0:T(8,128)} %fusion.65), channel_id=1, source_target_pairs={{0,16},{16,0},{8,24},{24,8},{32,48},{48,32},{40,56},{56,40},{64,80... | collective-permute-start | bytes 3145736 | tf_op jit(solution)/shard_map/ppermute | solution.py:24
  142.5 14.0 %copy-start.4 = (bf16[4,256,2,128]{3,1,2,0:T(8,128)(2,1)S(1)}, bf16[4,256,2,128]{3,1,2,0:T(8,128)(2,1)}, u32[]{:S(2)}) copy-start(bf16[4,256,2,128]{3,1,2,0:T(8,128)(2,1)} %copy-done.3) | copy-start | bytes 1572868
  151.8 9.4 %all-to-all-start.3 = ((bf16[8,128,128]{2,1,0:T(8,128)(2,1)}), bf16[8,128,128]{2,1,0:T(8,128)(2,1)S(1)}, u32[]{:S(2)}, u32[]{:S(2)}) async-start(bf16[8,128,128]{2,1,0:T(8,128)(2,1)} %bitcast.35), calls=%async_computation.3 | async-start | bytes 524288 | tf_op jit(solution)/shard_map/all_to_all | solution.py:156
where the time goes:
time: 164 us; the launch traced here: 162 us
  waiting for transfers between devices  54 us (33%)
  matrix products  47.5 us (29%)
  starting transfers between devices  27.8 us (17%)
  local copies, waits for them, and re-layouts  13 us (8%)
  blocking collectives  8.51 us (5%)
  other arithmetic  7.71 us (5%)
  between operations  3.63 us (2%)
    ppermute x4, waiting for transfers between devices, partner(): return lax.ppermute(block, axis, route)  41.9 us
    ppermute x4, starting transfers between devices, partner(): return lax.ppermute(block, axis, route)  15 us
    dot_general x4, matrix products, one_item(): jnp.einsum('hrk,rhd->kd', weights_low, grad_item, preferred_element_type=...  11.2 us
    sub x4, matrix products, one_item(): exp_terms = jnp.exp(scores - jnp.max(scores, axis=-1, keepdims=True))  10.3 us
    dot_general x4, matrix products, one_item(): jnp.einsum('rhd,kd->hrk', grad_item, value_rows, preferred_element_type=j...  9.68 us
    all_to_all x1, blocking collectives, on_device(): lax.all_to_all(summed[0], 'head', split_axis=0, concat_axis=1, tiled=True)  8.51 us
    dot_general x4, matrix products, one_item(): jnp.einsum('hrk,kd->rhd', weights_low, value_rows, preferred_element_type...  8.44 us
    unnamed x26, local copies, waits for them, and re-layouts  6.63 us
  transfers between devices with their start and end apart: 7, of which 6 were waited for; matrix products, arithmetic and copies ran while one was open for 5% of the time, Pallas kernels for 0%

commit v1 on v0

v1 whole, which is shorter than its diff:
```python
import math

import jax
import jax.numpy as jnp
from jax import lax
from jax.experimental import pallas as pl
from jax.experimental.pallas import tpu as pltpu
from jax.sharding import PartitionSpec as P

HD = 128
QH = 64
KVH = 8
BLOCK = 4
GROUP = QH // KVH
CHUNK = 256
MASKED = -1e30

F32 = jnp.float32
BF16 = jnp.bfloat16
VMEM = pl.BlockSpec(memory_space=pltpu.VMEM)
SMEM = pl.BlockSpec(memory_space=pltpu.SMEM)
PARAMS = pltpu.CompilerParams(vmem_limit_bytes=48 * 1024 * 1024)


def place():
    index = lax.axis_index("dp")
    return index // BLOCK, (index % BLOCK) // 2, index % 2


def call(kernel, outs, *args, scratch=(), flops=0):
    specs = [SMEM if a.dtype == jnp.int32 and a.ndim == 1 else VMEM for a in args]
    size = sum(math.prod(a.shape) * a.dtype.itemsize for a in list(args) + list(outs))
    return pl.pallas_call(
        kernel,
        out_shape=tuple(outs),
        in_specs=specs,
        out_specs=tuple(VMEM for _ in outs),
        scratch_shapes=list(scratch),
        compiler_params=PARAMS,
        cost_estimate=pl.CostEstimate(flops=flops, bytes_accessed=size, transcendentals=0),
    )(*args)


def struct(shape, dtype):
    return jax.ShapeDtypeStruct(shape, dtype)


def half_kernel(key_ref, value_ref, out_ref):
    _, _, core = place()
    half = out_ref.shape[1]
    rows = pl.ds(pl.multiple_of((1 - core) * half, half), half)
    out_ref[0] = key_ref[rows, :]
    out_ref[1] = value_ref[rows, :]


def spread_kernel(owner_ref, key_ref, value_ref, got_ref, out_ref):
    prompt, _, core = place()
    half = got_ref.shape[1]
    rows = pl.ds(pl.multiple_of(core * half, half), half)
    own = owner_ref[prompt] % 2 == core

    @pl.when(own)
    def _():
        for n, ref in enumerate((key_ref, value_ref)):
            for h in range(KVH):
                block = ref[rows, h * HD : (h + 1) * HD]
                out_ref[h, n] = block
                out_ref[KVH + h, n] = block

    @pl.when(jnp.logical_not(own))
    def _():
        for n in range(2):
            for h in range(KVH):
                block = got_ref[n, :, h * HD : (h + 1) * HD]
                out_ref[h, n] = block
                out_ref[KVH + h, n] = block


def side_kernel(owner_ref, got_ref, out_ref):
    prompt, _, _ = place()
    side = owner_ref[prompt] // 2
    out_ref[...] = got_ref[pl.ds(side * KVH, KVH)]


def attention_kernel(
    len_ref, slot_ref, query_ref, grad_ref, own_ref, other_ref, rkey_ref, rvalue_ref,
    dq_ref, drk_ref, drv_ref, part_ref, send_ref,
    key, value, key_t, query, grad, score, dprod, weight, sgrad, bias, rbias,
):
    prompt, _, core = place()
    count = len_ref[prompt]
    rows = query_ref.shape[0]
    pieces, _, half, _ = own_ref.shape
    pre = pieces * half
    total = 2 * pre + rows
    chunks = total // CHUNK
    scale = 1.0 / math.sqrt(HD)
    log_scale = scale * math.log2(math.e)

    for base, ref in ((0, own_ref), (pre, other_ref)):
        for p in range(pieces):
            key[base + p * half : base + (p + 1) * half] = ref[p, 0]
            value[base + p * half : base + (p + 1) * half] = ref[p, 1]
    key[2 * pre :] = rkey_ref[...]
    value[2 * pre :] = rvalue_ref[...]
    for k in range(chunks):
        cut = slice(k * CHUNK, (k + 1) * CHUNK)
        key_t[:, cut] = key[cut].astype(F32).T.astype(BF16)
    for g in range(GROUP):
        query[g * rows : (g + 1) * rows] = query_ref[:, g * HD : (g + 1) * HD]
        grad[g * rows : (g + 1) * rows] = grad_ref[:, g * HD : (g + 1) * HD]

    column = lax.broadcasted_iota(jnp.int32, (pre, HD), 0)
    for n, which in enumerate((core, 1 - core)):
        position = (column // half) * (2 * half) + which * half + column % half
        bias[n * pre : (n + 1) * pre] = jnp.where(position < count, 0.0, MASKED).astype(F32)
    slot = slot_ref[...].astype(F32)
    slot_row = jnp.broadcast_to(slot, (rows, rows))
    slot_col = slot_row.T
    at_key = lax.broadcasted_iota(jnp.int32, (rows, rows), 0)
    at_row = lax.broadcasted_iota(jnp.int32, (rows, rows), 1)
    seen = jnp.logical_and(slot_row == slot_col, at_key <= at_row)
    rbias[...] = jnp.where(seen, 0.0, MASKED).astype(F32)
    live = jnp.where(slot < BLOCK, 1.0, 0.0).astype(F32)

    def head(g, carry):
        at = pl.ds(pl.multiple_of(g * rows, rows), rows)
        query_g = query[at]
        grad_g = grad[at]
        top = jnp.full((1, rows), -jnp.inf, F32)
        for k in range(chunks):
            cut = slice(k * CHUNK, (k + 1) * CHUNK)
            s = lax.dot_general(key[cut], query_g, (((1,), (1,)), ((), ())), preferred_element_type=F32)
            if k == chunks - 1:
                s = s + rbias[...]
            else:
                b = bias[cut]
                s = s + jnp.concatenate([b, b], axis=1)
            score[cut] = s
            top = jnp.maximum(top, jnp.max(s, axis=0, keepdims=True))
        denom = jnp.zeros((1, rows), F32)
        dot = jnp.zeros((1, rows), F32)
        for k in range(chunks):
            cut = slice(k * CHUNK, (k + 1) * CHUNK)
            e = jnp.exp2((score[cut] - top) * log_scale)
            d = lax.dot_general(value[cut], grad_g, (((1,), (1,)), ((), ())), preferred_element_type=F32)
            denom = denom + jnp.sum(e, axis=0, keepdims=True)
            dot = dot + jnp.sum(e * d, axis=0, keepdims=True)
            score[cut] = e
            dprod[cut] = d
        inverse = live / denom
        dot = dot * inverse
        dq = jnp.zeros((HD, rows), F32)
        for k in range(chunks):
            cut = slice(k * CHUNK, (k + 1) * CHUNK)
            w = score[cut] * inverse
            weight[cut, at] = w.astype(BF16)
            ds = (w * (dprod[cut] - dot)).astype(BF16)
            sgrad[cut, at] = ds
            dq = dq + jnp.dot(key_t[:, cut], ds, preferred_element_type=F32)
        lanes = pl.ds(pl.multiple_of(g * HD, HD), HD)
        dq_ref[:, lanes] = (dq * scale).T.astype(BF16)
        return carry

    lax.fori_loop(0, GROUP, head, 0)

    def grads(k):
        cut = slice(k * CHUNK, (k + 1) * CHUNK)
        dk = jnp.dot(sgrad[cut], query[...], preferred_element_type=F32) * scale
        dv = jnp.dot(weight[cut], grad[...], preferred_element_type=F32)
        return dk, dv

    drk, drv = grads(chunks - 1)
    drk_ref[...] = drk.astype(BF16)
    drv_ref[...] = drv.astype(BF16)
    per = CHUNK // half
    for ref, base in ((part_ref, 0), (send_ref, pre // CHUNK)):
        for k in range(pre // CHUNK):
            dk, dv = grads(base + k)
            for p in range(per):
                ref[k * per + p, 0] = dk[p * half : (p + 1) * half].astype(ref.dtype)
                ref[k * per + p, 1] = dv[p * half : (p + 1) * half].astype(ref.dtype)


def chip_sum_kernel(part_ref, got_ref, out_ref):
    for h in range(KVH):
        block = (part_ref[h] + got_ref[h].astype(F32)).astype(BF16)
        out_ref[h] = block
        out_ref[KVH + h] = block


def prompt_sum_kernel(got_ref, out_ref):
    for n in range(2):
        for h in range(KVH):
            block = got_ref[h, n].astype(F32) + got_ref[KVH + h, n].astype(F32)
            out_ref[n, :, h * HD : (h + 1) * HD] = block.astype(BF16)


def final_kernel(owner_ref, mine_ref, got_ref, dk_ref, dv_ref):
    prompt, side, core = place()
    half = mine_ref.shape[1]
    own = owner_ref[prompt] == side * 2 + core
    mine = pl.ds(pl.multiple_of(core * half, half), half)
    other = pl.ds(pl.multiple_of((1 - core) * half, half), half)

    @pl.when(own)
    def _():
        for n, ref in enumerate((dk_ref, dv_ref)):
            ref[mine, :] = mine_ref[n]
            ref[other, :] = got_ref[n]

    @pl.when(jnp.logical_not(own))
    def _():
        for ref in (dk_ref, dv_ref):
            ref[...] = jnp.zeros_like(ref)


def on_device(
    queries,
    resp_keys,
    resp_values,
    out_grad,
    prefix_keys,
    prefix_values,
    resp_slot,
    prefix_len,
    prefix_owner,
):
    dp, heads = lax.axis_size("dp"), lax.axis_size("head")
    rows = queries.shape[0]
    local, width = prefix_keys.shape
    half = local // 2
    total = local * heads + rows
    swap = [(d, d ^ 1) for d in range(dp)]
    groups = [
        [(base + 2 * side + core) * heads + h for side in range(2) for h in range(heads)]
        for base in range(0, dp, BLOCK)
        for core in range(2)
    ]

    def exchange(block):
        flat = block.reshape(2 * heads, 2 * half, HD)
        flat = lax.all_to_all(flat, ("dp", "head"), 0, 0, axis_index_groups=groups, tiled=True)
        return flat.reshape(block.shape)

    piece = (heads, 2, half, HD)
    (sent,) = call(half_kernel, [struct((2, half, width), BF16)], prefix_keys, prefix_values)
    got = lax.ppermute(sent, "dp", swap)
    (spread,) = call(
        spread_kernel, [struct((2 * heads, 2, half, HD), BF16)], prefix_owner, prefix_keys, prefix_values, got
    )
    arrived = exchange(spread)
    (own,) = call(side_kernel, [struct(piece, BF16)], prefix_owner, arrived)
    other = lax.ppermute(own, "dp", swap)
    dq, drk, drv, part, send = call(
        attention_kernel,
        [
            struct(queries.shape, BF16),
            struct(resp_keys.shape, BF16),
            struct(resp_values.shape, BF16),
            struct(piece, F32),
            struct(piece, BF16),
        ],
        prefix_len,
        resp_slot.reshape(1, rows),
        queries,
        out_grad,
        own,
        other,
        resp_keys,
        resp_values,
        scratch=[
            pltpu.VMEM((total, HD), BF16),
            pltpu.VMEM((total, HD), BF16),
            pltpu.VMEM((HD, total), BF16),
            pltpu.VMEM((GROUP * rows, HD), BF16),
            pltpu.VMEM((GROUP * rows, HD), BF16),
            pltpu.VMEM((total, rows), F32),
            pltpu.VMEM((total, rows), F32),
            pltpu.VMEM((total, GROUP * rows), BF16),
            pltpu.VMEM((total, GROUP * rows), BF16),
            pltpu.VMEM((local * heads, HD), F32),
            pltpu.VMEM((rows, rows), F32),
        ],
        flops=10 * GROUP * rows * total * HD,
    )
    got = lax.ppermute(send, "dp", swap)
    (spread,) = call(chip_sum_kernel, [struct((2 * heads, 2, half, HD), BF16)], part, got)
    arrived = exchange(spread)
    (mine,) = call(prompt_sum_kernel, [struct((2, half, width), BF16)], arrived)
    got = lax.ppermute(mine, "dp", swap)
    dk, dv = call(
        final_kernel,
        [struct(prefix_keys.shape, BF16), struct(prefix_values.shape, BF16)],
        prefix_owner,
        mine,
        got,
    )
    return dq, drk, drv, dk, dv


def solution(mesh):
    placed = (
        P("dp", "head"),
        P("dp", "head"),
        P("dp", "head"),
        P("dp", "head"),
        P(("dp", "head"), None),
        P(("dp", "head"), None),
        P("dp"),
        P(),
        P(),
    )
    return jax.shard_map(
        on_device,
        mesh=mesh,
        in_specs=placed,
        out_specs=(
            P("dp", "head"),
            P("dp", "head"),
            P("dp", "head"),
            P(("dp", "head"), None),
            P(("dp", "head"), None),
        ),
        check_vma=False,
    )
```

time: 164 us -> 71.4 us (0.44)
  waiting for transfers between devices: 54 us -> 4.56 us
  matrix products: 47.5 us -> 0 us
  Pallas kernels: 0 us -> 18.3 us
  blocking collectives: 8.51 us -> 26.3 us
  local copies, waits for them, and re-layouts: 13 us -> 1.93 us
  starting transfers between devices: 27.8 us -> 19.2 us
  other arithmetic: 7.71 us -> 0 us
  between operations: 3.63 us -> 0.76 us
    ppermute x4, waiting for transfers between devices: 41.9 us -> 4.56 us  [the longest x1 1.14 us: on_device(): got = lax.ppermute(sent, 'dp', swap)]
    dot_general x20 -> x0, matrix products: 37.2 us -> none  [the longest x4 11.2 us: one_item(): jnp.einsum('hrk,rhd->kd', weights_low, grad_item, preferred_element_type=...]
    pallas_call x0 -> x7, Pallas kernels: none -> 18.3 us  [call(): pl.pallas_call(kernel, out_shape=tuple(outs), in_specs=specs, out_specs=t...]
    all_to_all x1 -> x2, blocking collectives: 8.51 us -> 26.3 us  [exchange(): lax.all_to_all(flat, ('dp', 'head'), 0, 0, axis_index_groups=groups, tile...]
    all_to_all x3 -> x0, starting transfers between devices: 12.8 us -> none  [the longest x1 5.95 us: on_device(): lax.all_to_all(prefix_keys, 'head', split_axis=1, concat_axis=0, tiled=True)]
    all_to_all x3 -> x0, waiting for transfers between devices: 12.1 us -> none  [the longest x1 5.82 us: on_device(): lax.all_to_all(prefix_values, 'head', split_axis=1, concat_axis=0, tiled=...]
    sub x4 -> x0, matrix products: 10.3 us -> none  [one_item(): exp_terms = jnp.exp(scores - jnp.max(scores, axis=-1, keepdims=True))]
    unnamed x26 -> x18, local copies, waits for them, and re-layouts: 6.63 us -> 1.93 us
  transfers between devices with their start and end apart: 7 -> 4, of which waited for: 6 -> 4; matrix products, arithmetic and copies ran while one was open for 5% -> 0% of each run, Pallas kernels for 0% -> 0%
where the time goes in v1:
time: 71.4 us; the launch traced here: 71.1 us
  blocking collectives  26.3 us (37%)
  starting transfers between devices  19.2 us (27%)
  Pallas kernels  18.3 us (26%)
  waiting for transfers between devices  4.56 us (6%)
  local copies, waits for them, and re-layouts  1.93 us (3%)
  between operations  0.76 us (1%)
    all_to_all x2, blocking collectives, exchange(): lax.all_to_all(flat, ('dp', 'head'), 0, 0, axis_index_groups=groups, tile...  26.3 us
    pallas_call x7, Pallas kernels, call(): pl.pallas_call(kernel, out_shape=tuple(outs), in_specs=specs, out_specs=t...  18.3 us
    ppermute x1, starting transfers between devices, on_device(): got = lax.ppermute(sent, 'dp', swap)  8.79 us
    ppermute x1, starting transfers between devices, on_device(): other = lax.ppermute(own, 'dp', swap)  4.08 us
    ppermute x1, starting transfers between devices, on_device(): got = lax.ppermute(mine, 'dp', swap)  4 us
    ppermute x1, starting transfers between devices, on_device(): got = lax.ppermute(send, 'dp', swap)  2.3 us
    unnamed x18, local copies, waits for them, and re-layouts  1.93 us
  transfers between devices with their start and end apart: 4, of which 4 were waited for; matrix products, arithmetic and copies ran while one was open for 0% of the time, Pallas kernels for 0%

profile of v1, /device:TPU:1, one launch (start us, length us, event | category | flops | bytes accessed | tf_op | source)
XLA Modules:
  0.0 71.1 jit_solution(10756617592647827778)
XLA Ops:
  0.6 0.0 copy-start
  0.6 0.9 %copy-done = bf16[128,1024]{1,0:T(8,128)(2,1)S(1)} copy-done((bf16[128,1024]{1,0:T(8,128)(2,1)S(1)}, bf16[128,1024]{1,0:T(8,128)(2,1)}, u32[]{:S(2)}) %copy-start) | copy-done | bytes 262168
  1.6 0.0 copy-start.1
  1.6 0.9 %copy-done.1 = bf16[128,1024]{1,0:T(8,128)(2,1)S(1)} copy-done((bf16[128,1024]{1,0:T(8,128)(2,1)S(1)}, bf16[128,1024]{1,0:T(8,128)(2,1)}, u32[]{:S(2)}) %copy-start.1) | copy-done | bytes 262168
  2.5 0.0 copy-start.2
  2.6 8.8 %collective-permute-start = (bf16[2,64,1024]{2,1,0:T(8,128)(2,1)S(1)}, bf16[2,64,1024]{2,1,0:T(8,128)(2,1)S(1)}, u32[]{:S(2)}, u32[]{:S(2)}) collective-permute-start(bf16[2,64,1024]{2,1,0:T(8,128)(2,1)S(1)} %shard_map.128), channel_id=1, source_target_pairs={{0,8},{8,0},{16,24},{24,16},{32,40},{40,32},{48,56},{56,48},{64,72... | collective-permute-start | bytes 786440 | tf_op jit(solution)/shard_map/ppermute | solution.py:248
  11.4 1.1 %collective-permute-done.got_ref = bf16[2,64,1024]{2,1,0:T(8,128)(2,1)S(1)} collective-permute-done((bf16[2,64,1024]{2,1,0:T(8,128)(2,1)S(1)}, bf16[2,64,1024]{2,1,0:T(8,128)(2,1)S(1)}, u32[]{:S(2)}, u32[]{:S(2)}) %collective-permute-start) | collective-permute-done | bytes 262176 | tf_op jit(solution)/shard_map/ppermute | solution.py:248
  12.5 0.0 copy-done.2
  12.5 0.6 shard_map.129
  13.1 0.0 copy-start.4
  13.2 13.0 %all_to_all.10 = bf16[16,128,128]{2,1,0:T(8,128)(2,1)S(1)} all-to-all(bf16[16,128,128]{2,1,0:T(8,128)(2,1)S(1)} %bitcast.5), channel_id=1, replica_groups={{0,1,2,3,4,5,6,7,16,17,18,19,20,21,22,23},{8,9,10,11,12,13,14,15,24,25,..., dimensions={0} | all-to-all | bytes 1048576 | tf_op jit(solution)/shard_map/all_to_all | solution.py:243
  26.2 0.0 copy-start.3
  26.2 0.6 shard_map.130.own_ref
  26.8 0.0 copy-start.7
  26.8 0.0 copy-start.8
  26.8 4.1 %collective-permute-start.1 = (bf16[8,2,64,128]{3,2,1,0:T(8,128)(2,1)S(1)}, bf16[8,2,64,128]{3,2,1,0:T(8,128)(2,1)S(1)}, u32[]{:S(2)}, u32[]{:S(2)}) collective-permute-start(bf16[8,2,64,128]{3,2,1,0:T(8,128)(2,1)S(1)} %shard_map.130.own_ref), channel_id=1, source_target_pairs={{0,8},{8,0},{16,24},{24,16},{32,40},{40,32},{48,56},{56,48},{64,72... | collective-permute-start | bytes 786440 | tf_op jit(solution)/shard_map/ppermute | solution.py:254
  30.9 1.1 %collective-permute-done.1.other_ref = bf16[8,2,64,128]{3,2,1,0:T(8,128)(2,1)S(1)} collective-permute-done((bf16[8,2,64,128]{3,2,1,0:T(8,128)(2,1)S(1)}, bf16[8,2,64,128]{3,2,1,0:T(8,128)(2,1)S(1)}, u32[]{:S(2)}, u32[]{:S(2)}) %collective-permute-start.1) | collective-permute-done | bytes 262176 | tf_op jit(solution)/shard_map/ppermute | solution.py:254
  32.0 0.0 copy-done.4
  32.0 0.0 copy-done.3
  32.0 0.0 copy-done.5
  32.0 0.0 copy-done.6
  32.0 0.0 copy-done.7
  32.0 0.0 copy-done.8
  32.1 15.6 %shard_map.131 = (bf16[256,1024]{1,0:T(8,128)(2,1)}, bf16[256,128]{1,0:T(8,128)(2,1)}, bf16[256,128]{1,0:T(8,128)(2,1)}, f32[8,2,64,128]{3,2,1,0:T(8,128)S(1)}, bf16[8,2,64,128]{3,2,1,0:T(8,128)(2,1)S(1)}) custom-call(s32[16]{0:T(128)S(1)} %copy-done.8, s32[1,256]{1,0:T(1,128)S(1)} %bitcast.9, bf16[256,1024]{1,0:T(8,128)(2,1)S(1)} %copy-done.3, ...), custom_call_target="tpu_custom_call" | custom-call | flops 3355443200 | bytes 3146816 | tf_op jit(solution)/shard_map/pallas_call | solution.py:33
  47.6 2.3 %collective-permute-start.2 = (bf16[8,2,64,128]{3,2,1,0:T(8,128)(2,1)S(1)}, bf16[8,2,64,128]{3,2,1,0:T(8,128)(2,1)S(1)}, u32[]{:S(2)}, u32[]{:S(2)}) collective-permute-start(bf16[8,2,64,128]{3,2,1,0:T(8,128)(2,1)S(1)} %get-tuple-element.16), channel_id=1, source_target_pairs={{0,8},{8,0},{16,24},{24,16},{32,40},{40,32},{48,56},{56,48},{64,72... | collective-permute-start | bytes 786440 | tf_op jit(solution)/shard_map/ppermute | solution.py:287
  50.0 1.1 %collective-permute-done.2.got_ref = bf16[8,2,64,128]{3,2,1,0:T(8,128)(2,1)S(1)} collective-permute-done((bf16[8,2,64,128]{3,2,1,0:T(8,128)(2,1)S(1)}, bf16[8,2,64,128]{3,2,1,0:T(8,128)(2,1)S(1)}, u32[]{:S(2)}, u32[]{:S(2)}) %collective-permute-start.2) | collective-permute-done | bytes 262176 | tf_op jit(solution)/shard_map/ppermute | solution.py:287
  51.1 0.1 shard_map.132
  51.2 13.3 %all_to_all.11 = bf16[16,128,128]{2,1,0:T(8,128)(2,1)S(1)} all-to-all(bf16[16,128,128]{2,1,0:T(8,128)(2,1)S(1)} %bitcast.6), channel_id=1, replica_groups={{0,1,2,3,4,5,6,7,16,17,18,19,20,21,22,23},{8,9,10,11,12,13,14,15,24,25,..., dimensions={0} | all-to-all | bytes 1048576 | tf_op jit(solution)/shard_map/all_to_all | solution.py:243
  64.5 0.1 shard_map.133.mine_ref
  64.6 4.0 %collective-permute-start.3 = (bf16[2,64,1024]{2,1,0:T(8,128)(2,1)S(1)}, bf16[2,64,1024]{2,1,0:T(8,128)(2,1)S(1)}, u32[]{:S(2)}, u32[]{:S(2)}) collective-permute-start(bf16[2,64,1024]{2,1,0:T(8,128)(2,1)S(1)} %shard_map.133.mine_ref), channel_id=1, source_target_pairs={{0,8},{8,0},{16,24},{24,16},{32,40},{40,32},{48,56},{56,48},{64,72... | collective-permute-start | bytes 786440 | tf_op jit(solution)/shard_map/ppermute | solution.py:291
  68.6 1.1 %collective-permute-done.3.got_ref = bf16[2,64,1024]{2,1,0:T(8,128)(2,1)S(1)} collective-permute-done((bf16[2,64,1024]{2,1,0:T(8,128)(2,1)S(1)}, bf16[2,64,1024]{2,1,0:T(8,128)(2,1)S(1)}, u32[]{:S(2)}, u32[]{:S(2)}) %collective-permute-start.3) | collective-permute-done | bytes 262176 | tf_op jit(solution)/shard_map/ppermute | solution.py:291
  69.7 1.4 %shard_map.134 = (bf16[128,1024]{1,0:T(8,128)(2,1)}, bf16[128,1024]{1,0:T(8,128)(2,1)}) custom-call(s32[16]{0:T(128)S(1)} %copy-done.2, bf16[2,64,1024]{2,1,0:T(8,128)(2,1)S(1)} %shard_map.133.mine_ref, bf16[2,64,1024]{2,1,0:T(8,128)(2,1)S(1)} %collective-permute-done.3.got_ref), custom_call_target="tpu_custom_call" | custom-call | bytes 1048640 | tf_op jit(solution)/shard_map/pallas_call | solution.py:33
  (3 shorter events, 0.0 us)
Async XLA Ops:
  0.6 1.0 %copy-start = (bf16[128,1024]{1,0:T(8,128)(2,1)S(1)}, bf16[128,1024]{1,0:T(8,128)(2,1)}, u32[]{:S(2)}) copy-start(bf16[128,1024]{1,0:T(8,128)(2,1)} %key_ref.3) | copy-start | bytes 786436
  1.6 0.9 %copy-start.1 = (bf16[128,1024]{1,0:T(8,128)(2,1)S(1)}, bf16[128,1024]{1,0:T(8,128)(2,1)}, u32[]{:S(2)}) copy-start(bf16[128,1024]{1,0:T(8,128)(2,1)} %value_ref.3) | copy-start | bytes 786436
  2.5 10.0 %copy-start.2 = (s32[16]{0:T(128)S(1)}, s32[16]{0:T(128)}, u32[]{:S(2)}) copy-start(s32[16]{0:T(128)} %owner_ref.5) | copy-start | bytes 196
  2.6 9.9 %collective-permute-start = (bf16[2,64,1024]{2,1,0:T(8,128)(2,1)S(1)}, bf16[2,64,1024]{2,1,0:T(8,128)(2,1)S(1)}, u32[]{:S(2)}, u32[]{:S(2)}) collective-permute-start(bf16[2,64,1024]{2,1,0:T(8,128)(2,1)S(1)} %shard_map.128), channel_id=1, source_target_pairs={{0,8},{8,0},{16,24},{24,16},{32,40},{40,32},{48,56},{56,48},{64,72... | collective-permute-start | bytes 786440 | tf_op jit(solution)/shard_map/ppermute | solution.py:248
  13.1 18.9 %copy-start.4 = (bf16[256,1024]{1,0:T(8,128)(2,1)S(1)}, bf16[256,1024]{1,0:T(8,128)(2,1)}, u32[]{:S(2)}) copy-start(bf16[256,1024]{1,0:T(8,128)(2,1)} %grad_ref.1) | copy-start | bytes 1572868
  26.2 5.9 %copy-start.3 = (bf16[256,1024]{1,0:T(8,128)(2,1)S(1)}, bf16[256,1024]{1,0:T(8,128)(2,1)}, u32[]{:S(2)}) copy-start(bf16[256,1024]{1,0:T(8,128)(2,1)} %query_ref.1) | copy-start | bytes 1572868
  26.2 5.9 %copy-start.5 = (bf16[256,128]{1,0:T(8,128)(2,1)S(1)}, bf16[256,128]{1,0:T(8,128)(2,1)}, u32[]{:S(2)}) copy-start(bf16[256,128]{1,0:T(8,128)(2,1)} %rkey_ref.1) | copy-start | bytes 196612
  26.2 5.9 %copy-start.6 = (bf16[256,128]{1,0:T(8,128)(2,1)S(1)}, bf16[256,128]{1,0:T(8,128)(2,1)}, u32[]{:S(2)}) copy-start(bf16[256,128]{1,0:T(8,128)(2,1)} %rvalue_ref.1) | copy-start | bytes 196612
  26.8 5.3 %copy-start.7 = (s32[256]{0:T(256)S(1)}, s32[256]{0:T(256)}, u32[]{:S(2)}) copy-start(s32[256]{0:T(256)} %param.15) | copy-start | bytes 3076
  26.8 5.3 %copy-start.8 = (s32[16]{0:T(128)S(1)}, s32[16]{0:T(128)}, u32[]{:S(2)}) copy-start(s32[16]{0:T(128)} %len_ref.1) | copy-start | bytes 196
  26.8 5.2 %collective-permute-start.1 = (bf16[8,2,64,128]{3,2,1,0:T(8,128)(2,1)S(1)}, bf16[8,2,64,128]{3,2,1,0:T(8,128)(2,1)S(1)}, u32[]{:S(2)}, u32[]{:S(2)}) collective-permute-start(bf16[8,2,64,128]{3,2,1,0:T(8,128)(2,1)S(1)} %shard_map.130.own_ref), channel_id=1, source_target_pairs={{0,8},{8,0},{16,24},{24,16},{32,40},{40,32},{48,56},{56,48},{64,72... | collective-permute-start | bytes 786440 | tf_op jit(solution)/shard_map/ppermute | solution.py:254
  47.6 3.4 %collective-permute-start.2 = (bf16[8,2,64,128]{3,2,1,0:T(8,128)(2,1)S(1)}, bf16[8,2,64,128]{3,2,1,0:T(8,128)(2,1)S(1)}, u32[]{:S(2)}, u32[]{:S(2)}) collective-permute-start(bf16[8,2,64,128]{3,2,1,0:T(8,128)(2,1)S(1)} %get-tuple-element.16), channel_id=1, source_target_pairs={{0,8},{8,0},{16,24},{24,16},{32,40},{40,32},{48,56},{56,48},{64,72... | collective-permute-start | bytes 786440 | tf_op jit(solution)/shard_map/ppermute | solution.py:287
  64.6 5.1 %collective-permute-start.3 = (bf16[2,64,1024]{2,1,0:T(8,128)(2,1)S(1)}, bf16[2,64,1024]{2,1,0:T(8,128)(2,1)S(1)}, u32[]{:S(2)}, u32[]{:S(2)}) collective-permute-start(bf16[2,64,1024]{2,1,0:T(8,128)(2,1)S(1)} %shard_map.133.mine_ref), channel_id=1, source_target_pairs={{0,8},{8,0},{16,24},{24,16},{32,40},{40,32},{48,56},{56,48},{64,72... | collective-permute-start | bytes 786440 | tf_op jit(solution)/shard_map/ppermute | solution.py:291

commit v2 on v1

v2 whole, which is shorter than its diff:
```python
import math

import jax
import jax.numpy as jnp
from jax import lax
from jax.experimental import pallas as pl
from jax.experimental.pallas import tpu as pltpu
from jax.sharding import PartitionSpec as P

HD = 128
QH = 64
KVH = 8
BLOCK = 4
GROUP = QH // KVH
CHUNK = 256
MASKED = -1e30

F32 = jnp.float32
BF16 = jnp.bfloat16
VMEM = pl.BlockSpec(memory_space=pltpu.VMEM)
HBM = pl.BlockSpec(memory_space=pltpu.HBM)
PARAMS = pltpu.CompilerParams(vmem_limit_bytes=48 * 1024 * 1024)


def place():
    index = lax.axis_index("dp")
    return index // BLOCK, (index % BLOCK) // 2, index % 2


def owner_of(ref):
    prompt, _, _ = place()
    lane = lax.broadcasted_iota(jnp.int32, ref.shape, 1)
    return jnp.sum(jnp.where(lane == prompt, ref[...], 0).astype(F32)).astype(jnp.int32)


def nt(a, b):
    return lax.dot_general(a, b, (((1,), (1,)), ((), ())), preferred_element_type=F32)


def nn(a, b):
    return jnp.dot(a, b, preferred_element_type=F32)


def call(kernel, outs, *args, specs=None, scratch=(), flops=0):
    size = sum(math.prod(a.shape) * a.dtype.itemsize for a in list(args) + list(outs))
    return pl.pallas_call(
        kernel,
        out_shape=tuple(outs),
        in_specs=specs or [VMEM for _ in args],
        out_specs=tuple(VMEM for _ in outs),
        scratch_shapes=list(scratch),
        compiler_params=PARAMS,
        cost_estimate=pl.CostEstimate(flops=flops, bytes_accessed=size, transcendentals=0),
    )(*args)


def struct(shape, dtype):
    return jax.ShapeDtypeStruct(shape, dtype)


def spread_kernel(key_ref, value_ref, out_ref, sems):
    copies = []
    for n, ref in enumerate((key_ref, value_ref)):
        for h in range(KVH):
            for side in range(2):
                source = ref.at[:, h * HD : (h + 1) * HD]
                target = out_ref.at[side * KVH + h, n]
                copies.append(pltpu.make_async_copy(source, target, sems.at[len(copies)]))
    for copy in copies:
        copy.start()
    for copy in copies:
        copy.wait()


def side_kernel(owner_ref, got_ref, out_ref):
    side = owner_of(owner_ref) // 2

    @pl.when(side == 0)
    def _():
        out_ref[...] = got_ref[:KVH]

    @pl.when(side == 1)
    def _():
        out_ref[...] = got_ref[KVH:]


def prepare_kernel(len_ref, slot_ref, query_ref, grad_ref, query_t, grad_t, bias, rbias):
    rows = query_ref.shape[0]
    for g in range(GROUP):
        at = slice(g * rows, (g + 1) * rows)
        lanes = slice(g * HD, (g + 1) * HD)
        query_t[:, at] = query_ref[:, lanes].T
        grad_t[:, at] = grad_ref[:, lanes].T
    prompt, _, _ = place()
    lane = lax.broadcasted_iota(jnp.int32, len_ref.shape, 1)
    count = jnp.sum(jnp.where(lane == prompt, len_ref[...], 0).astype(F32), axis=1, keepdims=True)
    column = lax.broadcasted_iota(jnp.int32, bias.shape, 0).astype(F32)
    bias[...] = jnp.where(column < count, 0.0, MASKED).astype(F32)
    slot_row = jnp.broadcast_to(slot_ref[...].astype(F32), (rows, rows))
    slot_col = slot_row.T
    at_key = lax.broadcasted_iota(jnp.int32, (rows, rows), 0)
    at_row = lax.broadcasted_iota(jnp.int32, (rows, rows), 1)
    seen = jnp.logical_and(slot_row == slot_col, at_key <= at_row)
    rbias[...] = jnp.where(seen, 0.0, MASKED).astype(F32)


def attention_kernel(
    owner_ref, slot_ref, query, grad, bias, rbias, own_ref, other_ref, rkey_ref, rvalue_ref,
    dq_ref, drk_ref, drv_ref, part_ref,
    key, value, key_t, value_t, query_s, grad_s, score, weight, sgrad, factor,
):
    _, _, core = place()
    rows = slot_ref.shape[1]
    pieces, _, local, _ = own_ref.shape
    pre = pieces * local
    total = pre + rows
    chunks = total // CHUNK
    scale = 1.0 / math.sqrt(HD)
    log_scale = scale * math.log2(math.e)
    live = jnp.where(slot_ref[...] < BLOCK, 1.0, 0.0).astype(F32)

    def take(ref):
        for p in range(pieces):
            key[p * local : (p + 1) * local] = ref[p, 0]
            value[p * local : (p + 1) * local] = ref[p, 1]

    own = owner_of(owner_ref) % 2 == core
    pl.when(own)(lambda: take(own_ref))
    pl.when(jnp.logical_not(own))(lambda: take(other_ref))
    key[pre:] = rkey_ref[...]
    value[pre:] = rvalue_ref[...]

    def cut(k):
        return slice(k * CHUNK, (k + 1) * CHUNK)

    def at(g):
        return slice(g * rows, (g + 1) * rows)

    for k in range(chunks):
        key_t[:, cut(k)] = key[cut(k)].T
        value_t[:HD, cut(k)] = value[cut(k)].T
    value_t[HD:] = jnp.ones((value_t.shape[0] - HD, total), BF16)

    tops, dots = {}, {}

    def scores(g, k):
        s = nn(key[cut(k)], query[:, at(g)])
        if k == chunks - 1:
            s = s + rbias[...]
        else:
            b = bias[cut(k)]
            s = s + jnp.concatenate([b] * (rows // HD), axis=1)
        score[g % 2, cut(k)] = s
        top = jnp.max(s, axis=0, keepdims=True)
        tops[g] = top if k == 0 else jnp.maximum(tops[g], top)

    def weights(g, k):
        weight[cut(k), at(g)] = jnp.exp2((score[g % 2, cut(k)] - tops[g]) * log_scale).astype(BF16)

    def attend(g):
        both = nn(value_t[...], weight[:, at(g)])
        denom = both[HD : HD + 1]
        inverse = live / denom
        dots[g] = jnp.sum(both[:HD] * grad[:, at(g)].astype(F32), axis=0, keepdims=True) / denom
        factor[:, at(g)] = inverse * scale
        query_s[:, at(g)] = (query[:, at(g)].astype(F32) * (inverse * scale)).astype(BF16)
        grad_s[:, at(g)] = (grad[:, at(g)].astype(F32) * inverse).astype(BF16)

    def score_grads(g, k):
        d = nn(value[cut(k)], grad[:, at(g)])
        sgrad[cut(k), at(g)] = weight[cut(k), at(g)] * (d - dots[g]).astype(BF16)

    for t in range(GROUP + 2):
        for k in range(chunks):
            if t < GROUP:
                scores(t, k)
            if 1 <= t <= GROUP:
                weights(t - 1, k)
            if t >= 2:
                score_grads(t - 2, k)
        if 1 <= t <= GROUP:
            attend(t - 1)

    for k in range(chunks):
        dk = nt(query_s[...], sgrad[cut(k)])
        dv = nt(grad_s[...], weight[cut(k)])
        if k == chunks - 1:
            drk_ref[...] = dk.T.astype(BF16)
            drv_ref[...] = dv.T.astype(BF16)
        else:
            for p in range(CHUNK // local):
                for n, d in enumerate((dk, dv)):
                    block = d[:, p * local : (p + 1) * local].T.astype(BF16)
                    part_ref[k * (CHUNK // local) + p, n] = block
                    part_ref[pieces + k * (CHUNK // local) + p, n] = block
    for g in range(GROUP):
        dq = nn(key_t[...], sgrad[:, at(g)]) * factor[:, at(g)]
        dq_ref[:, g * HD : (g + 1) * HD] = dq.T.astype(BF16)


def side_sum_kernel(got_ref, out_ref):
    for n in range(2):
        for h in range(KVH):
            block = got_ref[h, n].astype(F32) + got_ref[KVH + h, n].astype(F32)
            out_ref[n, :, h * HD : (h + 1) * HD] = block.astype(BF16)


def final_kernel(owner_ref, mine_ref, got_ref, dk_ref, dv_ref):
    _, side, core = place()
    own = owner_of(owner_ref) == side * 2 + core

    @pl.when(own)
    def _():
        for n, ref in enumerate((dk_ref, dv_ref)):
            ref[...] = (mine_ref[n].astype(F32) + got_ref[n].astype(F32)).astype(BF16)

    @pl.when(jnp.logical_not(own))
    def _():
        for ref in (dk_ref, dv_ref):
            ref[...] = jnp.zeros_like(ref)


def on_device(
    queries,
    resp_keys,
    resp_values,
    out_grad,
    prefix_keys,
    prefix_values,
    resp_slot,
    prefix_len,
    prefix_owner,
):
    dp, heads = lax.axis_size("dp"), lax.axis_size("head")
    rows = queries.shape[0]
    local, width = prefix_keys.shape
    pre = local * heads
    total = pre + rows
    swap = [(d, d ^ 1) for d in range(dp)]
    groups = [
        [(base + 2 * side + core) * heads + h for side in range(2) for h in range(heads)]
        for base in range(0, dp, BLOCK)
        for core in range(2)
    ]

    def exchange(block):
        flat = block.reshape(2 * heads, 2 * local, HD)
        flat = lax.all_to_all(flat, ("dp", "head"), 0, 0, axis_index_groups=groups, tiled=True)
        return flat.reshape(block.shape)

    owner = prefix_owner.reshape(1, -1)
    slot = resp_slot.reshape(1, rows)
    both = (2 * heads, 2, local, HD)
    (spread,) = call(
        spread_kernel,
        [struct(both, BF16)],
        prefix_keys,
        prefix_values,
        specs=[HBM, HBM],
        scratch=[pltpu.SemaphoreType.DMA((4 * heads,))],
    )
    (own,) = call(side_kernel, [struct((heads, 2, local, HD), BF16)], owner, exchange(spread))
    other = lax.ppermute(own, "dp", swap)
    query_t, grad_t, bias, rbias = call(
        prepare_kernel,
        [
            struct((HD, GROUP * rows), BF16),
            struct((HD, GROUP * rows), BF16),
            struct((pre, HD), F32),
            struct((rows, rows), F32),
        ],
        prefix_len.reshape(1, -1),
        slot,
        queries,
        out_grad,
    )
    dq, drk, drv, part = call(
        attention_kernel,
        [
            struct(queries.shape, BF16),
            struct(resp_keys.shape, BF16),
            struct(resp_values.shape, BF16),
            struct(both, BF16),
        ],
        owner,
        slot,
        query_t,
        grad_t,
        bias,
        rbias,
        own,
        other,
        resp_keys,
        resp_values,
        scratch=[
            pltpu.VMEM((total, HD), BF16),
            pltpu.VMEM((total, HD), BF16),
            pltpu.VMEM((HD, total), BF16),
            pltpu.VMEM((HD + 16, total), BF16),
            pltpu.VMEM((HD, GROUP * rows), BF16),
            pltpu.VMEM((HD, GROUP * rows), BF16),
            pltpu.VMEM((2, total, rows), F32),
            pltpu.VMEM((total, GROUP * rows), BF16),
            pltpu.VMEM((total, GROUP * rows), BF16),
            pltpu.VMEM((1, GROUP * rows), F32),
        ],
        flops=12 * GROUP * rows * total * HD,
    )
    (mine,) = call(side_sum_kernel, [struct((2, local, width), BF16)], exchange(part))
    got = lax.ppermute(mine, "dp", swap)
    dk, dv = call(
        final_kernel,
        [struct(prefix_keys.shape, BF16), struct(prefix_values.shape, BF16)],
        owner,
        mine,
        got,
    )
    return dq, drk, drv, dk, dv


def solution(mesh):
    placed = (
        P("dp", "head"),
        P("dp", "head"),
        P("dp", "head"),
        P("dp", "head"),
        P(("dp", "head"), None),
        P(("dp", "head"), None),
        P("dp"),
        P(),
        P(),
    )
    return jax.shard_map(
        on_device,
        mesh=mesh,
        in_specs=placed,
        out_specs=(
            P("dp", "head"),
            P("dp", "head"),
            P("dp", "head"),
            P(("dp", "head"), None),
            P(("dp", "head"), None),
        ),
        check_vma=False,
    )
```

time: 71.4 us -> 68.7 us (0.962)
  blocking collectives: 26.3 us -> 41.4 us
  starting transfers between devices: 19.2 us -> 9.09 us
  Pallas kernels: 18.3 us -> 12 us
  waiting for transfers between devices: 4.56 us -> 1.88 us
  local copies, waits for them, and re-layouts: 1.93 us -> 3.25 us
    all_to_all x2, blocking collectives: 26.3 us -> 41.4 us  [exchange(): lax.all_to_all(flat, ('dp', 'head'), 0, 0, axis_index_groups=groups, tile...]
    ppermute x2 -> x0, starting transfers between devices: 11.1 us -> none  [the longest x1 8.79 us: on_device(): got = lax.ppermute(sent, 'dp', swap)]
    pallas_call x7 -> x6, Pallas kernels: 18.3 us -> 12 us  [call(): pl.pallas_call(kernel, out_shape=tuple(outs), in_specs=specs or [VMEM for...]
    ppermute x2 -> x0, waiting for transfers between devices: 2.28 us -> none  [the longest x1 1.14 us: on_device(): got = lax.ppermute(sent, 'dp', swap)]
    unnamed x18, local copies, waits for them, and re-layouts: 1.93 us -> 3.25 us
    ppermute x1, starting transfers between devices: 4.08 us -> 5.1 us  [on_device(): other = lax.ppermute(own, 'dp', swap)]
    ppermute x1, waiting for transfers between devices: 1.14 us -> 0.37 us  [on_device(): other = lax.ppermute(own, 'dp', swap)]
  transfers between devices with their start and end apart: 4 -> 2, of which waited for: 4 -> 2; matrix products, arithmetic and copies ran while one was open for 0% -> 0% of each run, Pallas kernels for 0% -> 1%
where the time goes in v2:
time: 68.7 us; the launch traced here: 68.3 us
  blocking collectives  41.4 us (60%)
  Pallas kernels  12 us (17%)
  starting transfers between devices  9.09 us (13%)
  local copies, waits for them, and re-layouts  3.25 us (5%)
  waiting for transfers between devices  1.88 us (3%)
  between operations  0.73 us (1%)
    all_to_all x2, blocking collectives, exchange(): lax.all_to_all(flat, ('dp', 'head'), 0, 0, axis_index_groups=groups, tile...  41.4 us
    pallas_call x6, Pallas kernels, call(): pl.pallas_call(kernel, out_shape=tuple(outs), in_specs=specs or [VMEM for...  12 us
    ppermute x1, starting transfers between devices, on_device(): other = lax.ppermute(own, 'dp', swap)  5.1 us
    ppermute x1, starting transfers between devices, on_device(): got = lax.ppermute(mine, 'dp', swap)  3.99 us
    unnamed x18, local copies, waits for them, and re-layouts  3.25 us
    ppermute x1, waiting for transfers between devices, on_device(): got = lax.ppermute(mine, 'dp', swap)  1.51 us
  transfers between devices with their start and end apart: 2, of which 2 were waited for; matrix products, arithmetic and copies ran while one was open for 0% of the time, Pallas kernels for 1%

profile of v2, /device:TPU:1, one launch (start us, length us, event | category | flops | bytes accessed | tf_op | source)
XLA Modules:
  0.0 68.3 jit_solution(2424139935317767799)
XLA Ops:
  0.6 0.0 copy-start.2
  0.6 0.9 %copy-done.2 = bf16[128,1024]{1,0:T(8,128)(2,1)S(1)} copy-done((bf16[128,1024]{1,0:T(8,128)(2,1)S(1)}, bf16[128,1024]{1,0:T(8,128)(2,1)}, u32[]{:S(2)}) %copy-start.2) | copy-done | bytes 262168
  1.6 0.0 copy-start.3
  1.6 0.9 %copy-done.3 = bf16[128,1024]{1,0:T(8,128)(2,1)S(1)} copy-done((bf16[128,1024]{1,0:T(8,128)(2,1)S(1)}, bf16[128,1024]{1,0:T(8,128)(2,1)}, u32[]{:S(2)}) %copy-start.3) | copy-done | bytes 262168
  2.5 0.6 shard_map.129
  3.2 22.4 %all_to_all.10 = bf16[16,256,128]{2,1,0:T(8,128)(2,1)S(1)} all-to-all(bf16[16,256,128]{2,1,0:T(8,128)(2,1)S(1)} %bitcast.9), channel_id=1, replica_groups={{0,1,2,3,4,5,6,7,16,17,18,19,20,21,22,23},{8,9,10,11,12,13,14,15,24,25,..., dimensions={0} | all-to-all | bytes 2097152 | tf_op jit(solution)/shard_map/all_to_all | solution.py:248
  25.6 0.0 copy-start.4
  25.6 0.7 copy-done.4
  26.2 0.0 copy-start
  26.2 0.0 copy-start.1
  26.2 0.2 shard_map.130.own_ref
  26.4 5.1 %collective-permute-start = (bf16[8,2,128,128]{3,2,1,0:T(8,128)(2,1)S(1)}, bf16[8,2,128,128]{3,2,1,0:T(8,128)(2,1)S(1)}, u32[]{:S(2)}, u32[]{:S(2)}) collective-permute-start(bf16[8,2,128,128]{3,2,1,0:T(8,128)(2,1)S(1)} %shard_map.130.own_ref), channel_id=1, source_target_pairs={{0,8},{8,0},{16,24},{24,16},{32,40},{40,32},{48,56},{56,48},{64,72... | collective-permute-start | bytes 1572872 | tf_op jit(solution)/shard_map/ppermute | solution.py:263
  31.5 0.0 copy-start.5
  31.5 0.0 copy-start.6
  31.5 0.0 copy-done
  31.5 0.0 copy-done.1
  31.5 0.6 copy-done.5
  32.2 0.0 copy-done.6
  32.2 0.0 copy-start.7
  32.2 0.0 copy-start.8
  32.2 0.5 shard_map.128
  32.6 0.4 collective-permute-done.other_ref
  33.0 0.0 copy-done.7
  33.0 0.0 copy-done.8
  33.1 9.6 %shard_map.131 = (bf16[256,1024]{1,0:T(8,128)(2,1)}, bf16[256,128]{1,0:T(8,128)(2,1)}, bf16[256,128]{1,0:T(8,128)(2,1)}, bf16[16,2,128,128]{3,2,1,0:T(8,128)(2,1)S(1)}) custom-call(s32[1,16]{1,0:T(1,128)S(1)} %bitcast.12, s32[1,256]{1,0:T(1,128)S(1)} %bitcast.15, bf16[128,2048]{1,0:T(8,128)(2,1)S(1)} %get-tuple-element.15.query, ...), custom_call_target="tpu_custom_call" | custom-call | flops 4026531840 | bytes 4719680 | tf_op jit(solution)/shard_map/pallas_call | solution.py:46
  42.7 19.0 %all_to_all.11 = bf16[16,256,128]{2,1,0:T(8,128)(2,1)S(1)} all-to-all(bf16[16,256,128]{2,1,0:T(8,128)(2,1)S(1)} %bitcast.10), channel_id=1, replica_groups={{0,1,2,3,4,5,6,7,16,17,18,19,20,21,22,23},{8,9,10,11,12,13,14,15,24,25,..., dimensions={0} | all-to-all | bytes 2097152 | tf_op jit(solution)/shard_map/all_to_all | solution.py:248
  61.7 0.2 shard_map.132.mine_ref
  61.8 4.0 %collective-permute-start.1 = (bf16[2,128,1024]{2,1,0:T(8,128)(2,1)S(1)}, bf16[2,128,1024]{2,1,0:T(8,128)(2,1)S(1)}, u32[]{:S(2)}, u32[]{:S(2)}) collective-permute-start(bf16[2,128,1024]{2,1,0:T(8,128)(2,1)S(1)} %shard_map.132.mine_ref), channel_id=1, source_target_pairs={{0,8},{8,0},{16,24},{24,16},{32,40},{40,32},{48,56},{56,48},{64,72... | collective-permute-start | bytes 1572872 | tf_op jit(solution)/shard_map/ppermute | solution.py:310
  65.8 1.5 %collective-permute-done.1.got_ref = bf16[2,128,1024]{2,1,0:T(8,128)(2,1)S(1)} collective-permute-done((bf16[2,128,1024]{2,1,0:T(8,128)(2,1)S(1)}, bf16[2,128,1024]{2,1,0:T(8,128)(2,1)S(1)}, u32[]{:S(2)}, u32[]{:S(2)}) %collective-permute-start.1) | collective-permute-done | bytes 524320 | tf_op jit(solution)/shard_map/ppermute | solution.py:310
  67.4 0.9 %shard_map.133 = (bf16[128,1024]{1,0:T(8,128)(2,1)}, bf16[128,1024]{1,0:T(8,128)(2,1)}) custom-call(s32[1,16]{1,0:T(1,128)S(1)} %bitcast.13, bf16[2,128,1024]{2,1,0:T(8,128)(2,1)S(1)} %shard_map.132.mine_ref, bf16[2,128,1024]{2,1,0:T(8,128)(2,1)S(1)} %collective-permute-done.1.got_ref), custom_call_target="tpu_custom_call" | custom-call | bytes 1572928 | tf_op jit(solution)/shard_map/pallas_call | solution.py:46
Async XLA Ops:
  0.6 1.0 %copy-start.2 = (bf16[128,1024]{1,0:T(8,128)(2,1)S(1)}, bf16[128,1024]{1,0:T(8,128)(2,1)}, u32[]{:S(2)}) copy-start(bf16[128,1024]{1,0:T(8,128)(2,1)} %key_ref.1) | copy-start | bytes 786436
  1.6 0.9 %copy-start.3 = (bf16[128,1024]{1,0:T(8,128)(2,1)S(1)}, bf16[128,1024]{1,0:T(8,128)(2,1)}, u32[]{:S(2)}) copy-start(bf16[128,1024]{1,0:T(8,128)(2,1)} %value_ref.1) | copy-start | bytes 786436
  25.6 0.7 copy-start.4
  26.2 5.3 %copy-start = (bf16[256,1024]{1,0:T(8,128)(2,1)S(1)}, bf16[256,1024]{1,0:T(8,128)(2,1)}, u32[]{:S(2)}) copy-start(bf16[256,1024]{1,0:T(8,128)(2,1)} %query_ref.1) | copy-start | bytes 1572868
  26.2 5.3 %copy-start.1 = (bf16[256,1024]{1,0:T(8,128)(2,1)S(1)}, bf16[256,1024]{1,0:T(8,128)(2,1)}, u32[]{:S(2)}) copy-start(bf16[256,1024]{1,0:T(8,128)(2,1)} %grad_ref.1) | copy-start | bytes 1572868
  26.4 6.6 %collective-permute-start = (bf16[8,2,128,128]{3,2,1,0:T(8,128)(2,1)S(1)}, bf16[8,2,128,128]{3,2,1,0:T(8,128)(2,1)S(1)}, u32[]{:S(2)}, u32[]{:S(2)}) collective-permute-start(bf16[8,2,128,128]{3,2,1,0:T(8,128)(2,1)S(1)} %shard_map.130.own_ref), channel_id=1, source_target_pairs={{0,8},{8,0},{16,24},{24,16},{32,40},{40,32},{48,56},{56,48},{64,72... | collective-permute-start | bytes 1572872 | tf_op jit(solution)/shard_map/ppermute | solution.py:263
  31.5 0.7 copy-start.5
  31.5 0.7 copy-start.6
  32.2 0.8 %copy-start.7 = (bf16[256,128]{1,0:T(8,128)(2,1)S(1)}, bf16[256,128]{1,0:T(8,128)(2,1)}, u32[]{:S(2)}) copy-start(bf16[256,128]{1,0:T(8,128)(2,1)} %rkey_ref.1) | copy-start | bytes 196612
  32.2 0.9 %copy-start.8 = (bf16[256,128]{1,0:T(8,128)(2,1)S(1)}, bf16[256,128]{1,0:T(8,128)(2,1)}, u32[]{:S(2)}) copy-start(bf16[256,128]{1,0:T(8,128)(2,1)} %rvalue_ref.1) | copy-start | bytes 196612
  61.8 5.5 %collective-permute-start.1 = (bf16[2,128,1024]{2,1,0:T(8,128)(2,1)S(1)}, bf16[2,128,1024]{2,1,0:T(8,128)(2,1)S(1)}, u32[]{:S(2)}, u32[]{:S(2)}) collective-permute-start(bf16[2,128,1024]{2,1,0:T(8,128)(2,1)S(1)} %shard_map.132.mine_ref), channel_id=1, source_target_pairs={{0,8},{8,0},{16,24},{24,16},{32,40},{40,32},{48,56},{56,48},{64,72... | collective-permute-start | bytes 1572872 | tf_op jit(solution)/shard_map/ppermute | solution.py:310

commit v3 on v2

--- a/solution.py
+++ b/solution.py
@@ -19,7 +19,7 @@
 BF16 = jnp.bfloat16
 VMEM = pl.BlockSpec(memory_space=pltpu.VMEM)
 HBM = pl.BlockSpec(memory_space=pltpu.HBM)
-PARAMS = pltpu.CompilerParams(vmem_limit_bytes=48 * 1024 * 1024)
+MIB = 1024 * 1024
 
 
 def place():
@@ -27,12 +27,6 @@
     return index // BLOCK, (index % BLOCK) // 2, index % 2
 
 
-def owner_of(ref):
-    prompt, _, _ = place()
-    lane = lax.broadcasted_iota(jnp.int32, ref.shape, 1)
-    return jnp.sum(jnp.where(lane == prompt, ref[...], 0).astype(F32)).astype(jnp.int32)
-
-
 def nt(a, b):
     return lax.dot_general(a, b, (((1,), (1,)), ((), ())), preferred_element_type=F32)
 
@@ -41,7 +35,7 @@
     return jnp.dot(a, b, preferred_element_type=F32)
 
 
-def call(kernel, outs, *args, specs=None, scratch=(), flops=0):
+def call(kernel, outs, *args, specs=None, scratch=(), flops=0, vmem=32):
     size = sum(math.prod(a.shape) * a.dtype.itemsize for a in list(args) + list(outs))
     return pl.pallas_call(
         kernel,
@@ -49,7 +43,7 @@
         in_specs=specs or [VMEM for _ in args],
         out_specs=tuple(VMEM for _ in outs),
         scratch_shapes=list(scratch),
-        compiler_params=PARAMS,
+        compiler_params=pltpu.CompilerParams(vmem_limit_bytes=vmem * MIB),
         cost_estimate=pl.CostEstimate(flops=flops, bytes_accessed=size, transcendentals=0),
     )(*args)
 
@@ -58,8 +52,8 @@
     return jax.ShapeDtypeStruct(shape, dtype)
 
 
-def spread_kernel(key_ref, value_ref, out_ref, sems):
-    copies = []
+def spread_kernel(owner_ref, key_ref, value_ref, out_ref, flag_ref, place_ref, owners, sems):
+    copies = [pltpu.make_async_copy(owner_ref, owners, sems.at[0])]
     for n, ref in enumerate((key_ref, value_ref)):
         for h in range(KVH):
             for side in range(2):
@@ -68,12 +62,17 @@
                 copies.append(pltpu.make_async_copy(source, target, sems.at[len(copies)]))
     for copy in copies:
         copy.start()
-    for copy in copies:
+    copies[0].wait()
+    prompt, _, core = place()
+    owner = owners[0, prompt]
+    flag_ref[...] = jnp.full(flag_ref.shape, (owner % 2 == core).astype(jnp.int32))
+    place_ref[...] = jnp.full(place_ref.shape, owner)
+    for copy in copies[1:]:
         copy.wait()
 
 
-def side_kernel(owner_ref, got_ref, out_ref):
-    side = owner_of(owner_ref) // 2
+def side_kernel(place_ref, got_ref, out_ref):
+    side = place_ref[0, 0] // 2
 
     @pl.when(side == 0)
     def _():
@@ -105,7 +104,7 @@
 
 
 def attention_kernel(
-    owner_ref, slot_ref, query, grad, bias, rbias, own_ref, other_ref, rkey_ref, rvalue_ref,
+    place_ref, slot_ref, query, grad, bias, rbias, own_ref, other_ref, rkey_ref, rvalue_ref,
     dq_ref, drk_ref, drv_ref, part_ref,
     key, value, key_t, value_t, query_s, grad_s, score, weight, sgrad, factor,
 ):
@@ -124,7 +123,7 @@
             key[p * local : (p + 1) * local] = ref[p, 0]
             value[p * local : (p + 1) * local] = ref[p, 1]
 
-    own = owner_of(owner_ref) % 2 == core
+    own = place_ref[0, 0] % 2 == core
     pl.when(own)(lambda: take(own_ref))
     pl.when(jnp.logical_not(own))(lambda: take(other_ref))
     key[pre:] = rkey_ref[...]
@@ -192,27 +191,28 @@
                 for n, d in enumerate((dk, dv)):
                     block = d[:, p * local : (p + 1) * local].T.astype(BF16)
                     part_ref[k * (CHUNK // local) + p, n] = block
-                    part_ref[pieces + k * (CHUNK // local) + p, n] = block
     for g in range(GROUP):
         dq = nn(key_t[...], sgrad[:, at(g)]) * factor[:, at(g)]
         dq_ref[:, g * HD : (g + 1) * HD] = dq.T.astype(BF16)
 
 
-def side_sum_kernel(got_ref, out_ref):
-    for n in range(2):
-        for h in range(KVH):
-            block = got_ref[h, n].astype(F32) + got_ref[KVH + h, n].astype(F32)
-            out_ref[n, :, h * HD : (h + 1) * HD] = block.astype(BF16)
-
-
-def final_kernel(owner_ref, mine_ref, got_ref, dk_ref, dv_ref):
+def chip_sum_kernel(mine_ref, got_ref, out_ref):
+    for h in range(KVH):
+        block = (mine_ref[h].astype(F32) + got_ref[h].astype(F32)).astype(BF16)
+        out_ref[h] = block
+        out_ref[KVH + h] = block
+
+
+def final_kernel(place_ref, got_ref, dk_ref, dv_ref):
     _, side, core = place()
-    own = owner_of(owner_ref) == side * 2 + core
+    own = place_ref[0, 0] == side * 2 + core
 
     @pl.when(own)
     def _():
         for n, ref in enumerate((dk_ref, dv_ref)):
-            ref[...] = (mine_ref[n].astype(F32) + got_ref[n].astype(F32)).astype(BF16)
+            for h in range(KVH):
+                block = got_ref[h, n].astype(F32) + got_ref[KVH + h, n].astype(F32)
+                ref[:, h * HD : (h + 1) * HD] = block.astype(BF16)
 
     @pl.when(jnp.logical_not(own))
     def _():
@@ -248,18 +248,22 @@
         flat = lax.all_to_all(flat, ("dp", "head"), 0, 0, axis_index_groups=groups, tiled=True)
         return flat.reshape(block.shape)
 
-    owner = prefix_owner.reshape(1, -1)
     slot = resp_slot.reshape(1, rows)
+    piece = (heads, 2, local, HD)
     both = (2 * heads, 2, local, HD)
-    (spread,) = call(
+    spread, flag, owner = call(
         spread_kernel,
-        [struct(both, BF16)],
+        [struct(both, BF16), struct((1, 1), jnp.int32), struct((1, HD), jnp.int32)],
+        prefix_owner.reshape(1, -1),
         prefix_keys,
         prefix_values,
-        specs=[HBM, HBM],
-        scratch=[pltpu.SemaphoreType.DMA((4 * heads,))],
-    )
-    (own,) = call(side_kernel, [struct((heads, 2, local, HD), BF16)], owner, exchange(spread))
+        specs=[HBM, HBM, HBM],
+        scratch=[pltpu.SMEM((1, prefix_owner.shape[0]), jnp.int32), pltpu.SemaphoreType.DMA((4 * heads + 1,))],
+        vmem=60,
+    )
+    active = flag[0, 0] == 1
+    arrived = lax.cond(active, exchange, lambda block: block, spread)
+    (own,) = call(side_kernel, [struct(piece, BF16)], owner, arrived)
     other = lax.ppermute(own, "dp", swap)
     query_t, grad_t, bias, rbias = call(
         prepare_kernel,
@@ -280,7 +284,7 @@
             struct(queries.shape, BF16),
             struct(resp_keys.shape, BF16),
             struct(resp_values.shape, BF16),
-            struct(both, BF16),
+            struct(piece, BF16),
         ],
         owner,
         slot,
@@ -306,14 +310,14 @@
         ],
         flops=12 * GROUP * rows * total * HD,
     )
-    (mine,) = call(side_sum_kernel, [struct((2, local, width), BF16)], exchange(part))
-    got = lax.ppermute(mine, "dp", swap)
+    got = lax.ppermute(part, "dp", swap)
+    (spread,) = call(chip_sum_kernel, [struct(both, BF16)], part, got)
+    arrived = lax.cond(active, exchange, lambda block: block, spread)
     dk, dv = call(
         final_kernel,
         [struct(prefix_keys.shape, BF16), struct(prefix_values.shape, BF16)],
         owner,
-        mine,
-        got,
+        arrived,
     )
     return dq, drk, drv, dk, dv
 

time: 68.7 us -> 59.4 us (0.86)
  the two profiles are of different devices: /device:TPU:1 before, /device:TPU:128 now
where the time goes in v3:
time: 59.4 us; the launch traced here: 59 us
  blocking collectives  35.9 us (60%)
  Pallas kernels  13.7 us (23%)
  starting transfers between devices  4.12 us (7%)
  waiting for transfers between devices  2.45 us (4%)
  local copies, waits for them, and re-layouts  1.47 us (2%)
  between operations  1.36 us (2%)
    all_to_all x2, blocking collectives, exchange(): lax.all_to_all(flat, ('dp', 'head'), 0, 0, axis_index_groups=groups, tile...  35.9 us
    pallas_call x6, Pallas kernels, call(): pl.pallas_call(kernel, out_shape=tuple(outs), in_specs=specs or [VMEM for...  13.7 us
    ppermute x1, starting transfers between devices, on_device(): got = lax.ppermute(part, 'dp', swap)  2.07 us
    ppermute x1, starting transfers between devices, on_device(): other = lax.ppermute(own, 'dp', swap)  2.05 us
    ppermute x1, waiting for transfers between devices, on_device(): got = lax.ppermute(part, 'dp', swap)  1.71 us
    unnamed x14, local copies, waits for them, and re-layouts  1.32 us
  transfers between devices with their start and end apart: 2, of which 2 were waited for; matrix products, arithmetic and copies ran while one was open for 0% of the time, Pallas kernels for 1%

profile of v3, /device:TPU:128, one launch (start us, length us, event | category | flops | bytes accessed | tf_op | source)
XLA Modules:
  0.0 59.0 jit_solution(3517910365831729020)
XLA Ops:
  0.6 2.0 %shard_map.128 = (bf16[16,2,128,128]{3,2,1,0:T(8,128)(2,1)S(1)}, s32[1,1]{1,0:T(1,128)}, s32[1,128]{1,0:T(1,128)}) custom-call(s32[1,16]{1,0:T(1,128)} %bitcast.15, bf16[128,1024]{1,0:T(8,128)(2,1)} %key_ref.1, bf16[128,1024]{1,0:T(8,128)(2,1)} %value_ref.1), custom_call_target="tpu_custom_call" | custom-call | bytes 1573444 | tf_op jit(solution)/shard_map/pallas_call | solution.py:40
  3.3 19.8 %conditional.2 = (bf16[16,2,128,128]{3,2,1,0:T(8,128)(2,1)S(1)}) conditional(s32[]{:T(128)} %bitcast.7, bf16[16,2,128,128]{3,2,1,0:T(8,128)(2,1)S(1)} %get-tuple-element.34, bf16[16,2,128,128]{3,2,1,0:T(8,128)(2,1)S(1)} %get-tuple-element.34), branch_computations={%region_0.0_spmd, %region_1.0_spmd} | conditional | bytes 4194312 | solution.py:265
  3.3 0.1 copy.18
  3.4 19.7 %all_to_all.8 = bf16[16,256,128]{2,1,0:T(8,128)(2,1)S(1)} all-to-all(bf16[16,256,128]{2,1,0:T(8,128)(2,1)S(1)} %copy.18), channel_id=1, replica_groups={{0,1,2,3,4,5,6,7,16,17,18,19,20,21,22,23},{8,9,10,11,12,13,14,15,24,25,..., dimensions={0} | all-to-all | bytes 2097152 | tf_op jit(solution)/shard_map/cond/branch_1_fun/all_to_all | solution.py:248
  23.2 0.0 copy-start.2
  23.2 0.7 %copy-done.2 = s32[1,128]{1,0:T(1,128)S(1)} copy-done((s32[1,128]{1,0:T(1,128)S(1)}, s32[1,128]{1,0:T(1,128)}, u32[]{:S(2)}) %copy-start.2) | copy-done | bytes 536
  23.8 0.0 copy-start
  23.8 0.0 copy-start.1
  23.8 0.1 shard_map.130.own_ref
  23.9 2.1 %collective-permute-start = (bf16[8,2,128,128]{3,2,1,0:T(8,128)(2,1)S(1)}, bf16[8,2,128,128]{3,2,1,0:T(8,128)(2,1)S(1)}, u32[]{:S(2)}, u32[]{:S(2)}) collective-permute-start(bf16[8,2,128,128]{3,2,1,0:T(8,128)(2,1)S(1)} %shard_map.130.own_ref), channel_id=1, source_target_pairs={{0,8},{8,0},{16,24},{24,16},{32,40},{40,32},{48,56},{56,48},{64,72... | collective-permute-start | bytes 1572872 | tf_op jit(solution)/shard_map/ppermute | solution.py:267
  26.0 0.0 copy-start.3
  26.0 0.0 copy-start.4
  26.0 0.0 copy-done
  26.0 0.0 copy-done.1
  26.0 0.6 %copy-done.3 = s32[256]{0:T(256)S(1)} copy-done((s32[256]{0:T(256)S(1)}, s32[256]{0:T(256)}, u32[]{:S(2)}) %copy-start.3) | copy-done | bytes 1048
  26.7 0.0 copy-done.4
  26.7 0.0 copy-start.5
  26.7 0.0 copy-start.6
  26.7 0.4 shard_map.129
  27.1 0.7 %collective-permute-done.other_ref = bf16[8,2,128,128]{3,2,1,0:T(8,128)(2,1)S(1)} collective-permute-done((bf16[8,2,128,128]{3,2,1,0:T(8,128)(2,1)S(1)}, bf16[8,2,128,128]{3,2,1,0:T(8,128)(2,1)S(1)}, u32[]{:S(2)}, u32[]{:S(2)}) %collective-permute-start) | collective-permute-done | bytes 524320 | tf_op jit(solution)/shard_map/ppermute | solution.py:267
  27.9 0.0 copy-done.5
  27.9 0.0 copy-done.6
  27.9 10.0 %shard_map.131 = (bf16[256,1024]{1,0:T(8,128)(2,1)}, bf16[256,128]{1,0:T(8,128)(2,1)}, bf16[256,128]{1,0:T(8,128)(2,1)}, bf16[8,2,128,128]{3,2,1,0:T(8,128)(2,1)S(1)}) custom-call(s32[1,128]{1,0:T(1,128)S(1)} %copy-done.2, s32[1,256]{1,0:T(1,128)S(1)} %bitcast.9, bf16[128,2048]{1,0:T(8,128)(2,1)S(1)} %get-tuple-element.29.query, ...), custom_call_target="tpu_custom_call" | custom-call | flops 4026531840 | bytes 4195840 | tf_op jit(solution)/shard_map/pallas_call | solution.py:40
  37.9 2.1 %collective-permute-start.1 = (bf16[8,2,128,128]{3,2,1,0:T(8,128)(2,1)S(1)}, bf16[8,2,128,128]{3,2,1,0:T(8,128)(2,1)S(1)}, u32[]{:S(2)}, u32[]{:S(2)}) collective-permute-start(bf16[8,2,128,128]{3,2,1,0:T(8,128)(2,1)S(1)} %get-tuple-element.38.mine_ref), channel_id=1, source_target_pairs={{0,8},{8,0},{16,24},{24,16},{32,40},{40,32},{48,56},{56,48},{64,72... | collective-permute-start | bytes 1572872 | tf_op jit(solution)/shard_map/ppermute | solution.py:313
  39.9 1.7 %collective-permute-done.1.got_ref = bf16[8,2,128,128]{3,2,1,0:T(8,128)(2,1)S(1)} collective-permute-done((bf16[8,2,128,128]{3,2,1,0:T(8,128)(2,1)S(1)}, bf16[8,2,128,128]{3,2,1,0:T(8,128)(2,1)S(1)}, u32[]{:S(2)}, u32[]{:S(2)}) %collective-permute-start.1) | collective-permute-done | bytes 524320 | tf_op jit(solution)/shard_map/ppermute | solution.py:313
  41.7 0.1 shard_map.132
  41.8 16.3 %conditional.3 = (bf16[16,2,128,128]{3,2,1,0:T(8,128)(2,1)S(1)}) conditional(s32[]{:T(128)} %bitcast.7, bf16[16,2,128,128]{3,2,1,0:T(8,128)(2,1)S(1)} %shard_map.132, bf16[16,2,128,128]{3,2,1,0:T(8,128)(2,1)S(1)} %shard_map.132), branch_computations={%region_2.0_spmd, %region_3.0_spmd} | conditional | bytes 4194312 | solution.py:315
  41.8 0.1 copy.19
  41.9 16.2 %all_to_all.9 = bf16[16,256,128]{2,1,0:T(8,128)(2,1)S(1)} all-to-all(bf16[16,256,128]{2,1,0:T(8,128)(2,1)S(1)} %copy.19), channel_id=1, replica_groups={{0,1,2,3,4,5,6,7,16,17,18,19,20,21,22,23},{8,9,10,11,12,13,14,15,24,25,..., dimensions={0} | all-to-all | bytes 2097152 | tf_op jit(solution)/shard_map/cond/branch_1_fun/all_to_all | solution.py:248
  58.0 1.0 %shard_map.133 = (bf16[128,1024]{1,0:T(8,128)(2,1)}, bf16[128,1024]{1,0:T(8,128)(2,1)}) custom-call(s32[1,128]{1,0:T(1,128)S(1)} %copy-done.2, bf16[16,2,128,128]{3,2,1,0:T(8,128)(2,1)S(1)} %get-tuple-element.42.got_ref), custom_call_target="tpu_custom_call" | custom-call | bytes 1573376 | tf_op jit(solution)/shard_map/pallas_call | solution.py:40
Async XLA Ops:
  23.2 0.7 %copy-start.2 = (s32[1,128]{1,0:T(1,128)S(1)}, s32[1,128]{1,0:T(1,128)}, u32[]{:S(2)}) copy-start(s32[1,128]{1,0:T(1,128)} %get-tuple-element.28.place_ref) | copy-start | bytes 1540
  23.8 2.2 %copy-start = (bf16[256,1024]{1,0:T(8,128)(2,1)S(1)}, bf16[256,1024]{1,0:T(8,128)(2,1)}, u32[]{:S(2)}) copy-start(bf16[256,1024]{1,0:T(8,128)(2,1)} %query_ref.1) | copy-start | bytes 1572868
  23.8 2.2 %copy-start.1 = (bf16[256,1024]{1,0:T(8,128)(2,1)S(1)}, bf16[256,1024]{1,0:T(8,128)(2,1)}, u32[]{:S(2)}) copy-start(bf16[256,1024]{1,0:T(8,128)(2,1)} %grad_ref.1) | copy-start | bytes 1572868
  23.9 3.9 %collective-permute-start = (bf16[8,2,128,128]{3,2,1,0:T(8,128)(2,1)S(1)}, bf16[8,2,128,128]{3,2,1,0:T(8,128)(2,1)S(1)}, u32[]{:S(2)}, u32[]{:S(2)}) collective-permute-start(bf16[8,2,128,128]{3,2,1,0:T(8,128)(2,1)S(1)} %shard_map.130.own_ref), channel_id=1, source_target_pairs={{0,8},{8,0},{16,24},{24,16},{32,40},{40,32},{48,56},{56,48},{64,72... | collective-permute-start | bytes 1572872 | tf_op jit(solution)/shard_map/ppermute | solution.py:267
  26.0 0.7 %copy-start.3 = (s32[256]{0:T(256)S(1)}, s32[256]{0:T(256)}, u32[]{:S(2)}) copy-start(s32[256]{0:T(256)} %param.19) | copy-start | bytes 3076
  26.0 0.7 %copy-start.4 = (s32[16]{0:T(128)S(1)}, s32[16]{0:T(128)}, u32[]{:S(2)}) copy-start(s32[16]{0:T(128)} %param.20) | copy-start | bytes 196
  26.7 1.2 %copy-start.5 = (bf16[256,128]{1,0:T(8,128)(2,1)S(1)}, bf16[256,128]{1,0:T(8,128)(2,1)}, u32[]{:S(2)}) copy-start(bf16[256,128]{1,0:T(8,128)(2,1)} %rkey_ref.1) | copy-start | bytes 196612
  26.7 1.2 %copy-start.6 = (bf16[256,128]{1,0:T(8,128)(2,1)S(1)}, bf16[256,128]{1,0:T(8,128)(2,1)}, u32[]{:S(2)}) copy-start(bf16[256,128]{1,0:T(8,128)(2,1)} %rvalue_ref.1) | copy-start | bytes 196612
  37.9 3.8 %collective-permute-start.1 = (bf16[8,2,128,128]{3,2,1,0:T(8,128)(2,1)S(1)}, bf16[8,2,128,128]{3,2,1,0:T(8,128)(2,1)S(1)}, u32[]{:S(2)}, u32[]{:S(2)}) collective-permute-start(bf16[8,2,128,128]{3,2,1,0:T(8,128)(2,1)S(1)} %get-tuple-element.38.mine_ref), channel_id=1, source_target_pairs={{0,8},{8,0},{16,24},{24,16},{32,40},{40,32},{48,56},{56,48},{64,72... | collective-permute-start | bytes 1572872 | tf_op jit(solution)/shard_map/ppermute | solution.py:313

commit v4 on v3

--- a/solution.py
+++ b/solution.py
@@ -20,6 +20,7 @@
 VMEM = pl.BlockSpec(memory_space=pltpu.VMEM)
 HBM = pl.BlockSpec(memory_space=pltpu.HBM)
 MIB = 1024 * 1024
+PARTS = 4
 
 
 def place():
@@ -52,35 +53,40 @@
     return jax.ShapeDtypeStruct(shape, dtype)
 
 
-def spread_kernel(owner_ref, key_ref, value_ref, out_ref, flag_ref, place_ref, owners, sems):
-    copies = [pltpu.make_async_copy(owner_ref, owners, sems.at[0])]
+def spread_kernel(owner_ref, key_ref, value_ref, out_ref, flag_ref, place_ref, slots, owners, sems):
+    first = pltpu.make_async_copy(owner_ref, owners, sems.at[0])
+    first.start()
+    copies = []
     for n, ref in enumerate((key_ref, value_ref)):
-        for h in range(KVH):
-            for side in range(2):
-                source = ref.at[:, h * HD : (h + 1) * HD]
-                target = out_ref.at[side * KVH + h, n]
-                copies.append(pltpu.make_async_copy(source, target, sems.at[len(copies)]))
+        for part in range(PARTS):
+            rows = slice(part * HD // PARTS, (part + 1) * HD // PARTS)
+            copies.append(pltpu.make_async_copy(ref.at[rows, :], slots.at[n, rows, :], sems.at[len(copies) + 1]))
     for copy in copies:
         copy.start()
-    copies[0].wait()
-    prompt, _, core = place()
+    first.wait()
+    prompt, side, core = place()
     owner = owners[0, prompt]
     flag_ref[...] = jnp.full(flag_ref.shape, (owner % 2 == core).astype(jnp.int32))
     place_ref[...] = jnp.full(place_ref.shape, owner)
-    for copy in copies[1:]:
-        copy.wait()
-
-
-def side_kernel(place_ref, got_ref, out_ref):
-    side = place_ref[0, 0] // 2
-
-    @pl.when(side == 0)
+
+    @pl.when(owner // 2 != side)
     def _():
-        out_ref[...] = got_ref[:KVH]
-
-    @pl.when(side == 1)
-    def _():
-        out_ref[...] = got_ref[KVH:]
+        out_ref[...] = jnp.zeros_like(out_ref)
+
+    for n in range(2):
+        for copy in copies[n * PARTS : (n + 1) * PARTS]:
+            copy.wait()
+
+        @pl.when(owner // 2 == side)
+        def _():
+            for h in range(KVH):
+                block = slots[n, :, h * HD : (h + 1) * HD]
+                out_ref[h, n] = block
+                out_ref[KVH + h, n] = block
+
+
+def side_kernel(got_ref, out_ref):
+    out_ref[...] = got_ref[:KVH] + got_ref[KVH:]
 
 
 def prepare_kernel(len_ref, slot_ref, query_ref, grad_ref, query_t, grad_t, bias, rbias):
@@ -104,11 +110,10 @@
 
 
 def attention_kernel(
-    place_ref, slot_ref, query, grad, bias, rbias, own_ref, other_ref, rkey_ref, rvalue_ref,
-    dq_ref, drk_ref, drv_ref, part_ref,
-    key, value, key_t, value_t, query_s, grad_s, score, weight, sgrad, factor,
+    slot_ref, query, grad, bias, rbias, own_ref, other_ref, rkey_ref, rvalue_ref,
+    part_ref, weight, sgrad, query_s, grad_s, key_t, factor,
+    key, value, value_t, score,
 ):
-    _, _, core = place()
     rows = slot_ref.shape[1]
     pieces, _, local, _ = own_ref.shape
     pre = pieces * local
@@ -118,14 +123,9 @@
     log_scale = scale * math.log2(math.e)
     live = jnp.where(slot_ref[...] < BLOCK, 1.0, 0.0).astype(F32)
 
-    def take(ref):
-        for p in range(pieces):
-            key[p * local : (p + 1) * local] = ref[p, 0]
-            value[p * local : (p + 1) * local] = ref[p, 1]
-
-    own = place_ref[0, 0] % 2 == core
-    pl.when(own)(lambda: take(own_ref))
-    pl.when(jnp.logical_not(own))(lambda: take(other_ref))
+    for p in range(pieces):
+        key[p * local : (p + 1) * local] = own_ref[p, 0] + other_ref[p, 0]
+        value[p * local : (p + 1) * local] = own_ref[p, 1] + other_ref[p, 1]
     key[pre:] = rkey_ref[...]
     value[pre:] = rvalue_ref[...]
 
@@ -180,19 +180,22 @@
         if 1 <= t <= GROUP:
             attend(t - 1)
 
-    for k in range(chunks):
+    for k in range(pre // CHUNK):
         dk = nt(query_s[...], sgrad[cut(k)])
         dv = nt(grad_s[...], weight[cut(k)])
-        if k == chunks - 1:
-            drk_ref[...] = dk.T.astype(BF16)
-            drv_ref[...] = dv.T.astype(BF16)
-        else:
-            for p in range(CHUNK // local):
-                for n, d in enumerate((dk, dv)):
-                    block = d[:, p * local : (p + 1) * local].T.astype(BF16)
-                    part_ref[k * (CHUNK // local) + p, n] = block
+        for p in range(CHUNK // local):
+            for n, d in enumerate((dk, dv)):
+                part_ref[k * (CHUNK // local) + p, n] = d[:, p * local : (p + 1) * local].T.astype(BF16)
+
+
+def response_kernel(weight, sgrad, query_s, grad_s, key_t, factor, dq_ref, drk_ref, drv_ref):
+    rows = drk_ref.shape[0]
+    pre = weight.shape[0] - rows
+    drk_ref[...] = nt(query_s[...], sgrad[pre:]).T.astype(BF16)
+    drv_ref[...] = nt(grad_s[...], weight[pre:]).T.astype(BF16)
     for g in range(GROUP):
-        dq = nn(key_t[...], sgrad[:, at(g)]) * factor[:, at(g)]
+        at = slice(g * rows, (g + 1) * rows)
+        dq = nn(key_t[...], sgrad[:, at]) * factor[:, at]
         dq_ref[:, g * HD : (g + 1) * HD] = dq.T.astype(BF16)
 
 
@@ -258,12 +261,16 @@
         prefix_keys,
         prefix_values,
         specs=[HBM, HBM, HBM],
-        scratch=[pltpu.SMEM((1, prefix_owner.shape[0]), jnp.int32), pltpu.SemaphoreType.DMA((4 * heads + 1,))],
+        scratch=[
+            pltpu.VMEM((2, local, width), BF16),
+            pltpu.SMEM((1, prefix_owner.shape[0]), jnp.int32),
+            pltpu.SemaphoreType.DMA((2 * PARTS + 1,)),
+        ],
         vmem=60,
     )
     active = flag[0, 0] == 1
-    arrived = lax.cond(active, exchange, lambda block: block, spread)
-    (own,) = call(side_kernel, [struct(piece, BF16)], owner, arrived)
+    arrived = lax.cond(active, exchange, jnp.zeros_like, spread)
+    (own,) = call(side_kernel, [struct(piece, BF16)], arrived)
     other = lax.ppermute(own, "dp", swap)
     query_t, grad_t, bias, rbias = call(
         prepare_kernel,
@@ -278,15 +285,17 @@
         queries,
         out_grad,
     )
-    dq, drk, drv, part = call(
+    part, *saved = call(
         attention_kernel,
         [
-            struct(queries.shape, BF16),
-            struct(resp_keys.shape, BF16),
-            struct(resp_values.shape, BF16),
             struct(piece, BF16),
+            struct((total, GROUP * rows), BF16),
+            struct((total, GROUP * rows), BF16),
+            struct((HD, GROUP * rows), BF16),
+            struct((HD, GROUP * rows), BF16),
+            struct((HD, total), BF16),
+            struct((1, GROUP * rows), F32),
         ],
-        owner,
         slot,
         query_t,
         grad_t,
@@ -299,18 +308,18 @@
         scratch=[
             pltpu.VMEM((total, HD), BF16),
             pltpu.VMEM((total, HD), BF16),
-            pltpu.VMEM((HD, total), BF16),
             pltpu.VMEM((HD + 16, total), BF16),
-            pltpu.VMEM((HD, GROUP * rows), BF16),
-            pltpu.VMEM((HD, GROUP * rows), BF16),
             pltpu.VMEM((2, total, rows), F32),
-            pltpu.VMEM((total, GROUP * rows), BF16),
-            pltpu.VMEM((total, GROUP * rows), BF16),
-            pltpu.VMEM((1, GROUP * rows), F32),
         ],
-        flops=12 * GROUP * rows * total * HD,
+        flops=10 * GROUP * rows * total * HD,
     )
     got = lax.ppermute(part, "dp", swap)
+    dq, drk, drv = call(
+        response_kernel,
+        [struct(queries.shape, BF16), struct(resp_keys.shape, BF16), struct(resp_values.shape, BF16)],
+        *saved,
+        flops=2 * GROUP * rows * total * HD,
+    )
     (spread,) = call(chip_sum_kernel, [struct(both, BF16)], part, got)
     arrived = lax.cond(active, exchange, lambda block: block, spread)
     dk, dv = call(

time: 59.4 us -> 57.9 us (0.975)
  the two profiles are of different devices: /device:TPU:128 before, /device:TPU:8 now
where the time goes in v4:
time: 57.9 us; the launch traced here: 57.7 us
  blocking collectives  36 us (62%)
  Pallas kernels  14.7 us (25%)
  starting transfers between devices  3.97 us (7%)
  between operations  1.41 us (2%)
  waiting for transfers between devices  1.38 us (2%)
    all_to_all x2, blocking collectives, exchange(): lax.all_to_all(flat, ('dp', 'head'), 0, 0, axis_index_groups=groups, tile...  36 us
    pallas_call x7, Pallas kernels, call(): pl.pallas_call(kernel, out_shape=tuple(outs), in_specs=specs or [VMEM for...  14.7 us
    ppermute x1, starting transfers between devices, on_device(): got = lax.ppermute(part, 'dp', swap)  2.05 us
    ppermute x1, starting transfers between devices, on_device(): other = lax.ppermute(own, 'dp', swap)  1.92 us
    ppermute x1, waiting for transfers between devices, on_device(): other = lax.ppermute(own, 'dp', swap)  1.38 us
  transfers between devices with their start and end apart: 2, of which 1 were waited for; matrix products, arithmetic and copies ran while one was open for 0% of the time, Pallas kernels for 5%

profile of v4, /device:TPU:8, one launch (start us, length us, event | category | flops | bytes accessed | tf_op | source)
XLA Modules:
  0.0 57.7 jit_solution(13447738546480001085)
XLA Ops:
  0.6 0.0 copy-start.3
  0.6 0.0 copy-start.2
  0.7 0.0 copy-start.1
  0.7 0.0 copy-start
  0.7 0.0 copy-start.6
  0.7 0.0 copy-start.5
  0.7 1.8 %shard_map.129 = (bf16[16,2,128,128]{3,2,1,0:T(8,128)(2,1)S(1)}, s32[1,1]{1,0:T(1,128)}, s32[1,128]{1,0:T(1,128)}) custom-call(s32[1,16]{1,0:T(1,128)} %bitcast.15, bf16[128,1024]{1,0:T(8,128)(2,1)} %key_ref.1, bf16[128,1024]{1,0:T(8,128)(2,1)} %value_ref.1), custom_call_target="tpu_custom_call" | custom-call | bytes 1573444 | tf_op jit(solution)/shard_map/pallas_call | solution.py:41
  3.2 19.9 %conditional.2 = (bf16[16,2,128,128]{3,2,1,0:T(8,128)(2,1)S(1)}) conditional(s32[]{:T(128)} %bitcast.7, () %tuple.20, bf16[16,2,128,128]{3,2,1,0:T(8,128)(2,1)S(1)} %get-tuple-element.38), branch_computations={%region_0.0_spmd, %region_1.0_spmd} | conditional | bytes 2097160 | solution.py:272
  3.2 19.9 %all_to_all.8 = bf16[16,256,128]{2,1,0:T(8,128)(2,1)S(1)} all-to-all(bf16[16,256,128]{2,1,0:T(8,128)(2,1)S(1)} %bitcast.14), channel_id=1, replica_groups={{0,1,2,3,4,5,6,7,16,17,18,19,20,21,22,23},{8,9,10,11,12,13,14,15,24,25,..., dimensions={0} | all-to-all | bytes 2097152 | tf_op jit(solution)/shard_map/cond/branch_1_fun/all_to_all | solution.py:251
  23.1 0.1 shard_map.130.own_ref
  23.2 1.9 %collective-permute-start = (bf16[8,2,128,128]{3,2,1,0:T(8,128)(2,1)S(1)}, bf16[8,2,128,128]{3,2,1,0:T(8,128)(2,1)S(1)}, u32[]{:S(2)}, u32[]{:S(2)}) collective-permute-start(bf16[8,2,128,128]{3,2,1,0:T(8,128)(2,1)S(1)} %shard_map.130.own_ref), channel_id=1, source_target_pairs={{0,8},{8,0},{16,24},{24,16},{32,40},{40,32},{48,56},{56,48},{64,72... | collective-permute-start | bytes 1572872 | tf_op jit(solution)/shard_map/ppermute | solution.py:274
  25.1 0.0 copy-done.3
  25.1 0.0 copy-done.2
  25.1 0.0 copy-done.1
  25.2 0.0 copy-done
  25.2 0.5 shard_map.128
  25.6 1.4 %collective-permute-done.other_ref = bf16[8,2,128,128]{3,2,1,0:T(8,128)(2,1)S(1)} collective-permute-done((bf16[8,2,128,128]{3,2,1,0:T(8,128)(2,1)S(1)}, bf16[8,2,128,128]{3,2,1,0:T(8,128)(2,1)S(1)}, u32[]{:S(2)}, u32[]{:S(2)}) %collective-permute-start) | collective-permute-done | bytes 524320 | tf_op jit(solution)/shard_map/ppermute | solution.py:274
  27.0 0.0 copy-done.6
  27.0 0.0 copy-done.5
  27.0 8.8 %shard_map.131 = (bf16[8,2,128,128]{3,2,1,0:T(8,128)(2,1)S(1)}, bf16[1280,2048]{1,0:T(8,128)(2,1)S(1)}, bf16[1280,2048]{1,0:T(8,128)(2,1)S(1)}, bf16[128,2048]{1...) custom-call(s32[1,256]{1,0:T(1,128)S(1)} %bitcast.9, ...), custom_call_target="tpu_custom_call" | custom-call | flops 3355443200 | bytes 15410176 | tf_op jit(solution)/shard_map/pallas_call | solution.py:41
  35.9 2.0 %collective-permute-start.1 = (bf16[8,2,128,128]{3,2,1,0:T(8,128)(2,1)S(1)}, bf16[8,2,128,128]{3,2,1,0:T(8,128)(2,1)S(1)}, u32[]{:S(2)}, u32[]{:S(2)}) collective-permute-start(bf16[8,2,128,128]{3,2,1,0:T(8,128)(2,1)S(1)} %get-tuple-element.49.mine_ref), channel_id=1, source_target_pairs={{0,8},{8,0},{16,24},{24,16},{32,40},{40,32},{48,56},{56,48},{64,72... | collective-permute-start | bytes 1572872 | tf_op jit(solution)/shard_map/ppermute | solution.py:316
  37.9 2.4 %shard_map.132 = (bf16[256,1024]{1,0:T(8,128)(2,1)}, bf16[256,128]{1,0:T(8,128)(2,1)}, bf16[256,128]{1,0:T(8,128)(2,1)}) custom-call(bf16[1280,2048]{1,0:T(8,128)(2,1)S(1)} %get-tuple-element.39.weight, bf16[1280,2048]{1,0:T(8,128)(2,1)S(1)} %get-tuple-element.40.sgrad, bf16[128,2048]{1,0:T(8,128)(2,1)S(1)} %get-tuple-element.41.query_s, ...), custom_call_target="tpu_custom_call" | custom-call | flops 671088640 | bytes 12525568 | tf_op jit(solution)/shard_map/pallas_call | solution.py:41
  40.3 0.0 copy-start.4
  40.3 0.0 collective-permute-done.1.got_ref
  40.3 0.1 shard_map.133
  40.4 16.3 %conditional.3 = (bf16[16,2,128,128]{3,2,1,0:T(8,128)(2,1)S(1)}) conditional(s32[]{:T(128)} %bitcast.7, bf16[16,2,128,128]{3,2,1,0:T(8,128)(2,1)S(1)} %shard_map.133, bf16[16,2,128,128]{3,2,1,0:T(8,128)(2,1)S(1)} %shard_map.133), branch_computations={%region_2.0_spmd, %region_3.0_spmd} | conditional | bytes 4194312 | solution.py:324
  40.4 0.1 copy.18
  40.5 16.2 %all_to_all.9 = bf16[16,256,128]{2,1,0:T(8,128)(2,1)S(1)} all-to-all(bf16[16,256,128]{2,1,0:T(8,128)(2,1)S(1)} %copy.18), channel_id=1, replica_groups={{0,1,2,3,4,5,6,7,16,17,18,19,20,21,22,23},{8,9,10,11,12,13,14,15,24,25,..., dimensions={0} | all-to-all | bytes 2097152 | tf_op jit(solution)/shard_map/cond/branch_1_fun/all_to_all | solution.py:251
  56.7 0.0 copy-done.4
  56.7 1.0 %shard_map.134 = (bf16[128,1024]{1,0:T(8,128)(2,1)}, bf16[128,1024]{1,0:T(8,128)(2,1)}) custom-call(s32[1,128]{1,0:T(1,128)S(1)} %copy-done.4, bf16[16,2,128,128]{3,2,1,0:T(8,128)(2,1)S(1)} %get-tuple-element.53.got_ref), custom_call_target="tpu_custom_call" | custom-call | bytes 1573376 | tf_op jit(solution)/shard_map/pallas_call | solution.py:41
Async XLA Ops:
  0.6 24.5 %copy-start.3 = (s32[16]{0:T(128)S(1)}, s32[16]{0:T(128)}, u32[]{:S(2)}) copy-start(s32[16]{0:T(128)} %param.20) | copy-start | bytes 196
  0.6 24.5 %copy-start.2 = (s32[256]{0:T(256)S(1)}, s32[256]{0:T(256)}, u32[]{:S(2)}) copy-start(s32[256]{0:T(256)} %param.19) | copy-start | bytes 3076
  0.7 24.5 %copy-start.1 = (bf16[256,1024]{1,0:T(8,128)(2,1)S(1)}, bf16[256,1024]{1,0:T(8,128)(2,1)}, u32[]{:S(2)}) copy-start(bf16[256,1024]{1,0:T(8,128)(2,1)} %grad_ref.1) | copy-start | bytes 1572868
  0.7 24.5 %copy-start = (bf16[256,1024]{1,0:T(8,128)(2,1)S(1)}, bf16[256,1024]{1,0:T(8,128)(2,1)}, u32[]{:S(2)}) copy-start(bf16[256,1024]{1,0:T(8,128)(2,1)} %query_ref.1) | copy-start | bytes 1572868
  0.7 26.3 %copy-start.6 = (bf16[256,128]{1,0:T(8,128)(2,1)S(1)}, bf16[256,128]{1,0:T(8,128)(2,1)}, u32[]{:S(2)}) copy-start(bf16[256,128]{1,0:T(8,128)(2,1)} %rvalue_ref.1) | copy-start | bytes 196612
  0.7 26.3 %copy-start.5 = (bf16[256,128]{1,0:T(8,128)(2,1)S(1)}, bf16[256,128]{1,0:T(8,128)(2,1)}, u32[]{:S(2)}) copy-start(bf16[256,128]{1,0:T(8,128)(2,1)} %rkey_ref.1) | copy-start | bytes 196612
  23.2 3.8 %collective-permute-start = (bf16[8,2,128,128]{3,2,1,0:T(8,128)(2,1)S(1)}, bf16[8,2,128,128]{3,2,1,0:T(8,128)(2,1)S(1)}, u32[]{:S(2)}, u32[]{:S(2)}) collective-permute-start(bf16[8,2,128,128]{3,2,1,0:T(8,128)(2,1)S(1)} %shard_map.130.own_ref), channel_id=1, source_target_pairs={{0,8},{8,0},{16,24},{24,16},{32,40},{40,32},{48,56},{56,48},{64,72... | collective-permute-start | bytes 1572872 | tf_op jit(solution)/shard_map/ppermute | solution.py:274
  35.9 4.4 %collective-permute-start.1 = (bf16[8,2,128,128]{3,2,1,0:T(8,128)(2,1)S(1)}, bf16[8,2,128,128]{3,2,1,0:T(8,128)(2,1)S(1)}, u32[]{:S(2)}, u32[]{:S(2)}) collective-permute-start(bf16[8,2,128,128]{3,2,1,0:T(8,128)(2,1)S(1)} %get-tuple-element.49.mine_ref), channel_id=1, source_target_pairs={{0,8},{8,0},{16,24},{24,16},{32,40},{40,32},{48,56},{56,48},{64,72... | collective-permute-start | bytes 1572872 | tf_op jit(solution)/shard_map/ppermute | solution.py:316
  40.3 16.4 %copy-start.4 = (s32[1,128]{1,0:T(1,128)S(1)}, s32[1,128]{1,0:T(1,128)}, u32[]{:S(2)}) copy-start(s32[1,128]{1,0:T(1,128)} %get-tuple-element.48.place_ref) | copy-start | bytes 1540

commit v5 on v4

--- a/solution.py
+++ b/solution.py
@@ -28,6 +28,18 @@
     return index // BLOCK, (index % BLOCK) // 2, index % 2
 
 
+def members(heads):
+    low, ring = 2, heads // 2
+    order = []
+    for y in range(ring):
+        line = [(x // low, x % low, y) for x in range(2 * low)]
+        order += line if y % 2 == 0 else line[::-1]
+    return [(side, x * ring + y) for side, x, y in order]
+
+
+PLACE = {member: n for n, member in enumerate(members(KVH))}
+
+
 def nt(a, b):
     return lax.dot_general(a, b, (((1,), (1,)), ((), ())), preferred_element_type=F32)
 
@@ -36,13 +48,13 @@
     return jnp.dot(a, b, preferred_element_type=F32)
 
 
-def call(kernel, outs, *args, specs=None, scratch=(), flops=0, vmem=32):
+def call(kernel, outs, *args, specs=None, out_specs=None, scratch=(), flops=0, vmem=32):
     size = sum(math.prod(a.shape) * a.dtype.itemsize for a in list(args) + list(outs))
     return pl.pallas_call(
         kernel,
         out_shape=tuple(outs),
         in_specs=specs or [VMEM for _ in args],
-        out_specs=tuple(VMEM for _ in outs),
+        out_specs=tuple(out_specs or [VMEM for _ in outs]),
         scratch_shapes=list(scratch),
         compiler_params=pltpu.CompilerParams(vmem_limit_bytes=vmem * MIB),
         cost_estimate=pl.CostEstimate(flops=flops, bytes_accessed=size, transcendentals=0),
@@ -53,7 +65,7 @@
     return jax.ShapeDtypeStruct(shape, dtype)
 
 
-def spread_kernel(owner_ref, key_ref, value_ref, out_ref, flag_ref, place_ref, slots, owners, sems):
+def spread_kernel(owner_ref, key_ref, value_ref, out_ref, flag_ref, place_ref, flag, spot, slots, owners, sems):
     first = pltpu.make_async_copy(owner_ref, owners, sems.at[0])
     first.start()
     copies = []
@@ -66,8 +78,14 @@
     first.wait()
     prompt, side, core = place()
     owner = owners[0, prompt]
-    flag_ref[...] = jnp.full(flag_ref.shape, (owner % 2 == core).astype(jnp.int32))
-    place_ref[...] = jnp.full(place_ref.shape, owner)
+    flag[...] = jnp.full(flag.shape, (owner % 2 == core).astype(jnp.int32))
+    spot[...] = jnp.full(spot.shape, owner)
+    small = [
+        pltpu.make_async_copy(flag, flag_ref, sems.at[2 * PARTS + 1]),
+        pltpu.make_async_copy(spot, place_ref, sems.at[2 * PARTS + 2]),
+    ]
+    for copy in small:
+        copy.start()
 
     @pl.when(owner // 2 != side)
     def _():
@@ -81,15 +99,21 @@
         def _():
             for h in range(KVH):
                 block = slots[n, :, h * HD : (h + 1) * HD]
-                out_ref[h, n] = block
-                out_ref[KVH + h, n] = block
+                out_ref[PLACE[0, h], n] = block
+                out_ref[PLACE[1, h], n] = block
+
+    for copy in small:
+        copy.wait()
 
 
 def side_kernel(got_ref, out_ref):
-    out_ref[...] = got_ref[:KVH] + got_ref[KVH:]
-
-
-def prepare_kernel(len_ref, slot_ref, query_ref, grad_ref, query_t, grad_t, bias, rbias):
+    for h in range(KVH):
+        out_ref[h] = got_ref[PLACE[0, h]] + got_ref[PLACE[1, h]]
+
+
+def prepare_kernel(
+    len_ref, slot_ref, query_ref, grad_ref, rkey_ref, rvalue_ref, query_t, grad_t, bias, rscore, rdprod
+):
     rows = query_ref.shape[0]
     for g in range(GROUP):
         at = slice(g * rows, (g + 1) * rows)
@@ -106,11 +130,15 @@
     at_key = lax.broadcasted_iota(jnp.int32, (rows, rows), 0)
     at_row = lax.broadcasted_iota(jnp.int32, (rows, rows), 1)
     seen = jnp.logical_and(slot_row == slot_col, at_key <= at_row)
-    rbias[...] = jnp.where(seen, 0.0, MASKED).astype(F32)
+    rbias = jnp.where(seen, 0.0, MASKED).astype(F32)
+    for g in range(GROUP):
+        at = slice(g * rows, (g + 1) * rows)
+        rscore[:, at] = nn(rkey_ref[...], query_t[:, at]) + rbias
+        rdprod[:, at] = nn(rvalue_ref[...], grad_t[:, at])
 
 
 def attention_kernel(
-    slot_ref, query, grad, bias, rbias, own_ref, other_ref, rkey_ref, rvalue_ref,
+    slot_ref, query, grad, bias, rscore, rdprod, own_ref, other_ref, rkey_ref, rvalue_ref,
     part_ref, weight, sgrad, query_s, grad_s, key_t, factor,
     key, value, value_t, score,
 ):
@@ -143,18 +171,18 @@
     tops, dots = {}, {}
 
     def scores(g, k):
-        s = nn(key[cut(k)], query[:, at(g)])
         if k == chunks - 1:
-            s = s + rbias[...]
+            s = rscore[:, at(g)]
         else:
             b = bias[cut(k)]
-            s = s + jnp.concatenate([b] * (rows // HD), axis=1)
-        score[g % 2, cut(k)] = s
+            s = nn(key[cut(k)], query[:, at(g)]) + jnp.concatenate([b] * (rows // HD), axis=1)
+            score[g % 2, cut(k)] = s
         top = jnp.max(s, axis=0, keepdims=True)
         tops[g] = top if k == 0 else jnp.maximum(tops[g], top)
 
     def weights(g, k):
-        weight[cut(k), at(g)] = jnp.exp2((score[g % 2, cut(k)] - tops[g]) * log_scale).astype(BF16)
+        s = rscore[:, at(g)] if k == chunks - 1 else score[g % 2, cut(k)]
+        weight[cut(k), at(g)] = jnp.exp2((s - tops[g]) * log_scale).astype(BF16)
 
     def attend(g):
         both = nn(value_t[...], weight[:, at(g)])
@@ -166,7 +194,7 @@
         grad_s[:, at(g)] = (grad[:, at(g)].astype(F32) * inverse).astype(BF16)
 
     def score_grads(g, k):
-        d = nn(value[cut(k)], grad[:, at(g)])
+        d = rdprod[:, at(g)] if k == chunks - 1 else nn(value[cut(k)], grad[:, at(g)])
         sgrad[cut(k), at(g)] = weight[cut(k), at(g)] * (d - dots[g]).astype(BF16)
 
     for t in range(GROUP + 2):
@@ -188,39 +216,58 @@
                 part_ref[k * (CHUNK // local) + p, n] = d[:, p * local : (p + 1) * local].T.astype(BF16)
 
 
-def response_kernel(weight, sgrad, query_s, grad_s, key_t, factor, dq_ref, drk_ref, drv_ref):
-    rows = drk_ref.shape[0]
+def response_kernel(weight, sgrad, query_s, grad_s, key_t, factor, dq_ref, drk_ref, drv_ref, dq, drk, drv, sems):
+    rows = drk.shape[0]
     pre = weight.shape[0] - rows
-    drk_ref[...] = nt(query_s[...], sgrad[pre:]).T.astype(BF16)
-    drv_ref[...] = nt(grad_s[...], weight[pre:]).T.astype(BF16)
+    copies = []
+
+    def leave(source, target):
+        copies.append(pltpu.make_async_copy(source, target, sems.at[len(copies)]))
+        copies[-1].start()
+
     for g in range(GROUP):
         at = slice(g * rows, (g + 1) * rows)
-        dq = nn(key_t[...], sgrad[:, at]) * factor[:, at]
-        dq_ref[:, g * HD : (g + 1) * HD] = dq.T.astype(BF16)
+        lanes = slice(g * HD, (g + 1) * HD)
+        dq[:, lanes] = (nn(key_t[...], sgrad[:, at]) * factor[:, at]).T.astype(BF16)
+        leave(dq.at[:, lanes], dq_ref.at[:, lanes])
+    drk[...] = nt(query_s[...], sgrad[pre:]).T.astype(BF16)
+    leave(drk, drk_ref)
+    drv[...] = nt(grad_s[...], weight[pre:]).T.astype(BF16)
+    leave(drv, drv_ref)
+    for copy in copies:
+        copy.wait()
 
 
 def chip_sum_kernel(mine_ref, got_ref, out_ref):
     for h in range(KVH):
         block = (mine_ref[h].astype(F32) + got_ref[h].astype(F32)).astype(BF16)
-        out_ref[h] = block
-        out_ref[KVH + h] = block
-
-
-def final_kernel(place_ref, got_ref, dk_ref, dv_ref):
+        out_ref[PLACE[0, h]] = block
+        out_ref[PLACE[1, h]] = block
+
+
+def final_kernel(place_ref, got_ref, dk_ref, dv_ref, sums, sems):
     _, side, core = place()
     own = place_ref[0, 0] == side * 2 + core
-
-    @pl.when(own)
-    def _():
-        for n, ref in enumerate((dk_ref, dv_ref)):
-            for h in range(KVH):
-                block = got_ref[h, n].astype(F32) + got_ref[KVH + h, n].astype(F32)
-                ref[:, h * HD : (h + 1) * HD] = block.astype(BF16)
-
-    @pl.when(jnp.logical_not(own))
-    def _():
-        for ref in (dk_ref, dv_ref):
-            ref[...] = jnp.zeros_like(ref)
+    half = sums.shape[1] // 2
+    copies = []
+    for n, ref in enumerate((dk_ref, dv_ref)):
+        for part in range(2):
+            rows = slice(part * half, (part + 1) * half)
+
+            @pl.when(own)
+            def _():
+                for h in range(KVH):
+                    block = got_ref[PLACE[0, h], n, rows].astype(F32) + got_ref[PLACE[1, h], n, rows].astype(F32)
+                    sums[n, rows, h * HD : (h + 1) * HD] = block.astype(BF16)
+
+            @pl.when(jnp.logical_not(own))
+            def _():
+                sums[n, rows] = jnp.zeros((half, sums.shape[2]), BF16)
+
+            copies.append(pltpu.make_async_copy(sums.at[n, rows], ref.at[rows], sems.at[len(copies)]))
+            copies[-1].start()
+    for copy in copies:
+        copy.wait()
 
 
 def on_device(
@@ -241,7 +288,7 @@
     total = pre + rows
     swap = [(d, d ^ 1) for d in range(dp)]
     groups = [
-        [(base + 2 * side + core) * heads + h for side in range(2) for h in range(heads)]
+        [(base + 2 * side + core) * heads + h for side, h in members(heads)]
         for base in range(0, dp, BLOCK)
         for core in range(2)
     ]
@@ -261,10 +308,13 @@
         prefix_keys,
         prefix_values,
         specs=[HBM, HBM, HBM],
+        out_specs=[VMEM, HBM, HBM],
         scratch=[
+            pltpu.VMEM((1, 1), jnp.int32),
+            pltpu.VMEM((1, HD), jnp.int32),
             pltpu.VMEM((2, local, width), BF16),
             pltpu.SMEM((1, prefix_owner.shape[0]), jnp.int32),
-            pltpu.SemaphoreType.DMA((2 * PARTS + 1,)),
+            pltpu.SemaphoreType.DMA((2 * PARTS + 3,)),
         ],
         vmem=60,
     )
@@ -272,18 +322,21 @@
     arrived = lax.cond(active, exchange, jnp.zeros_like, spread)
     (own,) = call(side_kernel, [struct(piece, BF16)], arrived)
     other = lax.ppermute(own, "dp", swap)
-    query_t, grad_t, bias, rbias = call(
+    query_t, grad_t, bias, rscore, rdprod = call(
         prepare_kernel,
         [
             struct((HD, GROUP * rows), BF16),
             struct((HD, GROUP * rows), BF16),
             struct((pre, HD), F32),
-            struct((rows, rows), F32),
+            struct((rows, GROUP * rows), F32),
+            struct((rows, GROUP * rows), F32),
         ],
         prefix_len.reshape(1, -1),
         slot,
         queries,
         out_grad,
+        resp_keys,
+        resp_values,
     )
     part, *saved = call(
         attention_kernel,
@@ -300,7 +353,8 @@
         query_t,
         grad_t,
         bias,
-        rbias,
+        rscore,
+        rdprod,
         own,
         other,
         resp_keys,
@@ -309,7 +363,7 @@
             pltpu.VMEM((total, HD), BF16),
             pltpu.VMEM((total, HD), BF16),
             pltpu.VMEM((HD + 16, total), BF16),
-            pltpu.VMEM((2, total, rows), F32),
+            pltpu.VMEM((2, pre, rows), F32),
         ],
         flops=10 * GROUP * rows * total * HD,
     )
@@ -318,6 +372,13 @@
         response_kernel,
         [struct(queries.shape, BF16), struct(resp_keys.shape, BF16), struct(resp_values.shape, BF16)],
         *saved,
+        out_specs=[HBM, HBM, HBM],
+        scratch=[
+            pltpu.VMEM(queries.shape, BF16),
+            pltpu.VMEM(resp_keys.shape, BF16),
+            pltpu.VMEM(resp_values.shape, BF16),
+            pltpu.SemaphoreType.DMA((GROUP + 2,)),
+        ],
         flops=2 * GROUP * rows * total * HD,
     )
     (spread,) = call(chip_sum_kernel, [struct(both, BF16)], part, got)
@@ -327,6 +388,8 @@
         [struct(prefix_keys.shape, BF16), struct(prefix_values.shape, BF16)],
         owner,
         arrived,
+        out_specs=[HBM, HBM],
+        scratch=[pltpu.VMEM((2, local, width), BF16), pltpu.SemaphoreType.DMA((4,))],
     )
     return dq, drk, drv, dk, dv
 

time: 57.9 us -> 56.2 us (0.971)
  blocking collectives: 36 us -> 35.3 us
  Pallas kernels: 14.7 us -> 14.1 us
    all_to_all x2, blocking collectives: 36 us -> 35.3 us  [exchange(): lax.all_to_all(flat, ('dp', 'head'), 0, 0, axis_index_groups=groups, tile...]
    pallas_call x7, Pallas kernels: 14.7 us -> 14.1 us  [call(): pl.pallas_call(kernel, out_shape=tuple(outs), in_specs=specs or [VMEM for...]
  transfers between devices with their start and end apart: 2 -> 2, of which waited for: 1 -> 1; matrix products, arithmetic and copies ran while one was open for 0% -> 0% of each run, Pallas kernels for 5% -> 6%
where the time goes in v5:
time: 56.2 us; the launch traced here: 55.9 us
  blocking collectives  35.3 us (63%)
  Pallas kernels  14.1 us (25%)
  starting transfers between devices  3.97 us (7%)
  between operations  1.45 us (3%)
  waiting for transfers between devices  0.94 us (2%)
    all_to_all x2, blocking collectives, exchange(): lax.all_to_all(flat, ('dp', 'head'), 0, 0, axis_index_groups=groups, tile...  35.3 us
    pallas_call x7, Pallas kernels, call(): pl.pallas_call(kernel, out_shape=tuple(outs), in_specs=specs or [VMEM for...  14.1 us
    ppermute x1, starting transfers between devices, on_device(): got = lax.ppermute(part, 'dp', swap)  2.05 us
    ppermute x1, starting transfers between devices, on_device(): other = lax.ppermute(own, 'dp', swap)  1.92 us
  transfers between devices with their start and end apart: 2, of which 1 were waited for; matrix products, arithmetic and copies ran while one was open for 0% of the time, Pallas kernels for 6%

profile of v5, /device:TPU:8, one launch (start us, length us, event | category | flops | bytes accessed | tf_op | source)
XLA Modules:
  0.0 55.9 jit_solution(4916401293943191107)
XLA Ops:
  0.6 0.0 copy-start.3
  0.6 0.0 copy-start.2
  0.7 0.0 copy-start.5
  0.7 0.0 copy-start.4
  0.7 0.0 copy-start.1
  0.7 0.0 copy-start
  0.7 1.4 %shard_map.129 = (bf16[16,2,128,128]{3,2,1,0:T(8,128)(2,1)S(1)}, s32[1,1]{1,0:T(1,128)}, s32[1,128]{1,0:T(1,128)}) custom-call(s32[1,16]{1,0:T(1,128)} %bitcast.15, bf16[128,1024]{1,0:T(8,128)(2,1)} %key_ref.1, bf16[128,1024]{1,0:T(8,128)(2,1)} %value_ref.1), custom_call_target="tpu_custom_call" | custom-call | bytes 1573444 | tf_op jit(solution)/shard_map/pallas_call | solution.py:53
  2.8 19.5 %conditional.2 = (bf16[16,2,128,128]{3,2,1,0:T(8,128)(2,1)S(1)}) conditional(s32[]{:T(128)} %bitcast.7, () %tuple.20, bf16[16,2,128,128]{3,2,1,0:T(8,128)(2,1)S(1)} %get-tuple-element.40), branch_computations={%region_0.0_spmd, %region_1.0_spmd} | conditional | bytes 2097160 | solution.py:322
  2.8 19.5 %all_to_all.8 = bf16[16,256,128]{2,1,0:T(8,128)(2,1)S(1)} all-to-all(bf16[16,256,128]{2,1,0:T(8,128)(2,1)S(1)} %bitcast.14), channel_id=1, replica_groups={{0,4,16,20,21,17,5,1,2,6,18,22,23,19,7,3},{8,12,24,28,29,25,13,9,10,14,..., dimensions={0} | all-to-all | bytes 2097152 | tf_op jit(solution)/shard_map/cond/branch_1_fun/all_to_all | solution.py:298
  22.3 0.1 shard_map.130.own_ref
  22.4 1.9 %collective-permute-start = (bf16[8,2,128,128]{3,2,1,0:T(8,128)(2,1)S(1)}, bf16[8,2,128,128]{3,2,1,0:T(8,128)(2,1)S(1)}, u32[]{:S(2)}, u32[]{:S(2)}) collective-permute-start(bf16[8,2,128,128]{3,2,1,0:T(8,128)(2,1)S(1)} %shard_map.130.own_ref), channel_id=1, source_target_pairs={{0,8},{8,0},{16,24},{24,16},{32,40},{40,32},{48,56},{56,48},{64,72... | collective-permute-start | bytes 1572872 | tf_op jit(solution)/shard_map/ppermute | solution.py:324
  24.4 0.0 copy-done.3
  24.4 0.0 copy-done.2
  24.4 0.0 copy-done.5
  24.4 0.0 copy-done.4
  24.4 0.0 copy-done.1
  24.4 0.0 copy-done
  24.4 0.9 %shard_map.128 = (bf16[128,2048]{1,0:T(8,128)(2,1)S(1)}, bf16[128,2048]{1,0:T(8,128)(2,1)S(1)}, f32[1024,128]{1,0:T(8,128)S(1)}, f32[256,2048]{1,0:T(8,128)S(1)}, f32[256,2048]{1,0:T(8,128)S(1)}) custom-call(s32[1,16]{1,0:T(1,128)S(1)} %bitcast.10, s32[1,256]{1,0:T(1,128)S(1)} %bitcast.8, bf16[256,1024]{1,0:T(8,128)(2,1)S(1)} %copy-done, ...), custom_call_target="tpu_custom_call" | custom-call | bytes 6947904 | tf_op jit(solution)/shard_map/pallas_call | solution.py:53
  25.3 0.9 %collective-permute-done.other_ref = bf16[8,2,128,128]{3,2,1,0:T(8,128)(2,1)S(1)} collective-permute-done((bf16[8,2,128,128]{3,2,1,0:T(8,128)(2,1)S(1)}, bf16[8,2,128,128]{3,2,1,0:T(8,128)(2,1)S(1)}, u32[]{:S(2)}, u32[]{:S(2)}) %collective-permute-start) | collective-permute-done | bytes 524320 | tf_op jit(solution)/shard_map/ppermute | solution.py:324
  26.3 8.3 %shard_map.131 = (bf16[8,2,128,128]{3,2,1,0:T(8,128)(2,1)S(1)}, bf16[1280,2048]{1,0:T(8,128)(2,1)S(1)}, bf16[1280,2048]{1,0:T(8,128)(2,1)S(1)}, bf16[128,2048]{1...) custom-call(s32[1,256]{1,0:T(1,128)S(1)} %bitcast.9, ...), custom_call_target="tpu_custom_call" | custom-call | flops 3355443200 | bytes 19342336 | tf_op jit(solution)/shard_map/pallas_call | solution.py:53
  34.5 2.0 %collective-permute-start.1 = (bf16[8,2,128,128]{3,2,1,0:T(8,128)(2,1)S(1)}, bf16[8,2,128,128]{3,2,1,0:T(8,128)(2,1)S(1)}, u32[]{:S(2)}, u32[]{:S(2)}) collective-permute-start(bf16[8,2,128,128]{3,2,1,0:T(8,128)(2,1)S(1)} %get-tuple-element.51.mine_ref), channel_id=1, source_target_pairs={{0,8},{8,0},{16,24},{24,16},{32,40},{40,32},{48,56},{56,48},{64,72... | collective-permute-start | bytes 1572872 | tf_op jit(solution)/shard_map/ppermute | solution.py:370
  36.6 2.4 %shard_map.132 = (bf16[256,1024]{1,0:T(8,128)(2,1)}, bf16[256,128]{1,0:T(8,128)(2,1)}, bf16[256,128]{1,0:T(8,128)(2,1)}) custom-call(bf16[1280,2048]{1,0:T(8,128)(2,1)S(1)} %get-tuple-element.41.weight, bf16[1280,2048]{1,0:T(8,128)(2,1)S(1)} %get-tuple-element.42.sgrad, bf16[128,2048]{1,0:T(8,128)(2,1)S(1)} %get-tuple-element.43.query_s, ...), custom_call_target="tpu_custom_call" | custom-call | flops 671088640 | bytes 12525568 | tf_op jit(solution)/shard_map/pallas_call | solution.py:53
  39.0 0.0 copy-start.6
  39.0 0.0 collective-permute-done.1.got_ref
  39.0 0.1 shard_map.133
  39.1 15.9 %conditional.3 = (bf16[16,2,128,128]{3,2,1,0:T(8,128)(2,1)S(1)}) conditional(s32[]{:T(128)} %bitcast.7, bf16[16,2,128,128]{3,2,1,0:T(8,128)(2,1)S(1)} %shard_map.133, bf16[16,2,128,128]{3,2,1,0:T(8,128)(2,1)S(1)} %shard_map.133), branch_computations={%region_2.0_spmd, %region_3.0_spmd} | conditional | bytes 4194312 | solution.py:385
  39.1 0.1 copy.18
  39.2 15.8 %all_to_all.9 = bf16[16,256,128]{2,1,0:T(8,128)(2,1)S(1)} all-to-all(bf16[16,256,128]{2,1,0:T(8,128)(2,1)S(1)} %copy.18), channel_id=1, replica_groups={{0,4,16,20,21,17,5,1,2,6,18,22,23,19,7,3},{8,12,24,28,29,25,13,9,10,14,..., dimensions={0} | all-to-all | bytes 2097152 | tf_op jit(solution)/shard_map/cond/branch_1_fun/all_to_all | solution.py:298
  55.0 0.0 copy-done.6
  55.0 0.9 %shard_map.134 = (bf16[128,1024]{1,0:T(8,128)(2,1)}, bf16[128,1024]{1,0:T(8,128)(2,1)}) custom-call(s32[1,128]{1,0:T(1,128)S(1)} %copy-done.6, bf16[16,2,128,128]{3,2,1,0:T(8,128)(2,1)S(1)} %get-tuple-element.55.got_ref), custom_call_target="tpu_custom_call" | custom-call | bytes 1573376 | tf_op jit(solution)/shard_map/pallas_call | solution.py:53
Async XLA Ops:
  0.6 23.7 %copy-start.3 = (bf16[256,128]{1,0:T(8,128)(2,1)S(1)}, bf16[256,128]{1,0:T(8,128)(2,1)}, u32[]{:S(2)}) copy-start(bf16[256,128]{1,0:T(8,128)(2,1)} %rvalue_ref.3) | copy-start | bytes 196612
  0.6 23.7 %copy-start.2 = (bf16[256,128]{1,0:T(8,128)(2,1)S(1)}, bf16[256,128]{1,0:T(8,128)(2,1)}, u32[]{:S(2)}) copy-start(bf16[256,128]{1,0:T(8,128)(2,1)} %rkey_ref.3) | copy-start | bytes 196612
  0.7 23.7 %copy-start.5 = (s32[16]{0:T(128)S(1)}, s32[16]{0:T(128)}, u32[]{:S(2)}) copy-start(s32[16]{0:T(128)} %param.20) | copy-start | bytes 196
  0.7 23.7 %copy-start.4 = (s32[256]{0:T(256)S(1)}, s32[256]{0:T(256)}, u32[]{:S(2)}) copy-start(s32[256]{0:T(256)} %param.19) | copy-start | bytes 3076
  0.7 23.7 %copy-start.1 = (bf16[256,1024]{1,0:T(8,128)(2,1)S(1)}, bf16[256,1024]{1,0:T(8,128)(2,1)}, u32[]{:S(2)}) copy-start(bf16[256,1024]{1,0:T(8,128)(2,1)} %grad_ref.1) | copy-start | bytes 1572868
  0.7 23.7 %copy-start = (bf16[256,1024]{1,0:T(8,128)(2,1)S(1)}, bf16[256,1024]{1,0:T(8,128)(2,1)}, u32[]{:S(2)}) copy-start(bf16[256,1024]{1,0:T(8,128)(2,1)} %query_ref.1) | copy-start | bytes 1572868
  22.4 3.8 %collective-permute-start = (bf16[8,2,128,128]{3,2,1,0:T(8,128)(2,1)S(1)}, bf16[8,2,128,128]{3,2,1,0:T(8,128)(2,1)S(1)}, u32[]{:S(2)}, u32[]{:S(2)}) collective-permute-start(bf16[8,2,128,128]{3,2,1,0:T(8,128)(2,1)S(1)} %shard_map.130.own_ref), channel_id=1, source_target_pairs={{0,8},{8,0},{16,24},{24,16},{32,40},{40,32},{48,56},{56,48},{64,72... | collective-permute-start | bytes 1572872 | tf_op jit(solution)/shard_map/ppermute | solution.py:324
  34.5 4.5 %collective-permute-start.1 = (bf16[8,2,128,128]{3,2,1,0:T(8,128)(2,1)S(1)}, bf16[8,2,128,128]{3,2,1,0:T(8,128)(2,1)S(1)}, u32[]{:S(2)}, u32[]{:S(2)}) collective-permute-start(bf16[8,2,128,128]{3,2,1,0:T(8,128)(2,1)S(1)} %get-tuple-element.51.mine_ref), channel_id=1, source_target_pairs={{0,8},{8,0},{16,24},{24,16},{32,40},{40,32},{48,56},{56,48},{64,72... | collective-permute-start | bytes 1572872 | tf_op jit(solution)/shard_map/ppermute | solution.py:370
  39.0 16.1 %copy-start.6 = (s32[1,128]{1,0:T(1,128)S(1)}, s32[1,128]{1,0:T(1,128)}, u32[]{:S(2)}) copy-start(s32[1,128]{1,0:T(1,128)} %get-tuple-element.50.place_ref) | copy-start | bytes 1540

commit v6 on v5

--- a/solution.py
+++ b/solution.py
@@ -12,7 +12,8 @@
 KVH = 8
 BLOCK = 4
 GROUP = QH // KVH
-CHUNK = 256
+CHUNK = 512
+SHORTEST = 512
 MASKED = -1e30
 
 F32 = jnp.float32
@@ -38,10 +39,6 @@
 
 
 PLACE = {member: n for n, member in enumerate(members(KVH))}
-
-
-def nt(a, b):
-    return lax.dot_general(a, b, (((1,), (1,)), ((), ())), preferred_element_type=F32)
 
 
 def nn(a, b):
@@ -146,7 +143,7 @@
     pieces, _, local, _ = own_ref.shape
     pre = pieces * local
     total = pre + rows
-    chunks = total // CHUNK
+    chunks, ahead = pre // CHUNK + 1, pre // CHUNK
     scale = 1.0 / math.sqrt(HD)
     log_scale = scale * math.log2(math.e)
     live = jnp.where(slot_ref[...] < BLOCK, 1.0, 0.0).astype(F32)
@@ -157,8 +154,10 @@
     key[pre:] = rkey_ref[...]
     value[pre:] = rvalue_ref[...]
 
+    cuts = [slice(a, a + CHUNK) for a in range(0, pre, CHUNK)] + [slice(pre, total)]
+
     def cut(k):
-        return slice(k * CHUNK, (k + 1) * CHUNK)
+        return cuts[k]
 
     def at(g):
         return slice(g * rows, (g + 1) * rows)
@@ -171,17 +170,18 @@
     tops, dots = {}, {}
 
     def scores(g, k):
-        if k == chunks - 1:
+        if k >= ahead:
             s = rscore[:, at(g)]
         else:
-            b = bias[cut(k)]
-            s = nn(key[cut(k)], query[:, at(g)]) + jnp.concatenate([b] * (rows // HD), axis=1)
+            s = nn(key[cut(k)], query[:, at(g)])
+            if cuts[k].stop > SHORTEST:
+                s = s + jnp.concatenate([bias[cut(k)]] * (rows // HD), axis=1)
             score[g % 2, cut(k)] = s
         top = jnp.max(s, axis=0, keepdims=True)
         tops[g] = top if k == 0 else jnp.maximum(tops[g], top)
 
     def weights(g, k):
-        s = rscore[:, at(g)] if k == chunks - 1 else score[g % 2, cut(k)]
+        s = rscore[:, at(g)] if k >= ahead else score[g % 2, cut(k)]
         weight[cut(k), at(g)] = jnp.exp2((s - tops[g]) * log_scale).astype(BF16)
 
     def attend(g):
@@ -190,11 +190,11 @@
         inverse = live / denom
         dots[g] = jnp.sum(both[:HD] * grad[:, at(g)].astype(F32), axis=0, keepdims=True) / denom
         factor[:, at(g)] = inverse * scale
-        query_s[:, at(g)] = (query[:, at(g)].astype(F32) * (inverse * scale)).astype(BF16)
-        grad_s[:, at(g)] = (grad[:, at(g)].astype(F32) * inverse).astype(BF16)
+        query_s[at(g)] = (query[:, at(g)].astype(F32) * (inverse * scale)).astype(BF16).T
+        grad_s[at(g)] = (grad[:, at(g)].astype(F32) * inverse).astype(BF16).T
 
     def score_grads(g, k):
-        d = rdprod[:, at(g)] if k == chunks - 1 else nn(value[cut(k)], grad[:, at(g)])
+        d = rdprod[:, at(g)] if k >= ahead else nn(value[cut(k)], grad[:, at(g)])
         sgrad[cut(k), at(g)] = weight[cut(k), at(g)] * (d - dots[g]).astype(BF16)
 
     for t in range(GROUP + 2):
@@ -208,34 +208,20 @@
         if 1 <= t <= GROUP:
             attend(t - 1)
 
-    for k in range(pre // CHUNK):
-        dk = nt(query_s[...], sgrad[cut(k)])
-        dv = nt(grad_s[...], weight[cut(k)])
-        for p in range(CHUNK // local):
-            for n, d in enumerate((dk, dv)):
-                part_ref[k * (CHUNK // local) + p, n] = d[:, p * local : (p + 1) * local].T.astype(BF16)
-
-
-def response_kernel(weight, sgrad, query_s, grad_s, key_t, factor, dq_ref, drk_ref, drv_ref, dq, drk, drv, sems):
-    rows = drk.shape[0]
+    for k in range(ahead):
+        for n, d in enumerate((nn(sgrad[cut(k)], query_s[...]), nn(weight[cut(k)], grad_s[...]))):
+            for p in range(CHUNK // local):
+                part_ref[k * (CHUNK // local) + p, n] = d[p * local : (p + 1) * local].astype(BF16)
+
+
+def response_kernel(weight, sgrad, query_s, grad_s, key_t, factor, dq_ref, drk_ref, drv_ref):
+    rows = drk_ref.shape[0]
     pre = weight.shape[0] - rows
-    copies = []
-
-    def leave(source, target):
-        copies.append(pltpu.make_async_copy(source, target, sems.at[len(copies)]))
-        copies[-1].start()
-
+    drk_ref[...] = nn(sgrad[pre:], query_s[...]).astype(BF16)
+    drv_ref[...] = nn(weight[pre:], grad_s[...]).astype(BF16)
     for g in range(GROUP):
         at = slice(g * rows, (g + 1) * rows)
-        lanes = slice(g * HD, (g + 1) * HD)
-        dq[:, lanes] = (nn(key_t[...], sgrad[:, at]) * factor[:, at]).T.astype(BF16)
-        leave(dq.at[:, lanes], dq_ref.at[:, lanes])
-    drk[...] = nt(query_s[...], sgrad[pre:]).T.astype(BF16)
-    leave(drk, drk_ref)
-    drv[...] = nt(grad_s[...], weight[pre:]).T.astype(BF16)
-    leave(drv, drv_ref)
-    for copy in copies:
-        copy.wait()
+        dq_ref[:, g * HD : (g + 1) * HD] = (nn(key_t[...], sgrad[:, at]) * factor[:, at]).T.astype(BF16)
 
 
 def chip_sum_kernel(mine_ref, got_ref, out_ref):
@@ -245,11 +231,19 @@
         out_ref[PLACE[1, h]] = block
 
 
-def final_kernel(place_ref, got_ref, dk_ref, dv_ref, sums, sems):
+def final_kernel(
+    place_ref, got_ref, dq, drk, drv, dq_ref, drk_ref, drv_ref, dk_ref, dv_ref, sums, sems
+):
     _, side, core = place()
     own = place_ref[0, 0] == side * 2 + core
     half = sums.shape[1] // 2
-    copies = []
+    copies = [
+        pltpu.make_async_copy(dq, dq_ref, sems.at[0]),
+        pltpu.make_async_copy(drk, drk_ref, sems.at[1]),
+        pltpu.make_async_copy(drv, drv_ref, sems.at[2]),
+    ]
+    for copy in copies:
+        copy.start()
     for n, ref in enumerate((dk_ref, dv_ref)):
         for part in range(2):
             rows = slice(part * half, (part + 1) * half)
@@ -344,8 +338,8 @@
             struct(piece, BF16),
             struct((total, GROUP * rows), BF16),
             struct((total, GROUP * rows), BF16),
-            struct((HD, GROUP * rows), BF16),
-            struct((HD, GROUP * rows), BF16),
+            struct((GROUP * rows, HD), BF16),
+            struct((GROUP * rows, HD), BF16),
             struct((HD, total), BF16),
             struct((1, GROUP * rows), F32),
         ],
@@ -372,26 +366,27 @@
         response_kernel,
         [struct(queries.shape, BF16), struct(resp_keys.shape, BF16), struct(resp_values.shape, BF16)],
         *saved,
-        out_specs=[HBM, HBM, HBM],
-        scratch=[
-            pltpu.VMEM(queries.shape, BF16),
-            pltpu.VMEM(resp_keys.shape, BF16),
-            pltpu.VMEM(resp_values.shape, BF16),
-            pltpu.SemaphoreType.DMA((GROUP + 2,)),
-        ],
         flops=2 * GROUP * rows * total * HD,
     )
     (spread,) = call(chip_sum_kernel, [struct(both, BF16)], part, got)
     arrived = lax.cond(active, exchange, lambda block: block, spread)
-    dk, dv = call(
+    return call(
         final_kernel,
-        [struct(prefix_keys.shape, BF16), struct(prefix_values.shape, BF16)],
+        [
+            struct(queries.shape, BF16),
+            struct(resp_keys.shape, BF16),
+            struct(resp_values.shape, BF16),
+            struct(prefix_keys.shape, BF16),
+            struct(prefix_values.shape, BF16),
+        ],
         owner,
         arrived,
-        out_specs=[HBM, HBM],
-        scratch=[pltpu.VMEM((2, local, width), BF16), pltpu.SemaphoreType.DMA((4,))],
-    )
-    return dq, drk, drv, dk, dv
+        dq,
+        drk,
+        drv,
+        out_specs=[HBM] * 5,
+        scratch=[pltpu.VMEM((2, local, width), BF16), pltpu.SemaphoreType.DMA((7,))],
+    )
 
 
 def solution(mesh):

time: 56.2 us -> 55 us (0.979)
  the two profiles are of different devices: /device:TPU:8 before, /device:TPU:192 now
where the time goes in v6:
time: 55 us; the launch traced here: 54.8 us
  blocking collectives  34.8 us (63%)
  Pallas kernels  13.2 us (24%)
  starting transfers between devices  3.97 us (7%)
  between operations  1.44 us (3%)
  waiting for transfers between devices  1.21 us (2%)
    all_to_all x2, blocking collectives, exchange(): lax.all_to_all(flat, ('dp', 'head'), 0, 0, axis_index_groups=groups, tile...  34.8 us
    pallas_call x7, Pallas kernels, call(): pl.pallas_call(kernel, out_shape=tuple(outs), in_specs=specs or [VMEM for...  13.2 us
    ppermute x1, starting transfers between devices, on_device(): got = lax.ppermute(part, 'dp', swap)  2.05 us
    ppermute x1, starting transfers between devices, on_device(): other = lax.ppermute(own, 'dp', swap)  1.92 us
  transfers between devices with their start and end apart: 2, of which 2 were waited for; matrix products, arithmetic and copies ran while one was open for 0% of the time, Pallas kernels for 4%

profile of v6, /device:TPU:192, one launch (start us, length us, event | category | flops | bytes accessed | tf_op | source)
XLA Modules:
  0.0 54.8 jit_solution(3829088724754043889)
XLA Ops:
  0.6 0.0 copy-start.3
  0.6 0.0 copy-start.2
  0.7 0.0 copy-start.5
  0.7 0.0 copy-start.4
  0.7 0.0 copy-start.1
  0.7 0.0 copy-start
  0.7 1.4 %shard_map.128 = (bf16[16,2,128,128]{3,2,1,0:T(8,128)(2,1)S(1)}, s32[1,1]{1,0:T(1,128)}, s32[1,128]{1,0:T(1,128)}) custom-call(s32[1,16]{1,0:T(1,128)} %bitcast.15, bf16[128,1024]{1,0:T(8,128)(2,1)} %key_ref.1, bf16[128,1024]{1,0:T(8,128)(2,1)} %value_ref.1), custom_call_target="tpu_custom_call" | custom-call | bytes 1573444 | tf_op jit(solution)/shard_map/pallas_call | solution.py:50
  2.8 19.1 %conditional.2 = (bf16[16,2,128,128]{3,2,1,0:T(8,128)(2,1)S(1)}) conditional(s32[]{:T(128)} %bitcast.5, () %tuple.19, bf16[16,2,128,128]{3,2,1,0:T(8,128)(2,1)S(1)} %get-tuple-element.39), branch_computations={%region_0.0_spmd, %region_1.0_spmd} | conditional | bytes 2097160 | solution.py:316
  2.8 19.0 %all_to_all.8 = bf16[16,256,128]{2,1,0:T(8,128)(2,1)S(1)} all-to-all(bf16[16,256,128]{2,1,0:T(8,128)(2,1)S(1)} %bitcast.14), channel_id=1, replica_groups={{0,4,16,20,21,17,5,1,2,6,18,22,23,19,7,3},{8,12,24,28,29,25,13,9,10,14,..., dimensions={0} | all-to-all | bytes 2097152 | tf_op jit(solution)/shard_map/cond/branch_1_fun/all_to_all | solution.py:292
  21.8 0.1 shard_map.130.own_ref
  22.0 1.9 %collective-permute-start = (bf16[8,2,128,128]{3,2,1,0:T(8,128)(2,1)S(1)}, bf16[8,2,128,128]{3,2,1,0:T(8,128)(2,1)S(1)}, u32[]{:S(2)}, u32[]{:S(2)}) collective-permute-start(bf16[8,2,128,128]{3,2,1,0:T(8,128)(2,1)S(1)} %shard_map.130.own_ref), channel_id=1, source_target_pairs={{0,8},{8,0},{16,24},{24,16},{32,40},{40,32},{48,56},{56,48},{64,72... | collective-permute-start | bytes 1572872 | tf_op jit(solution)/shard_map/ppermute | solution.py:318
  23.9 0.0 copy-done.3
  23.9 0.0 copy-done.2
  23.9 0.0 copy-done.5
  23.9 0.0 copy-done.4
  23.9 0.0 copy-done.1
  23.9 0.0 copy-done
  23.9 0.9 %shard_map.129 = (bf16[128,2048]{1,0:T(8,128)(2,1)S(1)}, bf16[128,2048]{1,0:T(8,128)(2,1)S(1)}, f32[1024,128]{1,0:T(8,128)S(1)}, f32[256,2048]{1,0:T(8,128)S(1)}, f32[256,2048]{1,0:T(8,128)S(1)}) custom-call(s32[1,16]{1,0:T(1,128)S(1)} %bitcast.10, s32[1,256]{1,0:T(1,128)S(1)} %bitcast.8, bf16[256,1024]{1,0:T(8,128)(2,1)S(1)} %copy-done, ...), custom_call_target="tpu_custom_call" | custom-call | bytes 6947904 | tf_op jit(solution)/shard_map/pallas_call | solution.py:50
  24.8 0.9 %collective-permute-done.other_ref = bf16[8,2,128,128]{3,2,1,0:T(8,128)(2,1)S(1)} collective-permute-done((bf16[8,2,128,128]{3,2,1,0:T(8,128)(2,1)S(1)}, bf16[8,2,128,128]{3,2,1,0:T(8,128)(2,1)S(1)}, u32[]{:S(2)}, u32[]{:S(2)}) %collective-permute-start) | collective-permute-done | bytes 524320 | tf_op jit(solution)/shard_map/ppermute | solution.py:318
  25.8 8.1 %shard_map.131 = (bf16[8,2,128,128]{3,2,1,0:T(8,128)(2,1)S(1)}, bf16[1280,2048]{1,0:T(8,128)(2,1)S(1)}, bf16[1280,2048]{1,0:T(8,128)(2,1)S(1)}, bf16[2048,128]{1...) custom-call(s32[1,256]{1,0:T(1,128)S(1)} %bitcast.9, ...), custom_call_target="tpu_custom_call" | custom-call | flops 3355443200 | bytes 19342336 | tf_op jit(solution)/shard_map/pallas_call | solution.py:50
  33.9 2.0 %collective-permute-start.1 = (bf16[8,2,128,128]{3,2,1,0:T(8,128)(2,1)S(1)}, bf16[8,2,128,128]{3,2,1,0:T(8,128)(2,1)S(1)}, u32[]{:S(2)}, u32[]{:S(2)}) collective-permute-start(bf16[8,2,128,128]{3,2,1,0:T(8,128)(2,1)S(1)} %get-tuple-element.40.mine_ref), channel_id=1, source_target_pairs={{0,8},{8,0},{16,24},{24,16},{32,40},{40,32},{48,56},{56,48},{64,72... | collective-permute-start | bytes 1572872 | tf_op jit(solution)/shard_map/ppermute | solution.py:364
  35.9 1.5 %shard_map.133 = (bf16[256,1024]{1,0:T(8,128)(2,1)S(1)}, bf16[256,128]{1,0:T(8,128)(2,1)S(1)}, bf16[256,128]{1,0:T(8,128)(2,1)S(1)}) custom-call(bf16[1280,2048]{1,0:T(8,128)(2,1)S(1)} %get-tuple-element.41.weight, bf16[1280,2048]{1,0:T(8,128)(2,1)S(1)} %get-tuple-element.42.sgrad, bf16[2048,128]{1,0:T(8,128)(2,1)S(1)} %get-tuple-element.43.query_s, ...), custom_call_target="tpu_custom_call" | custom-call | flops 671088640 | bytes 12525568 | tf_op jit(solution)/shard_map/pallas_call | solution.py:50
  37.4 0.0 copy-start.6
  37.4 0.3 collective-permute-done.1.got_ref
  37.7 0.1 shard_map.132
  37.8 15.9 %conditional.3 = (bf16[16,2,128,128]{3,2,1,0:T(8,128)(2,1)S(1)}) conditional(s32[]{:T(128)} %bitcast.5, bf16[16,2,128,128]{3,2,1,0:T(8,128)(2,1)S(1)} %shard_map.132, bf16[16,2,128,128]{3,2,1,0:T(8,128)(2,1)S(1)} %shard_map.132), branch_computations={%region_2.0_spmd, %region_3.0_spmd} | conditional | bytes 4194312 | solution.py:372
  37.8 0.1 copy.18
  37.9 15.8 %all_to_all.9 = bf16[16,256,128]{2,1,0:T(8,128)(2,1)S(1)} all-to-all(bf16[16,256,128]{2,1,0:T(8,128)(2,1)S(1)} %copy.18), channel_id=1, replica_groups={{0,4,16,20,21,17,5,1,2,6,18,22,23,19,7,3},{8,12,24,28,29,25,13,9,10,14,..., dimensions={0} | all-to-all | bytes 2097152 | tf_op jit(solution)/shard_map/cond/branch_1_fun/all_to_all | solution.py:292
  53.7 0.0 copy-done.6
  53.7 1.1 %shard_map.134 = (bf16[256,1024]{1,0:T(8,128)(2,1)}, bf16[256,128]{1,0:T(8,128)(2,1)}, bf16[256,128]{1,0:T(8,128)(2,1)}, bf16[128,1024]{1,0:T(8,128)(2,1)}, bf16[128,1024]{1,0:T(8,128)(2,1)}) custom-call(s32[1,128]{1,0:T(1,128)S(1)} %copy-done.6, bf16[16,2,128,128]{3,2,1,0:T(8,128)(2,1)S(1)} %get-tuple-element.51.got_ref, ...), custom_call_target="tpu_custom_call" | custom-call | bytes 2884096 | tf_op jit(solution)/shard_map/pallas_call | solution.py:50
Async XLA Ops:
  0.6 23.3 %copy-start.3 = (bf16[256,128]{1,0:T(8,128)(2,1)S(1)}, bf16[256,128]{1,0:T(8,128)(2,1)}, u32[]{:S(2)}) copy-start(bf16[256,128]{1,0:T(8,128)(2,1)} %rvalue_ref.3) | copy-start | bytes 196612
  0.6 23.3 %copy-start.2 = (bf16[256,128]{1,0:T(8,128)(2,1)S(1)}, bf16[256,128]{1,0:T(8,128)(2,1)}, u32[]{:S(2)}) copy-start(bf16[256,128]{1,0:T(8,128)(2,1)} %rkey_ref.3) | copy-start | bytes 196612
  0.7 23.3 %copy-start.5 = (s32[16]{0:T(128)S(1)}, s32[16]{0:T(128)}, u32[]{:S(2)}) copy-start(s32[16]{0:T(128)} %param.20) | copy-start | bytes 196
  0.7 23.3 %copy-start.4 = (s32[256]{0:T(256)S(1)}, s32[256]{0:T(256)}, u32[]{:S(2)}) copy-start(s32[256]{0:T(256)} %param.19) | copy-start | bytes 3076
  0.7 23.3 %copy-start.1 = (bf16[256,1024]{1,0:T(8,128)(2,1)S(1)}, bf16[256,1024]{1,0:T(8,128)(2,1)}, u32[]{:S(2)}) copy-start(bf16[256,1024]{1,0:T(8,128)(2,1)} %grad_ref.1) | copy-start | bytes 1572868
  0.7 23.3 %copy-start = (bf16[256,1024]{1,0:T(8,128)(2,1)S(1)}, bf16[256,1024]{1,0:T(8,128)(2,1)}, u32[]{:S(2)}) copy-start(bf16[256,1024]{1,0:T(8,128)(2,1)} %query_ref.1) | copy-start | bytes 1572868
  22.0 3.8 %collective-permute-start = (bf16[8,2,128,128]{3,2,1,0:T(8,128)(2,1)S(1)}, bf16[8,2,128,128]{3,2,1,0:T(8,128)(2,1)S(1)}, u32[]{:S(2)}, u32[]{:S(2)}) collective-permute-start(bf16[8,2,128,128]{3,2,1,0:T(8,128)(2,1)S(1)} %shard_map.130.own_ref), channel_id=1, source_target_pairs={{0,8},{8,0},{16,24},{24,16},{32,40},{40,32},{48,56},{56,48},{64,72... | collective-permute-start | bytes 1572872 | tf_op jit(solution)/shard_map/ppermute | solution.py:318
  33.9 3.8 %collective-permute-start.1 = (bf16[8,2,128,128]{3,2,1,0:T(8,128)(2,1)S(1)}, bf16[8,2,128,128]{3,2,1,0:T(8,128)(2,1)S(1)}, u32[]{:S(2)}, u32[]{:S(2)}) collective-permute-start(bf16[8,2,128,128]{3,2,1,0:T(8,128)(2,1)S(1)} %get-tuple-element.40.mine_ref), channel_id=1, source_target_pairs={{0,8},{8,0},{16,24},{24,16},{32,40},{40,32},{48,56},{56,48},{64,72... | collective-permute-start | bytes 1572872 | tf_op jit(solution)/shard_map/ppermute | solution.py:364
  37.4 16.3 %copy-start.6 = (s32[1,128]{1,0:T(1,128)S(1)}, s32[1,128]{1,0:T(1,128)}, u32[]{:S(2)}) copy-start(s32[1,128]{1,0:T(1,128)} %get-tuple-element.32.place_ref) | copy-start | bytes 1540

commit v7 on v6

--- a/solution.py
+++ b/solution.py
@@ -136,8 +136,8 @@
 
 def attention_kernel(
     slot_ref, query, grad, bias, rscore, rdprod, own_ref, other_ref, rkey_ref, rvalue_ref,
-    part_ref, weight, sgrad, query_s, grad_s, key_t, factor,
-    key, value, value_t, score,
+    part_ref, rweight, sgrad, query_s, grad_s, key_t, factor,
+    key, value, value_t, score, weight,
 ):
     rows = slot_ref.shape[1]
     pieces, _, local, _ = own_ref.shape
@@ -182,7 +182,10 @@
 
     def weights(g, k):
         s = rscore[:, at(g)] if k >= ahead else score[g % 2, cut(k)]
-        weight[cut(k), at(g)] = jnp.exp2((s - tops[g]) * log_scale).astype(BF16)
+        e = jnp.exp2((s - tops[g]) * log_scale).astype(BF16)
+        weight[cut(k), at(g)] = e
+        if k >= ahead:
+            rweight[:, at(g)] = e
 
     def attend(g):
         both = nn(value_t[...], weight[:, at(g)])
@@ -214,11 +217,11 @@
                 part_ref[k * (CHUNK // local) + p, n] = d[p * local : (p + 1) * local].astype(BF16)
 
 
-def response_kernel(weight, sgrad, query_s, grad_s, key_t, factor, dq_ref, drk_ref, drv_ref):
+def response_kernel(rweight, sgrad, query_s, grad_s, key_t, factor, dq_ref, drk_ref, drv_ref):
     rows = drk_ref.shape[0]
-    pre = weight.shape[0] - rows
+    pre = sgrad.shape[0] - rows
     drk_ref[...] = nn(sgrad[pre:], query_s[...]).astype(BF16)
-    drv_ref[...] = nn(weight[pre:], grad_s[...]).astype(BF16)
+    drv_ref[...] = nn(rweight[...], grad_s[...]).astype(BF16)
     for g in range(GROUP):
         at = slice(g * rows, (g + 1) * rows)
         dq_ref[:, g * HD : (g + 1) * HD] = (nn(key_t[...], sgrad[:, at]) * factor[:, at]).T.astype(BF16)
@@ -336,7 +339,7 @@
         attention_kernel,
         [
             struct(piece, BF16),
-            struct((total, GROUP * rows), BF16),
+            struct((rows, GROUP * rows), BF16),
             struct((total, GROUP * rows), BF16),
             struct((GROUP * rows, HD), BF16),
             struct((GROUP * rows, HD), BF16),
@@ -358,6 +361,7 @@
             pltpu.VMEM((total, HD), BF16),
             pltpu.VMEM((HD + 16, total), BF16),
             pltpu.VMEM((2, pre, rows), F32),
+            pltpu.VMEM((total, GROUP * rows), BF16),
         ],
         flops=10 * GROUP * rows * total * HD,
     )
@@ -369,7 +373,7 @@
         flops=2 * GROUP * rows * total * HD,
     )
     (spread,) = call(chip_sum_kernel, [struct(both, BF16)], part, got)
-    arrived = lax.cond(active, exchange, lambda block: block, spread)
+    arrived = lax.cond(active, exchange, jnp.zeros_like, spread)
     return call(
         final_kernel,
         [

time: 55 us -> 54.4 us (0.989)
  Pallas kernels: 13.2 us -> 12.5 us
    pallas_call x7, Pallas kernels: 13.2 us -> 12.5 us  [call(): pl.pallas_call(kernel, out_shape=tuple(outs), in_specs=specs or [VMEM for...]
where the time goes in v7:
time: 54.4 us; the launch traced here: 54.1 us
  blocking collectives  35 us (64%)
  Pallas kernels  12.5 us (23%)
  starting transfers between devices  3.97 us (7%)
  between operations  1.43 us (3%)
  waiting for transfers between devices  1.23 us (2%)
    all_to_all x2, blocking collectives, exchange(): lax.all_to_all(flat, ('dp', 'head'), 0, 0, axis_index_groups=groups, tile...  35 us
    pallas_call x7, Pallas kernels, call(): pl.pallas_call(kernel, out_shape=tuple(outs), in_specs=specs or [VMEM for...  12.5 us
    ppermute x1, starting transfers between devices, on_device(): got = lax.ppermute(part, 'dp', swap)  2.05 us
    ppermute x1, starting transfers between devices, on_device(): other = lax.ppermute(own, 'dp', swap)  1.92 us
  transfers between devices with their start and end apart: 2, of which 2 were waited for; matrix products, arithmetic and copies ran while one was open for 0% of the time, Pallas kernels for 4%

profile of v7, /device:TPU:192, one launch (start us, length us, event | category | flops | bytes accessed | tf_op | source)
XLA Modules:
  0.0 54.1 jit_solution(10802901566388860750)
XLA Ops:
  0.6 1.3 %shard_map.128 = (bf16[16,2,128,128]{3,2,1,0:T(8,128)(2,1)S(1)}, s32[1,1]{1,0:T(1,128)}, s32[1,128]{1,0:T(1,128)}) custom-call(s32[1,16]{1,0:T(1,128)} %bitcast.15, bf16[128,1024]{1,0:T(8,128)(2,1)} %key_ref.1, bf16[128,1024]{1,0:T(8,128)(2,1)} %value_ref.1), custom_call_target="tpu_custom_call" | custom-call | bytes 1573444 | tf_op jit(solution)/shard_map/pallas_call | solution.py:50
  2.6 0.0 copy-start
  2.6 0.0 copy-start.1
  2.6 0.0 copy-start.2
  2.6 0.0 copy-start.3
  2.6 0.0 copy-start.4
  2.7 0.0 copy-start.5
  2.7 19.2 %conditional.2 = (bf16[16,2,128,128]{3,2,1,0:T(8,128)(2,1)S(1)}) conditional(s32[]{:T(128)} %bitcast.5, () %tuple.20, bf16[16,2,128,128]{3,2,1,0:T(8,128)(2,1)S(1)} %get-tuple-element.38), branch_computations={%region_0.0_spmd, %region_1.0_spmd} | conditional | bytes 2097160 | solution.py:319
  2.7 19.2 %all_to_all.8 = bf16[16,256,128]{2,1,0:T(8,128)(2,1)S(1)} all-to-all(bf16[16,256,128]{2,1,0:T(8,128)(2,1)S(1)} %bitcast.14), channel_id=1, replica_groups={{0,4,16,20,21,17,5,1,2,6,18,22,23,19,7,3},{8,12,24,28,29,25,13,9,10,14,..., dimensions={0} | all-to-all | bytes 2097152 | tf_op jit(solution)/shard_map/cond/branch_1_fun/all_to_all | solution.py:295
  21.9 0.1 shard_map.130.own_ref
  22.0 1.9 %collective-permute-start = (bf16[8,2,128,128]{3,2,1,0:T(8,128)(2,1)S(1)}, bf16[8,2,128,128]{3,2,1,0:T(8,128)(2,1)S(1)}, u32[]{:S(2)}, u32[]{:S(2)}) collective-permute-start(bf16[8,2,128,128]{3,2,1,0:T(8,128)(2,1)S(1)} %shard_map.130.own_ref), channel_id=1, source_target_pairs={{0,8},{8,0},{16,24},{24,16},{32,40},{40,32},{48,56},{56,48},{64,72... | collective-permute-start | bytes 1572872 | tf_op jit(solution)/shard_map/ppermute | solution.py:321
  23.9 0.0 copy-done
  23.9 0.0 copy-done.1
  23.9 0.0 copy-done.2
  23.9 0.0 copy-done.3
  23.9 0.0 copy-done.4
  23.9 0.0 copy-done.5
  24.0 0.9 %shard_map.129 = (bf16[128,2048]{1,0:T(8,128)(2,1)S(1)}, bf16[128,2048]{1,0:T(8,128)(2,1)S(1)}, f32[1024,128]{1,0:T(8,128)S(1)}, f32[256,2048]{1,0:T(8,128)S(1)}, f32[256,2048]{1,0:T(8,128)S(1)}) custom-call(s32[1,16]{1,0:T(1,128)S(1)} %bitcast.10, s32[1,256]{1,0:T(1,128)S(1)} %bitcast.8, bf16[256,1024]{1,0:T(8,128)(2,1)S(1)} %copy-done, ...), custom_call_target="tpu_custom_call" | custom-call | bytes 6947904 | tf_op jit(solution)/shard_map/pallas_call | solution.py:50
  24.8 0.9 %collective-permute-done.other_ref = bf16[8,2,128,128]{3,2,1,0:T(8,128)(2,1)S(1)} collective-permute-done((bf16[8,2,128,128]{3,2,1,0:T(8,128)(2,1)S(1)}, bf16[8,2,128,128]{3,2,1,0:T(8,128)(2,1)S(1)}, u32[]{:S(2)}, u32[]{:S(2)}) %collective-permute-start) | collective-permute-done | bytes 524320 | tf_op jit(solution)/shard_map/ppermute | solution.py:321
  25.8 7.5 %shard_map.131 = (bf16[8,2,128,128]{3,2,1,0:T(8,128)(2,1)S(1)}, bf16[256,2048]{1,0:T(8,128)(2,1)S(1)}, bf16[1280,2048]{1,0:T(8,128)(2,1)S(1)}, bf16[2048,128]{1,...) custom-call(s32[1,256]{1,0:T(1,128)S(1)} %bitcast.9, ...), custom_call_target="tpu_custom_call" | custom-call | flops 3355443200 | bytes 15148032 | tf_op jit(solution)/shard_map/pallas_call | solution.py:50
  33.3 2.0 %collective-permute-start.1 = (bf16[8,2,128,128]{3,2,1,0:T(8,128)(2,1)S(1)}, bf16[8,2,128,128]{3,2,1,0:T(8,128)(2,1)S(1)}, u32[]{:S(2)}, u32[]{:S(2)}) collective-permute-start(bf16[8,2,128,128]{3,2,1,0:T(8,128)(2,1)S(1)} %get-tuple-element.39.mine_ref), channel_id=1, source_target_pairs={{0,8},{8,0},{16,24},{24,16},{32,40},{40,32},{48,56},{56,48},{64,72... | collective-permute-start | bytes 1572872 | tf_op jit(solution)/shard_map/ppermute | solution.py:368
  35.4 1.5 %shard_map.133 = (bf16[256,1024]{1,0:T(8,128)(2,1)S(1)}, bf16[256,128]{1,0:T(8,128)(2,1)S(1)}, bf16[256,128]{1,0:T(8,128)(2,1)S(1)}) custom-call(bf16[256,2048]{1,0:T(8,128)(2,1)S(1)} %get-tuple-element.40.rweight, bf16[1280,2048]{1,0:T(8,128)(2,1)S(1)} %get-tuple-element.41.sgrad, bf16[2048,128]{1,0:T(8,128)(2,1)S(1)} %get-tuple-element.42.query_s, ...), custom_call_target="tpu_custom_call" | custom-call | flops 671088640 | bytes 8331264 | tf_op jit(solution)/shard_map/pallas_call | solution.py:50
  36.8 0.3 collective-permute-done.1.got_ref
  37.1 0.1 shard_map.132
  37.2 0.0 copy-start.6
  37.3 15.8 %conditional.3 = (bf16[16,2,128,128]{3,2,1,0:T(8,128)(2,1)S(1)}) conditional(s32[]{:T(128)} %bitcast.5, () %tuple.19, bf16[16,2,128,128]{3,2,1,0:T(8,128)(2,1)S(1)} %shard_map.132), branch_computations={%region_2.0_spmd, %region_3.0_spmd} | conditional | bytes 2097160 | solution.py:376
  37.3 15.8 %all_to_all.9 = bf16[16,256,128]{2,1,0:T(8,128)(2,1)S(1)} all-to-all(bf16[16,256,128]{2,1,0:T(8,128)(2,1)S(1)} %bitcast.12), channel_id=1, replica_groups={{0,4,16,20,21,17,5,1,2,6,18,22,23,19,7,3},{8,12,24,28,29,25,13,9,10,14,..., dimensions={0} | all-to-all | bytes 2097152 | tf_op jit(solution)/shard_map/cond/branch_1_fun/all_to_all | solution.py:295
  53.1 0.0 copy-done.6
  53.1 1.1 %shard_map.134 = (bf16[256,1024]{1,0:T(8,128)(2,1)}, bf16[256,128]{1,0:T(8,128)(2,1)}, bf16[256,128]{1,0:T(8,128)(2,1)}, bf16[128,1024]{1,0:T(8,128)(2,1)}, bf16[128,1024]{1,0:T(8,128)(2,1)}) custom-call(s32[1,128]{1,0:T(1,128)S(1)} %copy-done.6, bf16[16,2,128,128]{3,2,1,0:T(8,128)(2,1)S(1)} %get-tuple-element.50.got_ref, ...), custom_call_target="tpu_custom_call" | custom-call | bytes 2884096 | tf_op jit(solution)/shard_map/pallas_call | solution.py:50
Async XLA Ops:
  2.6 21.3 %copy-start = (bf16[256,1024]{1,0:T(8,128)(2,1)S(1)}, bf16[256,1024]{1,0:T(8,128)(2,1)}, u32[]{:S(2)}) copy-start(bf16[256,1024]{1,0:T(8,128)(2,1)} %query_ref.1) | copy-start | bytes 1572868
  2.6 21.3 %copy-start.1 = (bf16[256,1024]{1,0:T(8,128)(2,1)S(1)}, bf16[256,1024]{1,0:T(8,128)(2,1)}, u32[]{:S(2)}) copy-start(bf16[256,1024]{1,0:T(8,128)(2,1)} %grad_ref.1) | copy-start | bytes 1572868
  2.6 21.3 %copy-start.2 = (bf16[256,128]{1,0:T(8,128)(2,1)S(1)}, bf16[256,128]{1,0:T(8,128)(2,1)}, u32[]{:S(2)}) copy-start(bf16[256,128]{1,0:T(8,128)(2,1)} %rkey_ref.3) | copy-start | bytes 196612
  2.6 21.3 %copy-start.3 = (bf16[256,128]{1,0:T(8,128)(2,1)S(1)}, bf16[256,128]{1,0:T(8,128)(2,1)}, u32[]{:S(2)}) copy-start(bf16[256,128]{1,0:T(8,128)(2,1)} %rvalue_ref.3) | copy-start | bytes 196612
  2.6 21.3 %copy-start.4 = (s32[256]{0:T(256)S(1)}, s32[256]{0:T(256)}, u32[]{:S(2)}) copy-start(s32[256]{0:T(256)} %param.19) | copy-start | bytes 3076
  2.7 21.3 %copy-start.5 = (s32[16]{0:T(128)S(1)}, s32[16]{0:T(128)}, u32[]{:S(2)}) copy-start(s32[16]{0:T(128)} %param.20) | copy-start | bytes 196
  22.0 3.8 %collective-permute-start = (bf16[8,2,128,128]{3,2,1,0:T(8,128)(2,1)S(1)}, bf16[8,2,128,128]{3,2,1,0:T(8,128)(2,1)S(1)}, u32[]{:S(2)}, u32[]{:S(2)}) collective-permute-start(bf16[8,2,128,128]{3,2,1,0:T(8,128)(2,1)S(1)} %shard_map.130.own_ref), channel_id=1, source_target_pairs={{0,8},{8,0},{16,24},{24,16},{32,40},{40,32},{48,56},{56,48},{64,72... | collective-permute-start | bytes 1572872 | tf_op jit(solution)/shard_map/ppermute | solution.py:321
  33.3 3.8 %collective-permute-start.1 = (bf16[8,2,128,128]{3,2,1,0:T(8,128)(2,1)S(1)}, bf16[8,2,128,128]{3,2,1,0:T(8,128)(2,1)S(1)}, u32[]{:S(2)}, u32[]{:S(2)}) collective-permute-start(bf16[8,2,128,128]{3,2,1,0:T(8,128)(2,1)S(1)} %get-tuple-element.39.mine_ref), channel_id=1, source_target_pairs={{0,8},{8,0},{16,24},{24,16},{32,40},{40,32},{48,56},{56,48},{64,72... | collective-permute-start | bytes 1572872 | tf_op jit(solution)/shard_map/ppermute | solution.py:368
  37.2 15.8 %copy-start.6 = (s32[1,128]{1,0:T(1,128)S(1)}, s32[1,128]{1,0:T(1,128)}, u32[]{:S(2)}) copy-start(s32[1,128]{1,0:T(1,128)} %get-tuple-element.31.place_ref) | copy-start | bytes 1540
